TPU v7x, 128 devices: a whole 4x4x4 slice. The times are simulated.
128 devices in a mesh: rep: 8 (over x, z_hi), tp: 16 (over y, z_lo, core).
Axes of the slice: x: 4, y: 4, z: 4 (z_hi: 2, z_lo: 2; z = z_hi * 2 + z_lo), core: 2. Of those that a mesh axis runs over, the one named last changes fastest.
Arguments:
- token_ids: int32 [32, 4], replicated, may hold values from 0 to 76031
- cache_len: int32 [32], P('rep'), may hold values from 1 to 8192, as said below
- embed_table: bfloat16 [76032, 5120], P('rep', 'tp'), may hold values from -400 to 400
- norm_gain: bfloat16 [5120], P('tp'), may hold values from 0.099609375 to 1.8984375
- old_qkv: bfloat16 [5120, 7168], P('tp'), may hold values from -0.078125 to 0.078125
- old_out: bfloat16 [5120, 5120], P(None, 'tp'), may hold values from -0.078125 to 0.078125
- new_qkv: bfloat16 [5120, 7168], P(('tp', 'rep')), may hold values from -0.078125 to 0.078125
- new_out: bfloat16 [5120, 5120], P(None, ('tp', 'rep')), may hold values from -0.078125 to 0.078125
- kv_cache: bfloat16 [32, 8192, 2048], P('rep', 'tp'), may hold values from -400 to 400
Outputs:
- attended: bfloat16 [32, 4, 5120], P('rep', None, 'tp')
Inputs may be any that keep to these rules, and one draw needn't show every extreme that they name: `cache_len`: some row's length is 8192.
All inputs are finite; a program needn't handle non-finite values.
Results may differ from a plain program's by a relative error of at most 0.009.
The roundings to bfloat16 on the way count: a program that leaves them out, or rounds other values in their place, can miss the bound.
Values may be sent and summed in bfloat16 or wider, within the bound.
No kernel may reach another device: no remote copies, remote signals or barrier semaphores. Data moves between devices by JAX's collectives and lax.ppermute only.
A program may use at most 128 MiB of HBM per device.

v0:
```python
import jax
import jax.numpy as jnp
from jax import lax
from jax.sharding import PartitionSpec as P

D = 5120
HEADS = 40
KV_HEADS = 8
HEAD_DIM = 128
STEPS = 4
OLD_STEPS = 2


NORM_EPSILON = 1e-06
ROPE_BASE = 1000000.0
MASK_VALUE = -1e30


def rotate(tensor, positions):
    half_dim = tensor.shape[-1] // 2
    inverse_freq = ROPE_BASE ** (-jnp.arange(half_dim, dtype=jnp.float32) * 2.0 / tensor.shape[-1])
    angles = positions.astype(jnp.float32)[:, None] * inverse_freq[None, :]
    cosine = jnp.cos(angles)[:, None, :]
    sine_part = jnp.sin(angles)[:, None, :]
    front_half = tensor[..., :half_dim]
    back_half = tensor[..., half_dim:]
    return jnp.concatenate(
        [front_half * cosine - back_half * sine_part, back_half * cosine + front_half * sine_part],
        axis=-1,
    )


def rotate_columns(summed, positions):
    query_width = HEADS * HEAD_DIM
    kv_width = KV_HEADS * HEAD_DIM
    query_part = rotate(summed[:, :query_width].reshape(-1, HEADS, HEAD_DIM), positions).reshape(
        -1, query_width
    )
    key_part = rotate(
        summed[:, query_width : query_width + kv_width].reshape(-1, KV_HEADS, HEAD_DIM), positions
    ).reshape(-1, kv_width)
    return jnp.concatenate([query_part, key_part, summed[:, query_width + kv_width :]], axis=1)


def finish(summed, squares, positions):
    root_mean = jnp.sqrt(squares / D + NORM_EPSILON)
    normed = summed / root_mean[:, None]
    return rotate_columns(normed, positions).astype(jnp.bfloat16)


def body(
    token_ids, cache_len, embed_table, norm_gain, old_qkv, old_out, new_qkv, new_out, kv_cache
):
    query_width = HEADS * HEAD_DIM
    kv_width = KV_HEADS * HEAD_DIM
    group_size = HEADS // KV_HEADS
    score_scale = 1.0 / HEAD_DIM**0.5
    row_count = cache_len.shape[0]
    later = STEPS - OLD_STEPS
    vocab_local = embed_table.shape[0]
    vocab_start = lax.axis_index("rep") * vocab_local
    local_ids = token_ids - vocab_start
    in_window = (local_ids >= 0) & (local_ids < vocab_local)
    found_rows = jnp.take(embed_table, jnp.clip(local_ids, 0, vocab_local - 1), axis=0)
    partial_rows = jnp.where(in_window[..., None], found_rows.astype(jnp.float32), 0.0)
    embedded = lax.psum_scatter(
        partial_rows.astype(jnp.bfloat16), "rep", scatter_dimension=0, tiled=True
    )
    fresh_qkv, fresh_out = (
        lax.all_gather(new_qkv, "rep", axis=0, tiled=True),
        lax.all_gather(new_out, "rep", axis=1, tiled=True),
    )
    step_positions = cache_len[:, None] + jnp.arange(STEPS, dtype=jnp.int32)[None, :]
    embedded_wide = embedded.astype(jnp.float32)
    squares = jnp.sum(embedded_wide * embedded_wide, axis=-1)
    scaled = (embedded_wide * norm_gain.astype(jnp.float32)).astype(jnp.bfloat16)
    cache_local = kv_cache.shape[1]
    cache_start = lax.axis_index("tp") * cache_local
    valid_mask = (cache_start + jnp.arange(cache_local, dtype=jnp.int32))[None, :] < cache_len[
        :, None
    ]
    keys_cache = kv_cache[..., :kv_width].reshape(row_count, cache_local, KV_HEADS, HEAD_DIM)
    values_cache = kv_cache[..., kv_width:].reshape(row_count, cache_local, KV_HEADS, HEAD_DIM)

    def project(partial_value, first_step, step_count):
        partial_rows_flat = partial_value.reshape(row_count * step_count, -1)
        squares_flat = squares[:, first_step : first_step + step_count].reshape(-1)
        positions_flat = step_positions[:, first_step : first_step + step_count].reshape(-1)
        summed, squares_all = lax.psum((partial_rows_flat, squares_flat), "tp")
        finished = finish(summed, squares_all, positions_flat)
        return finished.reshape(row_count, step_count, -1)

    def attend(projected, first_step, step_count):
        known = first_step + step_count
        queries = projected[:, first_step:known, :query_width].reshape(
            row_count, step_count, KV_HEADS, group_size, HEAD_DIM
        )
        keys_new = projected[:, :known, query_width : query_width + kv_width].reshape(
            row_count, known, KV_HEADS, HEAD_DIM
        )
        values_new = projected[:, :known, query_width + kv_width :].reshape(
            row_count, known, KV_HEADS, HEAD_DIM
        )
        scores_cache = (
            jnp.einsum("rgkhd,rpkd->rgkhp", queries, keys_cache, preferred_element_type=jnp.float32)
            * score_scale
        )
        scores_cache = jnp.where(valid_mask[:, None, None, None, :], scores_cache, MASK_VALUE)
        cache_peak = lax.pmax(jnp.max(scores_cache, axis=-1), "tp")
        scores_new = (
            jnp.einsum("rgkhd,rjkd->rgkhj", queries, keys_new, preferred_element_type=jnp.float32)
            * score_scale
        )
        causal = (
            jnp.arange(known, dtype=jnp.int32)[None, :]
            <= (first_step + jnp.arange(step_count, dtype=jnp.int32))[:, None]
        )
        scores_new = jnp.where(causal[None, :, None, None, :], scores_new, MASK_VALUE)
        peak_all = jnp.maximum(cache_peak, jnp.max(scores_new, axis=-1))
        weights_cache = jnp.exp(scores_cache - peak_all[..., None]).astype(jnp.bfloat16)
        numerator = jnp.einsum(
            "rgkhp,rpkd->rgkhd", weights_cache, values_cache, preferred_element_type=jnp.float32
        )
        denominator = jnp.sum(weights_cache.astype(jnp.float32), axis=-1)
        numerator, denominator = lax.psum((numerator, denominator), "tp")
        weights_new = jnp.exp(scores_new - peak_all[..., None]).astype(jnp.bfloat16)
        numerator = numerator + jnp.einsum(
            "rgkhj,rjkd->rgkhd", weights_new, values_new, preferred_element_type=jnp.float32
        )
        denominator = denominator + jnp.sum(weights_new.astype(jnp.float32), axis=-1)
        return (
            (numerator / denominator[..., None])
            .astype(jnp.bfloat16)
            .reshape(row_count, step_count, query_width)
        )

    early_partial = jnp.einsum(
        "rgd,de->rge", scaled[:, :OLD_STEPS], old_qkv, preferred_element_type=jnp.float32
    )
    early_proj = project(early_partial, 0, OLD_STEPS)
    early_heads = attend(early_proj, 0, OLD_STEPS)
    early_out = jnp.einsum(
        "rgi,ie->rge", early_heads, old_out, preferred_element_type=jnp.float32
    ).astype(jnp.bfloat16)
    late_partial = jnp.einsum(
        "rgd,de->rge", scaled[:, OLD_STEPS:], fresh_qkv, preferred_element_type=jnp.float32
    )
    late_proj = project(late_partial, OLD_STEPS, later)
    projected = jnp.concatenate([early_proj, late_proj], axis=1)
    late_heads = attend(projected, OLD_STEPS, later)
    late_out = jnp.einsum(
        "rgi,ie->rge", late_heads, fresh_out, preferred_element_type=jnp.float32
    ).astype(jnp.bfloat16)
    return jnp.concatenate([early_out, late_out], axis=1)


def solution(mesh):
    in_specs = (
        P(),
        P("rep"),
        P("rep", "tp"),
        P("tp"),
        P("tp", None),
        P(None, "tp"),
        P(("tp", "rep"), None),
        P(None, ("tp", "rep")),
        P("rep", "tp", None),
    )
    out_specs = P("rep", None, "tp")
    return jax.shard_map(body, mesh=mesh, in_specs=in_specs, out_specs=out_specs, check_vma=False)
```

profile of v0, /device:TPU:1, one launch (start us, length us, event | category | flops | bytes accessed | tf_op | source)
XLA Modules:
  0.0 579.1 jit_solution(13680349919752855187)
XLA Ops:
  6.5 0.8 compare_and_fusion
  7.6 9.7 %copy.44 = bf16[9504,320]{1,0:T(8,128)(2,1)} copy(bf16[9504,320]{0,1:T(8,128)(2,1)} %param.11) | data formatting | bytes 12165120 | tf_op args[2]
  17.4 4.9 gather_fusion
  22.6 0.6 copy.45
  23.3 0.7 all-gather.3.cloned.1.call-update
  24.4 6.0 %fusion.55 = (bf16[4,512,1024]{2,1,0:T(8,128)(2,1)}, bf16[4,512,1024]{2,1,0:T(8,128)(2,1)}) fusion(bf16[4,512,2048]{2,1,0:T(8,128)(2,1)} %param.17), kind=kLoop, calls=%fused_computation.115 | loop fusion | bytes 16777216 | tf_op jit(solution)/shard_map/slice | solution.py:82
  30.4 6.2 %copy.96 = bf16[4,512,1024]{1,2,0:T(8,128)(2,1)} copy(bf16[4,512,1024]{2,1,0:T(8,128)(2,1)} %get-tuple-element.17) | data formatting | bytes 8388608
  39.1 0.6 broadcast_compare_fusion
  39.7 0.7 multiply_cosine_fusion.1
  40.4 63.6 %all-reduce.10.cloned.1.call-done = bf16[32,4,320]{2,0,1:T(8,128)(2,1)} async-done(((bf16[32,4,320]{2,0,1:T(8,128)(2,1)}), bf16[32,4,320]{2,0,1:T(8,128)(2,1)}) %all-reduce.10.cloned.1.call-update) | async-done | bytes 81936
  104.1 0.8 fusion.48
  104.9 3.1 fusion.2
  108.0 0.9 reshape.268
  108.9 74.4 %all-gather.3.cloned.1.call-done = bf16[320,7168]{1,0:T(8,128)(2,1)} async-done(((bf16[40,7168]{1,0:T(8,128)(2,1)}), bf16[320,7168]{1,0:T(8,128)(2,1)}) %all-gather.3.cloned.1.call-update) | async-done | bytes 4587536 | tf_op jit(solution)/shard_map/all_gather | solution.py:70
  183.3 3.1 fusion
  186.4 0.9 reshape.278
  187.7 6.2 %copy.99 = bf16[4,512,1024]{1,2,0:T(8,128)(2,1)} copy(bf16[4,512,1024]{2,1,0:T(8,128)(2,1)} %get-tuple-element.18) | data formatting | bytes 8388608
  193.9 27.6 %all-reduce.2 = (f32[8]{0:T(128)S(1)}, f32[8]{0:T(128)S(1)}) all-reduce(f32[8]{0:T(128)S(1)} %reshape.279, f32[8]{0:T(128)S(1)} %reshape.269), channel_id=1, replica_groups=mesh['rep'=8,'tp'=16] {'tp'}, use_global_device_ids=true, to_apply=%region_12.13 | all-reduce | flops 16 | bytes 128 | tf_op jit(solution)/shard_map/psum | solution.py:89
  221.6 77.9 %all-reduce.14.cloned.1.call-done = (f32[8,7168]{1,0:T(8,128)}, f32[8,7168]{1,0:T(8,128)}) async-done(((f32[8,7168]{1,0:T(8,128)}, f32[8,7168]{1,0:T(8,128)}), (f32[8,7168]{1,0:T(8,128)}, f32[8,7168]{1,0:T(8,128)})) %all-reduce.14.cloned.1.call-update) | async-done | bytes 458768 | tf_op jit(solution)/shard_map/psum | solution.py:89
  299.4 1.2 broadcast_divide_fusion
  303.1 4.9 fusion.61
  308.1 2.3 fusion.60
  310.4 0.7 pad_maximum_fusion.9
  311.1 1.3 concatenate.48
  312.5 0.7 subtract_convert_fusion.2
  314.0 0.7 concatenate.47
  314.6 1.5 concatenate.51
  316.2 1.3 concatenate.49
  317.5 1.3 concatenate.54
  318.8 2.0 fusion.63
  320.9 51.9 %all-reduce.5 = (f32[4,2,8,5]{3,1,2,0:T(2,128)S(1)}, f32[4,2,8,5]{3,1,2,0:T(2,128)S(1)}) all-reduce(f32[4,2,8,5]{3,1,2,0:T(2,128)} %get-tuple-element.46, f32[4,2,8,5]{3,1,2,0:T(2,128)} %get-tuple-element.48), channel_id=1, replica_groups=mesh['rep'=8,'tp'=16] {'tp'}, use_global_device_ids=true, to_apply=%region_14.15 | all-reduce | flops 640 | bytes 5120 | tf_op jit(solution)/shard_map/pmax | solution.py:109
  372.8 1.6 fusion.62
  374.5 4.5 convolution_bitcast_fusion.1
  379.0 2.0 convolution_bitcast_fusion
  381.6 0.8 slice_bitcast_fusion.4
  382.4 1.6 convert_reduce_fusion.1
  384.0 1.6 convert_reduce_fusion
  385.6 53.8 %all-reduce.1 = (f32[4,2,8,5]{3,1,2,0:T(2,128)}, f32[4,2,8,5]{3,1,2,0:T(2,128)}) all-reduce(f32[4,2,8,5]{3,1,2,0:T(2,128)S(1)} %convert_reduce_fusion, f32[4,2,8,5]{3,1,2,0:T(2,128)S(1)} %convert_reduce_fusion.1), channel_id=1, replica_groups=mesh['rep'=8,'tp'=16] {'tp'}, use_global_device_ids=true, to_apply=%region_18.19 | all-reduce | flops 640 | bytes 5120 | tf_op jit(solution)/shard_map/psum | solution.py:125
  439.4 1.0 convert_reduce_fusion.3
  440.4 0.8 add.94
  441.3 0.8 add.100
  442.1 59.8 %all-reduce.12.cloned.1.call-done = (f32[4,2,8,5,128]{4,3,1,2,0:T(8,128)}, f32[4,2,8,5,128]{4,3,1,2,0:T(8,128)}) async-done(((f32[4,2,8,5,128]{4,3,1,2,0:T(8,128)}, f32[4,2,8,5,128]{4,3,1,2,0:T(8,128)}), (f32[4,2,8,5,128]{4,3,1,2,0:T(8,128)}, f32[4,2,8,5,128]{4,3,1,2,0:T(8,128)})) %all-reduce.12.cloned.1.call-update) | async-done | bytes 327696 | tf_op jit(solution)/shard_map/psum | solution.py:125
  501.8 1.2 fusion.16
  503.2 1.3 fusion.17
  504.5 0.7 reshape.285
  505.2 1.0 fusion.22
  506.2 62.7 %all-gather.5.cloned.1.call-done = bf16[5120,320]{0,1:T(8,128)(2,1)} async-done(((bf16[5120,40]{0,1:T(8,128)(2,1)}), bf16[5120,320]{0,1:T(8,128)(2,1)}) %all-gather.5.cloned.1.call-update) | async-done | bytes 3276816 | tf_op jit(solution)/shard_map/all_gather | solution.py:71
  569.0 3.0 fusion.25
  (92 shorter events, 8.0 us)
Async XLA Ops:
  6.5 498.7 %copy-start = (bf16[5120,320]{0,1:T(8,128)(2,1)S(1)}, bf16[5120,320]{0,1:T(8,128)(2,1)}, u32[]{:S(2)}) copy-start(bf16[5120,320]{0,1:T(8,128)(2,1)} %param.14) | copy-start | bytes 9830404
  6.5 97.6 %all-reduce.10.cloned.1.call-start = ((), (), s32[]{:S(2)}) async-start(), calls=%async_computation.2 | async-start | bytes 196608
  7.6 16.5 %copy-start.14 = (bf16[320]{0:T(512)(128)(2,1)S(1)}, bf16[320]{0:T(512)(128)(2,1)}, u32[]{:S(2)}) copy-start(bf16[320]{0:T(512)(128)(2,1)} %param.12) | copy-start | bytes 1924
  7.6 16.5 %copy-start.13 = (s32[4]{0:T(128)S(1)}, s32[4]{0:T(128)}, u32[]{:S(2)}) copy-start(s32[4]{0:T(128)} %param.10) | copy-start | bytes 52
  23.3 160.0 %all-gather.3.cloned.1.call-start = ((), (), s32[]{:S(2)}) async-start(), calls=%async_computation | async-start | bytes 5160960 | tf_op jit(solution)/shard_map/all_gather | solution.py:70
  24.0 275.4 %all-reduce.14.cloned.1.call-start = ((), (), s32[]{:S(2)}) async-start(), calls=%async_computation.4 | async-start | bytes 917504 | tf_op jit(solution)/shard_map/psum | solution.py:89
  30.4 6.2 %copy-start.15 = (u32[128]{0:T(128)S(1)}, u32[128]{0:T(128)}, u32[]{:S(2)}) copy-start(u32[128]{0:T(128)} %constant.63) | copy-start | bytes 1540
  40.4 261.5 %copy-start.9 = (f32[8,64]{1,0:T(8,128)}, f32[8,64]{1,0:T(8,128)S(1)}, u32[]{:S(2)}) copy-start(f32[8,64]{1,0:T(8,128)S(1)} %get-tuple-element.40) | copy-start | bytes 6148
  40.4 261.5 %copy-start.11 = (f32[8,64]{1,0:T(8,128)}, f32[8,64]{1,0:T(8,128)S(1)}, u32[]{:S(2)}) copy-start(f32[8,64]{1,0:T(8,128)S(1)} %get-tuple-element.41) | copy-start | bytes 6148
  187.2 314.6 %all-reduce.12.cloned.1.call-start = ((), (), s32[]{:S(2)}) async-start(), calls=%async_computation.3 | async-start | bytes 1048576 | tf_op jit(solution)/shard_map/psum | solution.py:125
  187.7 114.5 %copy-start.7 = (f32[8,64]{1,0:T(8,128)S(1)}, f32[8,64]{1,0:T(8,128)}, u32[]{:S(2)}) copy-start(f32[8,64]{1,0:T(8,128)} %get-tuple-element.44) | copy-start | bytes 6148
  187.7 114.5 %copy-start.8 = (f32[8,64]{1,0:T(8,128)S(1)}, f32[8,64]{1,0:T(8,128)}, u32[]{:S(2)}) copy-start(f32[8,64]{1,0:T(8,128)} %get-tuple-element.45) | copy-start | bytes 6148
  300.6 1.8 copy-start.4
  302.4 5.6 copy-start.1
  302.5 5.6 copy-start.5
  308.1 2.4 copy-start.10
  308.1 2.4 copy-start.12
  372.8 6.2 %copy-start.2 = (bf16[4,512,1024]{1,2,0:T(8,128)(2,1)S(1)}, bf16[4,512,1024]{1,2,0:T(8,128)(2,1)}, u32[]{:S(2)}) copy-start(bf16[4,512,1024]{1,2,0:T(8,128)(2,1)} %copy.99) | copy-start | bytes 12582916
  372.8 6.2 %copy-start.3 = (f32[4,2,8,5,512]{4,3,1,2,0:T(8,128)S(1)}, f32[4,2,8,5,512]{4,3,1,2,0:T(8,128)}, u32[]{:S(2)}) copy-start(f32[4,2,8,5,512]{4,3,1,2,0:T(8,128)} %get-tuple-element.47) | copy-start | bytes 1966084
  374.4 66.7 %copy-start.6 = (f32[4,2,8,5,4]{3,4,1,2,0:T(4,128)}, f32[4,2,8,5,4]{3,4,1,2,0:T(4,128)S(1)}, u32[]{:S(2)}) copy-start(f32[4,2,8,5,4]{3,4,1,2,0:T(4,128)S(1)} %get-tuple-element.51) | copy-start | bytes 15364
  381.1 187.9 %all-gather.5.cloned.1.call-start = ((), (), s32[]{:S(2)}) async-start(), calls=%async_computation.1 | async-start | bytes 3686400 | tf_op jit(solution)/shard_map/all_gather | solution.py:71
Sparse Core Ops, SparseCore 0:
  23.4 80.6 all-reduce.9
  106.7 76.5 all-gather.2
  187.4 112.0 all-reduce.13
  381.2 120.6 all-reduce.11
  504.3 64.6 all-gather.4
where the time goes:
time: 581 us; the launch traced here: 579 us
  waiting for transfers between devices  340 us (59%)
  blocking collectives  133 us (23%)
  local copies, waits for them, and re-layouts  47.4 us (8%)
  matrix products  30.1 us (5%)
  other arithmetic  14.2 us (2%)
  between operations  14.2 us (2%)
    psum x1, waiting for transfers between devices, project(): summed, squares_all = lax.psum((partial_rows_flat, squares_flat), 'tp')  77.9 us
    all_gather x1, waiting for transfers between devices, body(): lax.all_gather(new_qkv, 'rep', axis=0, tiled=True)  74.4 us
    unnamed x6, waiting for transfers between devices  64.9 us
    all_gather x1, waiting for transfers between devices, body(): lax.all_gather(new_out, 'rep', axis=1, tiled=True)  62.7 us
    psum x1, waiting for transfers between devices, attend(): numerator, denominator = lax.psum((numerator, denominator), 'tp')  59.8 us
    psum x1, blocking collectives, attend(): numerator, denominator = lax.psum((numerator, denominator), 'tp')  53.8 us
    pmax x1, blocking collectives, attend(): cache_peak = lax.pmax(jnp.max(scores_cache, axis=-1), 'tp')  51.9 us
    psum x1, blocking collectives, project(): summed, squares_all = lax.psum((partial_rows_flat, squares_flat), 'tp')  27.6 us
  transfers between devices with their start and end apart: 5, of which 5 were waited for; matrix products, arithmetic and copies ran while one was open for 7% of the time, Pallas kernels for 0%

commit v1 on v0

v1 whole, which is shorter than its diff:
```python
import functools

import jax
import jax.numpy as jnp
from jax import lax
from jax.experimental import pallas as pl
from jax.experimental.pallas import tpu as pltpu
from jax.sharding import PartitionSpec as P

D = 5120
HEADS = 40
KV_HEADS = 8
HEAD_DIM = 128
GROUP = HEADS // KV_HEADS
STEPS = 4
OLD_STEPS = 2
ROWS = 4
N_X = 4
N_REP = 8
N_TP = 16
TOKENS = N_REP * ROWS * STEPS

NORM_EPSILON = 1e-06
ROPE_BASE = 1000000.0
MASK_VALUE = -1e30
SCORE_SCALE = 1.0 / HEAD_DIM**0.5

FEAT = D // N_TP
PART = FEAT // N_X
SHARD = PART // 2
LANES = 128
SLOTS = 8
HALF_HEADS = KV_HEADS // 2
HALF_ROWS = HALF_HEADS * SLOTS
BLOCK = 2 * HALF_ROWS
DESTS = N_X * 8

f32 = jnp.float32
bf16 = jnp.bfloat16
MIB = 1 << 20

VMEM = pl.BlockSpec(memory_space=pltpu.VMEM)
SMEM = pl.BlockSpec(memory_space=pltpu.SMEM)
ANY = pl.BlockSpec(memory_space=pl.ANY)


def params(mib, grid=False):
    kwargs = dict(dimension_semantics=("arbitrary",) * grid) if grid else {}
    return pltpu.CompilerParams(vmem_limit_bytes=mib * MIB, **kwargs)


def gather_kernel(ids_ref, tail_ref, table_ref, out_ref, buf, cols, sems):
    window = table_ref.shape[1]
    tail_start = window // LANES * LANES
    start = lax.axis_index("rep") * window

    def local_id(i):
        zh, el, xx = i // 64, (i // 32) % 2, (i // 8) % 4
        row, par = (i // 2) % 4, i % 2
        return ids_ref[el * 2 + par, (xx * 2 + zh) * ROWS + row] - start

    def copy(i, local):
        base = pl.multiple_of(local // LANES * LANES, LANES)
        return pltpu.make_async_copy(
            table_ref.at[:, pl.ds(base, LANES)], buf.at[i], sems.at[i]
        )

    def begin(i, carry):
        local = local_id(i)

        @pl.when((local >= 0) & (local < tail_start))
        def _():
            copy(i, local).start()

        return carry

    lax.fori_loop(0, TOKENS, begin, 0, unroll=8)
    cols[...] = jnp.zeros_like(cols)
    lane = lax.broadcasted_iota(jnp.int32, (FEAT, LANES), 1)

    def place(i, local, block):
        shift = lax.rem(i - lax.rem(local, LANES) + LANES, LANES)
        moved = pltpu.roll(block.astype(f32), shift, 1)
        cols[...] = jnp.where(lane == i, moved, cols[...])

    def end(i, carry):
        local = local_id(i)

        @pl.when((local >= 0) & (local < tail_start))
        def _():
            copy(i, local).wait()
            place(i, local, buf[i])

        @pl.when((local >= tail_start) & (local < window))
        def _():
            place(i, local, tail_ref[...])

        return carry

    lax.fori_loop(0, TOKENS, end, 0)
    out_ref[...] = jnp.zeros_like(out_ref)
    for xx in range(N_X):
        rows = cols[xx * PART : (xx + 1) * PART, :].T.astype(bf16)
        for zh in range(2):
            out_ref[xx * 2 + zh, :, :PART] = rows[zh * 64 : (zh + 1) * 64]


def gather_rows(token_ids, embed_table):
    table = embed_table.T
    tail = table.shape[1] // LANES
    return pl.pallas_call(
        gather_kernel,
        grid=(1,),
        in_specs=[
            pl.BlockSpec(memory_space=pltpu.SMEM),
            pl.BlockSpec((FEAT, LANES), lambda i: (0, tail)),
            ANY,
        ],
        out_specs=pl.BlockSpec((N_REP, 64, LANES), lambda i: (0, 0, 0)),
        out_shape=jax.ShapeDtypeStruct((N_REP, 64, LANES), bf16),
        scratch_shapes=[
            pltpu.VMEM((TOKENS, FEAT, LANES), bf16),
            pltpu.VMEM((FEAT, LANES), f32),
            pltpu.SemaphoreType.DMA((TOKENS,)),
        ],
        compiler_params=params(24),
        name="gather_rows",
    )(token_ids.T, table, table)


def project_kernel(x_ref, gain_ref, new_ref, other_ref, old_ref, keep_ref, send_ref, old, sem):
    rep, tp = lax.axis_index("rep"), lax.axis_index("tp")
    xx, zh, core = rep // 2, rep % 2, tp % 2
    copy = pltpu.make_async_copy(
        old_ref.at[pl.ds(pl.multiple_of(xx * PART, 16), PART), :], old, sem
    )
    copy.start()
    embedded = jnp.sum(x_ref[...].astype(f32), axis=0)
    squares = jnp.sum(embedded * embedded, axis=1, keepdims=True)
    wide = gain_ref[...].astype(f32)
    gain = jnp.zeros((1, PART), f32)
    for i in range(N_X):
        gain = gain + jnp.where(xx == i, wide[:, i * PART : (i + 1) * PART], 0.0)
    scaled = (embedded[:, :PART] * gain).astype(bf16)
    early, late = scaled[:DESTS], scaled[DESTS:]
    first, second = late[:, :SHARD], late[:, SHARD:]
    late_own = jnp.where(zh == 0, first, second)
    late_other = jnp.where(zh == 0, second, first)
    copy.wait()
    for out_ref, half in ((keep_ref, core), (send_ref, 1 - core)):
        for j in range(HALF_HEADS):
            head = half * HALF_HEADS + j
            starts = (
                (head * (GROUP * HEAD_DIM), GROUP * HEAD_DIM, 0),
                (HEADS * HEAD_DIM + head * HEAD_DIM, HEAD_DIM, GROUP),
                ((HEADS + KV_HEADS) * HEAD_DIM + head * HEAD_DIM, HEAD_DIM, GROUP + 1),
            )
            for start, width, slot in starts:
                columns = pl.ds(pl.multiple_of(start, HEAD_DIM), width)
                sums = (
                    jnp.dot(early, old[:, columns], preferred_element_type=f32),
                    jnp.dot(late_own, new_ref[:, columns], preferred_element_type=f32)
                    + jnp.dot(late_other, other_ref[:, columns], preferred_element_type=f32),
                )
                for el in range(2):
                    for g in range(width // HEAD_DIM):
                        at = el * HALF_ROWS + j * SLOTS + slot + g
                        out_ref[pl.ds(at, DESTS, stride=BLOCK), :] = sums[el][
                            :, g * HEAD_DIM : (g + 1) * HEAD_DIM
                        ]
            for el in range(2):
                at = el * HALF_ROWS + j * SLOTS + SLOTS - 1
                out_ref[pl.ds(at, DESTS, stride=BLOCK), :] = jnp.broadcast_to(
                    squares[el * DESTS : (el + 1) * DESTS], (DESTS, LANES)
                )


def project(received, norm_gain, new_qkv, other_qkv, old_qkv):
    width = old_qkv.shape[1]
    out = jax.ShapeDtypeStruct((DESTS * BLOCK, LANES), f32)
    return pl.pallas_call(
        project_kernel,
        in_specs=[VMEM, VMEM, VMEM, VMEM, ANY],
        out_specs=[VMEM, VMEM],
        out_shape=[out, out],
        scratch_shapes=[pltpu.VMEM((PART, width), bf16), pltpu.SemaphoreType.DMA],
        compiler_params=params(24),
        name="project",
    )(received, norm_gain.reshape(1, FEAT), new_qkv, other_qkv, old_qkv)


def finish_kernel(x_ref, cos_ref, sin_ref, out_ref):
    summed = jnp.sum(x_ref[...], axis=0).reshape(2, HALF_HEADS, SLOTS, LANES)
    squares = summed[:, :, SLOTS - 1 :, :]
    normed = summed / jnp.sqrt(squares / D + NORM_EPSILON)
    swapped = pltpu.roll(normed.reshape(BLOCK, LANES), HEAD_DIM // 2, 1).reshape(normed.shape)
    rotated = normed * cos_ref[...].reshape(2, 1, 1, LANES) + swapped * sin_ref[...].reshape(
        2, 1, 1, LANES
    )
    slot = lax.broadcasted_iota(jnp.int32, normed.shape, 2)
    result = jnp.where(slot <= GROUP, rotated, jnp.where(slot == GROUP + 1, normed, 0.0))
    out_ref[...] = jnp.broadcast_to(
        result.reshape(1, BLOCK, LANES).astype(bf16), out_ref.shape
    )


def finish(received, cosine, sine):
    return pl.pallas_call(
        finish_kernel,
        in_specs=[VMEM, VMEM, VMEM],
        out_specs=VMEM,
        out_shape=jax.ShapeDtypeStruct((N_TP, BLOCK, LANES), bf16),
        compiler_params=params(16),
        name="finish",
    )(received, cosine, sine)


def attend_kernel(len_ref, q_ref, k_ref, v_ref, out_ref, q_wide, out_wide):
    row, half = pl.program_id(0), pl.program_id(1)
    tp = lax.axis_index("tp")
    chunk = k_ref.shape[1]

    @pl.when((row == 0) & (half == 0))
    def _():
        q_wide[...] = q_ref[...].reshape(q_wide.shape).astype(f32)

    valid = len_ref[row] - tp * chunk
    count = STEPS * SLOTS
    position = lax.broadcasted_iota(jnp.int32, (count, chunk), 1)
    cache_mask = position < valid
    from_step = lax.broadcasted_iota(jnp.int32, (count, count), 0) // SLOTS
    column = lax.broadcasted_iota(jnp.int32, (count, count), 1)
    new_mask = (column % SLOTS == GROUP) & (column // SLOTS <= from_step) & (tp == 0)
    slot = lax.broadcasted_iota(jnp.int32, (STEPS, SLOTS, LANES), 1)
    diagonal = slot == lax.broadcasted_iota(jnp.int32, (STEPS, SLOTS, LANES), 2)
    for j in range(HALF_HEADS):
        at = [
            pl.multiple_of(
                ((row * 2 + s % 2) * 2 + half) * BLOCK + (s // 2) * HALF_ROWS + j * SLOTS, SLOTS
            )
            for s in range(STEPS)
        ]
        wide = jnp.concatenate([q_wide[pl.ds(a, SLOTS), :] for a in at], axis=0)
        queries = wide.astype(bf16)
        shifted = pltpu.roll(wide, count - 1, 0).astype(bf16)
        columns = slice(j * HEAD_DIM, (j + 1) * HEAD_DIM)
        contract_last = (((1,), (1,)), ((), ()))
        scores = lax.dot_general(
            queries, k_ref[0, :, columns], contract_last, preferred_element_type=f32
        )
        scores = jnp.where(cache_mask, scores * SCORE_SCALE, MASK_VALUE)
        scores_new = lax.dot_general(
            queries, queries, contract_last, preferred_element_type=f32
        )
        scores_new = jnp.where(new_mask, scores_new * SCORE_SCALE, MASK_VALUE)
        peak = jnp.maximum(
            jnp.max(scores, axis=1, keepdims=True), jnp.max(scores_new, axis=1, keepdims=True)
        )
        weights = jnp.exp(scores - peak).astype(bf16)
        weights_new = jnp.exp(scores_new - peak).astype(bf16)
        total = jnp.sum(weights.astype(f32), axis=1, keepdims=True) + jnp.sum(
            weights_new.astype(f32), axis=1, keepdims=True
        )
        numerator = jnp.dot(
            weights, v_ref[0, :, columns], preferred_element_type=f32
        ) + jnp.dot(weights_new, shifted, preferred_element_type=f32)
        part = (numerator / total).reshape(STEPS, SLOTS, LANES)
        log_total = (peak + jnp.log(total)).reshape(STEPS, SLOTS, 1)
        log_row = jnp.sum(jnp.where(diagonal, log_total, 0.0), axis=1, keepdims=True)
        high = log_row.astype(bf16).astype(f32)
        middle = (log_row - high).astype(bf16).astype(f32)
        low = log_row - high - middle
        part = jnp.where(
            slot < GROUP,
            part,
            jnp.where(slot == GROUP, high, jnp.where(slot == GROUP + 1, middle, low)),
        )
        for s in range(STEPS):
            out_wide[pl.ds(at[s], SLOTS), :] = part[s]

    @pl.when((row == ROWS - 1) & (half == 1))
    def _():
        out_ref[...] = out_wide[...].astype(bf16).reshape(out_ref.shape)


def attend(cache_len, gathered, kv_cache):
    chunk = kv_cache.shape[1]
    width = HALF_HEADS * HEAD_DIM
    whole = pl.BlockSpec((N_TP, BLOCK, LANES), lambda r, h: (0, 0, 0))
    return pl.pallas_call(
        attend_kernel,
        grid=(ROWS, 2),
        in_specs=[
            pl.BlockSpec(memory_space=pltpu.SMEM),
            whole,
            pl.BlockSpec((1, chunk, width), lambda r, h: (r, 0, h)),
            pl.BlockSpec((1, chunk, width), lambda r, h: (r, 0, 2 + h)),
        ],
        out_specs=whole,
        out_shape=jax.ShapeDtypeStruct((N_TP, BLOCK, LANES), bf16),
        scratch_shapes=[
            pltpu.VMEM((N_TP * BLOCK, LANES), f32),
            pltpu.VMEM((N_TP * BLOCK, LANES), f32),
        ],
        compiler_params=params(24, 2),
        name="attend",
    )(cache_len, gathered, kv_cache, kv_cache)


def merge_kernel(x_ref, out_ref):
    x = x_ref[...].astype(f32).reshape(N_TP, 2 * HALF_HEADS, SLOTS, LANES)
    log_row = jnp.sum(x[:, :, GROUP:, :], axis=2, keepdims=True)
    slot = lax.broadcasted_iota(jnp.int32, x.shape, 2)
    lane = lax.broadcasted_iota(jnp.int32, x.shape, 3)
    log_total = jnp.sum(jnp.where(slot == lane, log_row, 0.0), axis=3, keepdims=True)
    share = jnp.exp(log_total - jnp.max(log_total, axis=0, keepdims=True))
    heads = jnp.sum(share * x, axis=0) / jnp.sum(share, axis=0)
    out_ref[...] = jnp.broadcast_to(
        heads.reshape(1, BLOCK, LANES).astype(bf16), out_ref.shape
    )


def merge(received):
    return pl.pallas_call(
        merge_kernel,
        in_specs=[VMEM],
        out_specs=VMEM,
        out_shape=jax.ShapeDtypeStruct((N_TP, BLOCK, LANES), bf16),
        compiler_params=params(16),
        name="merge",
    )(received)


def output_kernel(x_ref, old_ref, new_ref, out_ref, wide, heads, early_sum, late_sum):
    step = pl.program_id(0)
    half = N_TP // 2

    @pl.when(step == 0)
    def _():
        wide[...] = x_ref[...].reshape(wide.shape).astype(f32)
        early_sum[...] = jnp.zeros_like(early_sum)
        late_sum[...] = jnp.zeros_like(late_sum)
        for h in range(HEADS):
            core, j, g = h // (HEADS // 2), h // GROUP % HALF_HEADS, h % GROUP
            at = core * BLOCK + j * SLOTS + g
            rows = [
                wide[pl.ds(at + el * HALF_ROWS, half, stride=2 * BLOCK), :] for el in range(2)
            ]
            both = jnp.concatenate(rows, axis=0).astype(bf16)
            per_step = HEADS // heads.shape[0]
            heads[h // per_step, :, h % per_step * HEAD_DIM : (h % per_step + 1) * HEAD_DIM] = both

    contract_last = (((1,), (1,)), ((), ()))
    both = heads[step]
    early_sum[...] += lax.dot_general(
        both[:half], old_ref[...], contract_last, preferred_element_type=f32
    )
    late_sum[...] += lax.dot_general(
        both[half:], new_ref[...], contract_last, preferred_element_type=f32
    )

    @pl.when(step == pl.num_programs(0) - 1)
    def _():
        for r in range(ROWS):
            for el, total in enumerate((early_sum, late_sum)):
                out_ref[r, el * 2 : el * 2 + 2, :] = total[r * 2 : r * 2 + 2, :].astype(bf16)


def output(gathered, old_out, fresh_out):
    blocks = 4
    depth = D // blocks
    return pl.pallas_call(
        output_kernel,
        grid=(blocks,),
        in_specs=[
            pl.BlockSpec((N_TP, BLOCK, LANES), lambda i: (0, 0, 0)),
            pl.BlockSpec((FEAT, depth), lambda i: (0, i)),
            pl.BlockSpec((FEAT, depth), lambda i: (0, i)),
        ],
        out_specs=pl.BlockSpec((ROWS, STEPS, FEAT), lambda i: (0, 0, 0)),
        out_shape=jax.ShapeDtypeStruct((ROWS, STEPS, FEAT), bf16),
        scratch_shapes=[
            pltpu.VMEM((N_TP * BLOCK, LANES), f32),
            pltpu.VMEM((blocks, N_TP, depth), bf16),
            pltpu.VMEM((N_TP // 2, FEAT), f32),
            pltpu.VMEM((N_TP // 2, FEAT), f32),
        ],
        compiler_params=params(24, 1),
        name="output",
    )(gathered, old_out.T, fresh_out)


def rotation(cache_len):
    row = lax.axis_index("tp") // 4
    parity = lax.axis_index("tp") // 2 % 2
    half_dim = HEAD_DIM // 2
    inverse_freq = ROPE_BASE ** (-jnp.arange(half_dim, dtype=f32) * 2.0 / HEAD_DIM)
    positions = cache_len[row] + parity + 2 * jnp.arange(2, dtype=jnp.int32)
    angles = positions.astype(f32)[:, None] * inverse_freq[None, :]
    cosine, sine = jnp.cos(angles), jnp.sin(angles)
    return (
        jnp.concatenate([cosine, cosine], axis=1),
        jnp.concatenate([-sine, sine], axis=1),
    )


def body(
    token_ids, cache_len, embed_table, norm_gain, old_qkv, old_out, new_qkv, new_out, kv_cache
):
    fresh_out = lax.all_gather(new_out.T, "rep", axis=0, tiled=True)
    other_qkv = lax.ppermute(new_qkv, "rep", [(r, r ^ 1) for r in range(N_REP)])
    cosine, sine = rotation(cache_len)
    rows = gather_rows(token_ids, embed_table)
    rows = lax.all_to_all(rows, "rep", 0, 0)
    keep, send = project(rows, norm_gain, new_qkv, other_qkv, old_qkv)
    arrived = lax.ppermute(send, "tp", [(t, t ^ 1) for t in range(N_TP)])
    summed = (keep + arrived).reshape(DESTS, BLOCK, LANES)
    groups = [
        [(x * 2 + zh) * N_TP + k * 2 + core for x in range(N_X) for k in range(8)]
        for zh in range(2)
        for core in range(2)
    ]
    partials = lax.all_to_all(summed, ("rep", "tp"), 0, 0, axis_index_groups=groups)
    projected = lax.all_to_all(finish(partials, cosine, sine), "tp", 0, 0)
    parts = lax.all_to_all(attend(cache_len, projected, kv_cache), "tp", 0, 0)
    heads = lax.all_to_all(merge(parts), "tp", 0, 0)
    return output(heads, old_out, fresh_out)


def solution(mesh):
    in_specs = (
        P(),
        P("rep"),
        P("rep", "tp"),
        P("tp"),
        P("tp", None),
        P(None, "tp"),
        P(("tp", "rep"), None),
        P(None, ("tp", "rep")),
        P("rep", "tp", None),
    )
    out_specs = P("rep", None, "tp")
    return jax.shard_map(body, mesh=mesh, in_specs=in_specs, out_specs=out_specs, check_vma=False)
```

time: 581 us -> 136 us (0.23)
  waiting for transfers between devices: 340 us -> 26.2 us
  blocking collectives: 133 us -> 32.4 us
  local copies, waits for them, and re-layouts: 47.4 us -> 11.6 us
  Pallas kernels: 0 us -> 30.9 us
  matrix products: 30.1 us -> 0 us
  starting transfers between devices: 0.17 us -> 19.4 us
  other arithmetic: 14.2 us -> 1.28 us
    psum x2 -> x0, waiting for transfers between devices: 138 us -> none  [the longest x1 77.9 us: project(): summed, squares_all = lax.psum((partial_rows_flat, squares_flat), 'tp')]
    all_gather x2 -> x1, waiting for transfers between devices: 137 us -> 0.01 us  [body(): fresh_out = lax.all_gather(new_out.T, 'rep', axis=0, tiled=True)]
    psum x2 -> x0, blocking collectives: 81.4 us -> none  [the longest x1 53.8 us: attend(): numerator, denominator = lax.psum((numerator, denominator), 'tp')]
    unnamed x6 -> x1, waiting for transfers between devices: 64.9 us -> 0.71 us
    pmax x1 -> x0, blocking collectives: 51.9 us -> none  [attend(): cache_peak = lax.pmax(jnp.max(scores_cache, axis=-1), 'tp')]
    all_to_all x0 -> x3, blocking collectives: none -> 32.4 us  [the longest x1 11.6 us: body(): projected = lax.all_to_all(finish(partials, cosine, sine), 'tp', 0, 0)]
    pallas_call x0 -> x6, Pallas kernels: none -> 30.9 us  [the longest x1 13.8 us: gather_rows(): pl.pallas_call(gather_kernel, grid=(1,), in_specs=[pl.BlockSpec(memory_sp...]
    dot_general x12 -> x0, matrix products: 30.1 us -> none  [the longest x2 7.29 us: attend(): jnp.einsum('rgkhd,rpkd->rgkhp', queries, keys_cache, preferred_element_ty...]
  transfers between devices with their start and end apart: 5 -> 5, of which waited for: 5 -> 3; matrix products, arithmetic and copies ran while one was open for 7% -> 1% of each run, Pallas kernels for 0% -> 20%
where the time goes in v1:
time: 136 us
  blocking collectives  32.4 us (24%)
  Pallas kernels  30.9 us (23%)
  waiting for transfers between devices  26.2 us (19%)
  starting transfers between devices  19.4 us (14%)
  between operations  14.2 us (10%)
  local copies, waits for them, and re-layouts  11.6 us (9%)
    all_to_all x1, waiting for transfers between devices, body(): lax.all_to_all(summed, ('rep', 'tp'), 0, 0, axis_index_groups=groups)  16.4 us
    pallas_call x1, Pallas kernels, gather_rows(): pl.pallas_call(gather_kernel, grid=(1,), in_specs=[pl.BlockSpec(memory_sp...  13.8 us
    all_to_all x1, blocking collectives, body(): projected = lax.all_to_all(finish(partials, cosine, sine), 'tp', 0, 0)  11.6 us
    unnamed x18, local copies, waits for them, and re-layouts  11 us
    pallas_call x1, Pallas kernels, attend(): pl.pallas_call(attend_kernel, grid=(ROWS, 2), in_specs=[pl.BlockSpec(memo...  10.8 us
    all_to_all x1, blocking collectives, body(): parts = lax.all_to_all(attend(cache_len, projected, kv_cache), 'tp', 0, 0)  10.5 us
    all_to_all x1, blocking collectives, body(): heads = lax.all_to_all(merge(parts), 'tp', 0, 0)  10.3 us
    all_to_all x1, waiting for transfers between devices, body(): rows = lax.all_to_all(rows, 'rep', 0, 0)  6.73 us
  transfers between devices with their start and end apart: 5, of which 3 were waited for; matrix products, arithmetic and copies ran while one was open for 1% of the time, Pallas kernels for 20%

profile of v1, /device:TPU:1, one launch (start us, length us, event | category | flops | bytes accessed | tf_op | source)
XLA Modules:
  0.0 135.9 jit_solution(11459329386661227630)
XLA Ops:
  6.5 0.0 all-gather.2.cloned.1.call-start
  6.5 0.7 all-gather.2.cloned.1.call-update
  7.3 4.5 %collective-permute-start = (bf16[40,7168]{1,0:T(8,128)(2,1)}, bf16[40,7168]{1,0:T(8,128)(2,1)S(1)}, u32[]{:S(2)}, u32[]{:S(2)}) collective-permute-start(bf16[40,7168]{1,0:T(8,128)(2,1)} %new_ref.1), channel_id=1, source_target_pairs={{0,16},{16,0},{32,48},{48,32},{64,80},{80,64},{96,112},{112,96},{1... | collective-permute-start | bytes 1720328 | tf_op jit(solution)/shard_map/ppermute | solution.py:411
  11.8 0.0 copy-start.1
  11.8 2.7 %copy-done.1 = bf16[9504,320]{0,1:T(8,128)(2,1)S(1)} copy-done((bf16[9504,320]{0,1:T(8,128)(2,1)S(1)}, bf16[9504,320]{0,1:T(8,128)(2,1)}, u32[]{:S(2)}) %copy-start.1) | copy-done | bytes 6082584
  14.5 0.0 copy-start.6
  14.5 0.7 copy-done.6
  15.2 0.0 copy-start.8
  15.2 0.0 copy-start.5
  15.2 13.8 %gather_rows.1 = bf16[8,64,128]{2,1,0:T(8,128)(2,1)} custom-call(s32[4,32]{1,0:T(4,128)S(1)} %bitcast.9, bf16[320,9504]{1,0:T(8,128)(2,1)S(1)} %bitcast.6, bf16[320,9504]{1,0:T(8,128)(2,1)S(1)} %bitcast.7), custom_call_target="tpu_custom_call" | custom-call | tf_op jit(solution)/shard_map/gather_rows/pallas_call | solution.py:111
  29.0 6.5 %all-to-all-start = ((bf16[8,64,128]{2,1,0:T(8,128)(2,1)}), bf16[8,64,128]{2,1,0:T(8,128)(2,1)S(1)}, u32[]{:S(2)}, u32[]{:S(2)}) async-start(bf16[8,64,128]{2,1,0:T(8,128)(2,1)} %gather_rows.1), calls=%async_computation | async-start | bytes 262144 | tf_op jit(solution)/shard_map/all_to_all | solution.py:414
  35.5 0.0 copy-done.8
  35.5 0.0 copy-start.7
  35.5 6.7 %all-to-all-done.x_ref = bf16[8,64,128]{2,1,0:T(8,128)(2,1)S(1)} async-done(((bf16[8,64,128]{2,1,0:T(8,128)(2,1)}), bf16[8,64,128]{2,1,0:T(8,128)(2,1)S(1)}, u32[]{:S(2)}, u32[]{:S(2)}) %all-to-all-start) | async-done | bytes 131104 | tf_op jit(solution)/shard_map/all_to_all | solution.py:414
  42.2 0.0 collective-permute-done.other_ref
  42.2 0.0 copy-done.5
  42.2 0.0 copy-start.2
  42.3 2.3 %copy-done.2 = bf16[320,7168]{1,0:T(8,128)(2,1)S(1)} copy-done((bf16[320,7168]{1,0:T(8,128)(2,1)S(1)}, bf16[320,7168]{1,0:T(8,128)(2,1)}, u32[]{:S(2)}) %copy-start.2) | copy-done | bytes 4587544
  44.5 2.3 %project.1 = (f32[2048,128]{1,0:T(8,128)S(1)}, f32[2048,128]{1,0:T(8,128)S(1)}) custom-call(bf16[8,64,128]{2,1,0:T(8,128)(2,1)S(1)} %all-to-all-done.x_ref, bf16[1,320]{1,0:T(2,128)(2,1)S(1)} %reshape.18.gain_ref, bf16[40,7168]{1,0:T(8,128)(2,1)S(1)} %copy-done.5, bf16[40,7168]{1,0:T(8,128)(2,1)S(1)} %collective-permute-done.other_ref, ...), custom_call_target="tpu_custom_call" | custom-call | tf_op jit(solution)/shard_map/project/pallas_call | solution.py:181
  46.8 2.5 %collective-permute-start.1 = (f32[2048,128]{1,0:T(8,128)S(1)}, f32[2048,128]{1,0:T(8,128)S(1)}, u32[]{:S(2)}, u32[]{:S(2)}) collective-permute-start(f32[2048,128]{1,0:T(8,128)S(1)} %get-tuple-element.8), channel_id=1, source_target_pairs={{0,1},{1,0},{2,3},{3,2},{4,5},{5,4},{6,7},{7,6},{8,9},{9,8},{10,11... | collective-permute-start | bytes 3145736 | tf_op jit(solution)/shard_map/ppermute | solution.py:416
  49.3 2.3 %collective-permute-done.1 = f32[2048,128]{1,0:T(8,128)S(1)} collective-permute-done((f32[2048,128]{1,0:T(8,128)S(1)}, f32[2048,128]{1,0:T(8,128)S(1)}, u32[]{:S(2)}, u32[]{:S(2)}) %collective-permute-start.1) | collective-permute-done | bytes 1048608 | tf_op jit(solution)/shard_map/ppermute | solution.py:416
  51.6 1.1 add.25
  52.6 5.9 %all-to-all-start.1 = ((f32[32,64,128]{2,1,0:T(8,128)}), f32[32,64,128]{2,1,0:T(8,128)S(1)}, u32[]{:S(2)}, u32[]{:S(2)}) async-start(f32[32,64,128]{2,1,0:T(8,128)} %bitcast.2), calls=%async_computation.1 | async-start | bytes 2097152 | tf_op jit(solution)/shard_map/all_to_all | solution.py:423
  58.6 0.0 copy-done.7
  58.6 0.6 dynamic_slice.3
  59.9 0.1 fusion
  60.0 0.1 pad_maximum_fusion
  60.1 16.4 %all-to-all-done.1.x_ref = f32[32,64,128]{2,1,0:T(8,128)S(1)} async-done(((f32[32,64,128]{2,1,0:T(8,128)}), f32[32,64,128]{2,1,0:T(8,128)S(1)}, u32[]{:S(2)}, u32[]{:S(2)}) %all-to-all-start.1) | async-done | bytes 1048608 | tf_op jit(solution)/shard_map/all_to_all | solution.py:423
  76.5 0.2 finish.1
  76.7 11.6 %all_to_all.25.q_ref = bf16[16,64,128]{2,1,0:T(8,128)(2,1)S(1)} all-to-all(bf16[16,64,128]{2,1,0:T(8,128)(2,1)S(1)} %finish.1), channel_id=1, replica_groups=mesh['rep'=8,'tp'=16] {'tp'}, dimensions={0} | all-to-all | bytes 524288 | tf_op jit(solution)/shard_map/all_to_all | solution.py:424
  88.3 0.0 copy-start
  88.3 3.4 %copy-done = bf16[4,512,2048]{2,1,0:T(8,128)(2,1)S(1)} copy-done((bf16[4,512,2048]{2,1,0:T(8,128)(2,1)S(1)}, bf16[4,512,2048]{2,1,0:T(8,128)(2,1)}, u32[]{:S(2)}) %copy-start) | copy-done | bytes 8388632
  91.6 0.0 copy-start.3
  91.6 10.8 %attend.1 = bf16[16,64,128]{2,1,0:T(8,128)(2,1)S(1)} custom-call(s32[4]{0:T(128)S(1)} %copy-done.7, bf16[16,64,128]{2,1,0:T(8,128)(2,1)S(1)} %all_to_all.25.q_ref, bf16[4,512,2048]{2,1,0:T(8,128)(2,1)S(1)} %copy-done, bf16[4,512,2048]{2,1,0:T(8,128)(2,1)S(1)} %copy-done), custom_call_target="tpu_custom_call" | custom-call | tf_op jit(solution)/shard_map/attend/pallas_call | solution.py:290
  102.5 10.5 %all_to_all.26.x_ref = bf16[16,64,128]{2,1,0:T(8,128)(2,1)S(1)} all-to-all(bf16[16,64,128]{2,1,0:T(8,128)(2,1)S(1)} %attend.1), channel_id=1, replica_groups=mesh['rep'=8,'tp'=16] {'tp'}, dimensions={0} | all-to-all | bytes 524288 | tf_op jit(solution)/shard_map/all_to_all | solution.py:425
  113.0 0.4 merge.1
  113.4 10.3 %all_to_all.27.x_ref = bf16[16,64,128]{2,1,0:T(8,128)(2,1)S(1)} all-to-all(bf16[16,64,128]{2,1,0:T(8,128)(2,1)S(1)} %merge.1), channel_id=1, replica_groups=mesh['rep'=8,'tp'=16] {'tp'}, dimensions={0} | all-to-all | bytes 524288 | tf_op jit(solution)/shard_map/all_to_all | solution.py:426
  123.7 0.0 all-gather.2.cloned.1.call-done.new_ref
  123.7 0.0 copy-done.3
  123.7 0.0 copy-start.4
  123.7 1.9 %copy-done.4 = bf16[320,5120]{1,0:T(8,128)(2,1)S(1)} copy-done((bf16[320,5120]{1,0:T(8,128)(2,1)S(1)}, bf16[320,5120]{1,0:T(8,128)(2,1)}, u32[]{:S(2)}) %copy-start.4) | copy-done | bytes 3276824
  125.6 3.5 %output.1 = bf16[4,4,320]{2,1,0:T(4,128)(2,1)} custom-call(bf16[16,64,128]{2,1,0:T(8,128)(2,1)S(1)} %all_to_all.27.x_ref, bf16[320,5120]{1,0:T(8,128)(2,1)S(1)} %bitcast.8, bf16[320,5120]{1,0:T(8,128)(2,1)S(1)} %copy-done.4), custom_call_target="tpu_custom_call" | custom-call | tf_op jit(solution)/shard_map/output/pallas_call | solution.py:372
  (3 shorter events, 0.0 us)
Async XLA Ops:
  6.5 117.1 %all-gather.2.cloned.1.call-start = ((), (), s32[]{:S(2)}) async-start(), calls=%async_computation.5 | async-start | bytes 3686400 | tf_op jit(solution)/shard_map/all_gather | solution.py:410
  7.3 35.0 %collective-permute-start = (bf16[40,7168]{1,0:T(8,128)(2,1)}, bf16[40,7168]{1,0:T(8,128)(2,1)S(1)}, u32[]{:S(2)}, u32[]{:S(2)}) collective-permute-start(bf16[40,7168]{1,0:T(8,128)(2,1)} %new_ref.1), channel_id=1, source_target_pairs={{0,16},{16,0},{32,48},{48,32},{64,80},{80,64},{96,112},{112,96},{1... | collective-permute-start | bytes 1720328 | tf_op jit(solution)/shard_map/ppermute | solution.py:411
  11.8 2.7 %copy-start.1 = (bf16[9504,320]{0,1:T(8,128)(2,1)S(1)}, bf16[9504,320]{0,1:T(8,128)(2,1)}, u32[]{:S(2)}) copy-start(bf16[9504,320]{0,1:T(8,128)(2,1)} %param.11) | copy-start | bytes 18247684
  14.5 0.7 copy-start.6
  15.2 20.3 %copy-start.8 = (bf16[320]{0:T(512)(128)(2,1)S(1)}, bf16[320]{0:T(512)(128)(2,1)}, u32[]{:S(2)}) copy-start(bf16[320]{0:T(512)(128)(2,1)} %param.12) | copy-start | bytes 1924
  15.2 27.1 %copy-start.5 = (bf16[40,7168]{1,0:T(8,128)(2,1)S(1)}, bf16[40,7168]{1,0:T(8,128)(2,1)}, u32[]{:S(2)}) copy-start(bf16[40,7168]{1,0:T(8,128)(2,1)} %new_ref.1) | copy-start | bytes 1720324
  29.0 13.2 %all-to-all-start = ((bf16[8,64,128]{2,1,0:T(8,128)(2,1)}), bf16[8,64,128]{2,1,0:T(8,128)(2,1)S(1)}, u32[]{:S(2)}, u32[]{:S(2)}) async-start(bf16[8,64,128]{2,1,0:T(8,128)(2,1)} %gather_rows.1), calls=%async_computation | async-start | bytes 262144 | tf_op jit(solution)/shard_map/all_to_all | solution.py:414
  35.5 23.1 %copy-start.7 = (s32[4]{0:T(128)S(1)}, s32[4]{0:T(128)}, u32[]{:S(2)}) copy-start(s32[4]{0:T(128)} %len_ref.1) | copy-start | bytes 52
  42.2 2.3 %copy-start.2 = (bf16[320,7168]{1,0:T(8,128)(2,1)S(1)}, bf16[320,7168]{1,0:T(8,128)(2,1)}, u32[]{:S(2)}) copy-start(bf16[320,7168]{1,0:T(8,128)(2,1)} %old_ref.1) | copy-start | bytes 13762564
  46.8 4.7 %collective-permute-start.1 = (f32[2048,128]{1,0:T(8,128)S(1)}, f32[2048,128]{1,0:T(8,128)S(1)}, u32[]{:S(2)}, u32[]{:S(2)}) collective-permute-start(f32[2048,128]{1,0:T(8,128)S(1)} %get-tuple-element.8), channel_id=1, source_target_pairs={{0,1},{1,0},{2,3},{3,2},{4,5},{5,4},{6,7},{7,6},{8,9},{9,8},{10,11... | collective-permute-start | bytes 3145736 | tf_op jit(solution)/shard_map/ppermute | solution.py:416
  52.6 23.9 %all-to-all-start.1 = ((f32[32,64,128]{2,1,0:T(8,128)}), f32[32,64,128]{2,1,0:T(8,128)S(1)}, u32[]{:S(2)}, u32[]{:S(2)}) async-start(f32[32,64,128]{2,1,0:T(8,128)} %bitcast.2), calls=%async_computation.1 | async-start | bytes 2097152 | tf_op jit(solution)/shard_map/all_to_all | solution.py:423
  88.3 3.4 %copy-start = (bf16[4,512,2048]{2,1,0:T(8,128)(2,1)S(1)}, bf16[4,512,2048]{2,1,0:T(8,128)(2,1)}, u32[]{:S(2)}) copy-start(bf16[4,512,2048]{2,1,0:T(8,128)(2,1)} %v_ref.1) | copy-start | bytes 25165828
  91.6 32.0 %copy-start.3 = (bf16[5120,320]{0,1:T(8,128)(2,1)S(1)}, bf16[5120,320]{0,1:T(8,128)(2,1)}, u32[]{:S(2)}) copy-start(bf16[5120,320]{0,1:T(8,128)(2,1)} %param.14) | copy-start | bytes 9830404
  123.7 1.9 %copy-start.4 = (bf16[320,5120]{1,0:T(8,128)(2,1)S(1)}, bf16[320,5120]{1,0:T(8,128)(2,1)}, u32[]{:S(2)}) copy-start(bf16[320,5120]{1,0:T(8,128)(2,1)} %all-gather.2.cloned.1.call-done.new_ref) | copy-start | bytes 9830404
Sparse Core Ops, SparseCore 0:
  9.7 78.3 all-gather.1

commit v2 on v1

v2 whole, which is shorter than its diff:
```python
import functools

import jax
import jax.numpy as jnp
from jax import lax
from jax.experimental import pallas as pl
from jax.experimental.pallas import tpu as pltpu
from jax.sharding import PartitionSpec as P

D = 5120
HEADS = 40
KV_HEADS = 8
HEAD_DIM = 128
GROUP = HEADS // KV_HEADS
STEPS = 4
OLD_STEPS = 2
ROWS = 4
N_REP = 8
N_TP = 16
TOKENS = N_REP * ROWS * STEPS

NORM_EPSILON = 1e-06
ROPE_BASE = 1000000.0
MASK_VALUE = -1e30
SCORE_SCALE = 1.0 / HEAD_DIM**0.5

FEAT = D // N_TP
SHARD = FEAT // N_REP
LANES = 128
HALF_TP = N_TP // 2
N_X = 4
PART = FEAT // N_X
SLOTS = 8
USED = GROUP + 2
BLOCK = KV_HEADS * SLOTS
PER_CORE = KV_HEADS // 2
HALF_ROWS = PER_CORE * SLOTS
SUMS = HALF_ROWS + SLOTS
DESTS = N_X * HALF_TP
WIDE = 3 * LANES

f32 = jnp.float32
bf16 = jnp.bfloat16
MIB = 1 << 20

VMEM = pl.BlockSpec(memory_space=pltpu.VMEM)
SMEM = pl.BlockSpec(memory_space=pltpu.SMEM)
ANY = pl.BlockSpec(memory_space=pl.ANY)


def params(mib, grid=False):
    kwargs = dict(dimension_semantics=("arbitrary",) * grid) if grid else {}
    return pltpu.CompilerParams(vmem_limit_bytes=mib * MIB, **kwargs)

def gather_kernel(ids_ref, tail_ref, table_ref, out_ref, buf, cols, found, sems):
    window = table_ref.shape[1]
    tail_start = window // LANES * LANES
    start = lax.axis_index("rep") * window

    def local_id(i):
        step = ((i >> 5) & 1) * 2 + (i & 1)
        row = ((i >> 3) & 3) * 8 + (i >> 6) * 4 + ((i >> 1) & 3)
        return ids_ref[step, row] - start

    def note(i, count):
        local = local_id(i)
        found[count] = i
        return count + ((local >= 0) & (local < window)).astype(jnp.int32)

    count = lax.fori_loop(0, TOKENS, note, jnp.int32(0), unroll=32)

    def copy(j, local):
        base = pl.multiple_of((local >> 7) << 7, LANES)
        return pltpu.make_async_copy(
            table_ref.at[:, pl.ds(base, LANES)], buf.at[j], sems.at[j]
        )

    def begin(j, carry):
        local = local_id(found[j])

        @pl.when(local < tail_start)
        def _():
            copy(j, local).start()

        return carry

    lax.fori_loop(0, count, begin, 0)
    cols[...] = jnp.zeros_like(cols)
    lane = lax.broadcasted_iota(jnp.int32, (FEAT, LANES), 1)

    def place(i, local, block):
        shift = (i - local) & (LANES - 1)
        moved = pltpu.roll(block.astype(f32), shift, 1)
        cols[:FEAT] = jnp.where(lane == i, moved, cols[:FEAT])

    def end(j, carry):
        i = found[j]
        local = local_id(i)

        @pl.when(local < tail_start)
        def _():
            copy(j, local).wait()
            place(i, local, buf[j])

        @pl.when(local >= tail_start)
        def _():
            place(i, local, tail_ref[...])

        return carry

    lax.fori_loop(0, count, end, 0)
    rows = cols[...].T
    for zh in range(2):
        early = rows[zh * 64 : zh * 64 + DESTS]
        late = rows[zh * 64 + DESTS : zh * 64 + 2 * DESTS]
        tiles = [early[:, n * LANES : (n + 1) * LANES] for n in range(WIDE // LANES)]
        for xx in range(N_X):
            part = late[:, xx * PART : (xx + 1) * PART]
            blank = jnp.zeros((DESTS, LANES - PART), f32)
            block = jnp.concatenate(tiles + [jnp.concatenate([part, blank], axis=1)], axis=0)
            out_ref[xx * 2 + zh] = block.astype(bf16)


def gather_rows(token_ids, embed_table):
    table = embed_table.T
    tail = table.shape[1] // LANES
    return pl.pallas_call(
        gather_kernel,
        grid=(1,),
        in_specs=[SMEM, pl.BlockSpec((FEAT, LANES), lambda i: (0, tail)), ANY],
        out_specs=VMEM,
        out_shape=jax.ShapeDtypeStruct((N_REP, 4 * DESTS, LANES), bf16),
        scratch_shapes=[
            pltpu.VMEM((TOKENS, FEAT, LANES), bf16),
            pltpu.VMEM((WIDE, LANES), f32),
            pltpu.SMEM((TOKENS,), jnp.int32),
            pltpu.SemaphoreType.DMA((TOKENS,)),
        ],
        compiler_params=params(60),
        name="gather_rows",
    )(token_ids.T, table, table)


def project_kernel(x_ref, gain_ref, new_ref, other_ref, old_ref, keep_ref, send_ref, old, sems):
    rep, core = lax.axis_index("rep"), lax.axis_index("tp") & 1
    xx, zh = rep >> 1, rep & 1
    copies = []
    for n, (first, width, to) in enumerate(
        (
            (0, 2 * GROUP, 0),
            (HEADS, 2, 2 * GROUP),
            (HEADS + KV_HEADS, 2, 2 * GROUP + 2),
        )
    ):
        start = pl.multiple_of((first + xx * width) * HEAD_DIM, HEAD_DIM)
        copies.append(
            pltpu.make_async_copy(
                old_ref.at[:, pl.ds(start, width * HEAD_DIM)],
                old.at[:, pl.ds(to * HEAD_DIM, width * HEAD_DIM)],
                sems.at[n],
            )
        )
        copies[-1].start()
    embedded = jnp.sum(x_ref[...].astype(f32), axis=0)
    early = jnp.concatenate(
        [embedded[n * DESTS : (n + 1) * DESTS] for n in range(WIDE // LANES)], axis=1
    )
    late = embedded[3 * DESTS :]
    squares = [
        jnp.broadcast_to(jnp.sum(e * e, axis=1, keepdims=True), (DESTS, LANES))
        for e in (late, early)
    ]
    gain = gain_ref[...].astype(f32)
    part_gain = jnp.zeros((1, PART), f32)
    for i in range(N_X):
        part_gain = part_gain + jnp.where(xx == i, gain[:, i * PART : (i + 1) * PART], 0.0)
    early = (early[:, :FEAT] * gain).astype(bf16)
    late = (late[:, :PART] * part_gain).astype(bf16)
    first, second = late[:, :SHARD], late[:, SHARD:]
    late_own = jnp.where(zh == 0, first, second)
    late_other = jnp.where(zh == 0, second, first)

    def put(out_ref, group, slot, value):
        out_ref[pl.ds(group * SLOTS + slot, DESTS, stride=SUMS), :] = value

    for out_ref, side in ((keep_ref, core), (send_ref, 1 - core)):
        for j in range(PER_CORE):
            head = j * 2 + side
            starts = (
                (head * (GROUP * HEAD_DIM), GROUP, 0),
                (HEADS * HEAD_DIM + head * HEAD_DIM, 1, GROUP),
                ((HEADS + KV_HEADS) * HEAD_DIM + head * HEAD_DIM, 1, GROUP + 1),
            )
            for start, width, slot in starts:
                columns = pl.ds(pl.multiple_of(start, HEAD_DIM), width * HEAD_DIM)
                sums = jnp.dot(
                    late_own, new_ref[:, columns], preferred_element_type=f32
                ) + jnp.dot(late_other, other_ref[:, columns], preferred_element_type=f32)
                for g in range(width):
                    put(out_ref, j, slot + g, sums[:, g * HEAD_DIM : (g + 1) * HEAD_DIM])
            put(out_ref, j, SLOTS - 1, squares[0])
    for copy in copies:
        copy.wait()
    sums = jnp.dot(early, old[...], preferred_element_type=f32)
    for slot in range(USED):
        at = (slot, slot + GROUP) if slot < GROUP else (slot * 2, slot * 2 + 1)
        both = [sums[:, a * HEAD_DIM : (a + 1) * HEAD_DIM] for a in at]
        put(keep_ref, PER_CORE, slot, jnp.where(core == 0, both[0], both[1]))
        put(send_ref, PER_CORE, slot, jnp.where(core == 0, both[1], both[0]))
    for out_ref in (keep_ref, send_ref):
        put(out_ref, PER_CORE, SLOTS - 1, squares[1])


def project(received, norm_gain, new_qkv, other_qkv, old_qkv):
    out = jax.ShapeDtypeStruct((DESTS * SUMS, LANES), f32)
    return pl.pallas_call(
        project_kernel,
        in_specs=[VMEM, VMEM, VMEM, VMEM, ANY],
        out_specs=[VMEM, VMEM],
        out_shape=[out, out],
        scratch_shapes=[
            pltpu.VMEM((FEAT, 2 * USED * HEAD_DIM), bf16),
            pltpu.SemaphoreType.DMA((3,)),
        ],
        compiler_params=params(56),
        name="project",
    )(received, norm_gain.reshape(1, FEAT), new_qkv, other_qkv, old_qkv)


def add_kernel(a_ref, b_ref, out_ref):
    out_ref[...] = a_ref[...] + b_ref[...]


def add(a, b):
    return pl.pallas_call(
        add_kernel,
        in_specs=[VMEM, VMEM],
        out_specs=VMEM,
        out_shape=jax.ShapeDtypeStruct(a.shape, a.dtype),
        compiler_params=params(16),
        name="add",
    )(a, b)


def finish_kernel(x_ref, cos_ref, sin_ref, out_ref):
    parts = x_ref[...].reshape(N_X, HALF_TP, SUMS, LANES)
    late = jnp.sum(jnp.sum(parts[:, :, :HALF_ROWS], axis=1), axis=0)
    early = jnp.sum(parts[:, :, HALF_ROWS:], axis=1)
    summed = jnp.concatenate([early.reshape(HALF_ROWS, LANES), late], axis=0).reshape(
        2, PER_CORE, SLOTS, LANES
    )
    squares = summed[:, :, SLOTS - 1 :, :]
    normed = summed / jnp.sqrt(squares / D + NORM_EPSILON)
    swapped = pltpu.roll(normed.reshape(BLOCK, LANES), HEAD_DIM // 2, 1).reshape(normed.shape)
    rotated = normed * cos_ref[...].reshape(2, 1, 1, LANES) + swapped * sin_ref[...].reshape(
        2, 1, 1, LANES
    )
    slot = lax.broadcasted_iota(jnp.int32, normed.shape, 2)
    result = jnp.where(slot <= GROUP, rotated, jnp.where(slot == GROUP + 1, normed, 0.0))
    out_ref[...] = jnp.broadcast_to(
        result.reshape(1, BLOCK, LANES).astype(bf16), out_ref.shape
    )


def finish(received, cosine, sine):
    return pl.pallas_call(
        finish_kernel,
        in_specs=[VMEM, VMEM, VMEM],
        out_specs=VMEM,
        out_shape=jax.ShapeDtypeStruct((N_TP, BLOCK, LANES), bf16),
        compiler_params=params(16),
        name="finish",
    )(received, cosine, sine)


def attend_kernel(len_ref, q_ref, k_ref, v_ref, out_ref, scores_ref, weights_ref):
    row = pl.program_id(0)
    tp = lax.axis_index("tp")
    chunk = k_ref.shape[1]
    count = STEPS * SLOTS
    blocks = [(row * 2 + s % 2) * 2 for s in range(STEPS)]
    rows_of = [slice(s // 2 * HALF_ROWS, (s // 2 + 1) * HALF_ROWS) for s in range(STEPS)]
    contract_last = (((1,), (1,)), ((), ()))
    by_core = [
        jnp.stack(
            [
                q_ref[b + core, r].astype(f32).reshape(PER_CORE, SLOTS, LANES)
                for b, r in zip(blocks, rows_of)
            ],
            axis=1,
        )
        for core in range(2)
    ]
    wide = jnp.stack(by_core, axis=1).reshape(KV_HEADS, count, LANES)
    queries = [wide[h].astype(bf16) for h in range(KV_HEADS)]
    shifted = [pltpu.roll(wide[h], count - 1, 0).astype(bf16) for h in range(KV_HEADS)]
    new = []
    for h in range(KV_HEADS):
        columns = slice(h * HEAD_DIM, (h + 1) * HEAD_DIM)
        scores_ref[h * count : (h + 1) * count, :] = lax.dot_general(
            queries[h], k_ref[0, :, columns], contract_last, preferred_element_type=f32
        )
        new.append(
            lax.dot_general(queries[h], queries[h], contract_last, preferred_element_type=f32)
        )
    valid = len_ref[row] - tp * chunk
    shape = scores_ref.shape
    position = lax.broadcasted_iota(jnp.int32, shape, 1)
    scores = jnp.where(position < valid, scores_ref[...] * SCORE_SCALE, MASK_VALUE)
    from_step = (lax.broadcasted_iota(jnp.int32, (shape[0], count), 0) >> 3) & (STEPS - 1)
    column = lax.broadcasted_iota(jnp.int32, (shape[0], count), 1)
    new_mask = ((column & (SLOTS - 1)) == GROUP) & ((column >> 3) <= from_step) & (tp == 0)
    scores_new = jnp.where(new_mask, jnp.concatenate(new, axis=0) * SCORE_SCALE, MASK_VALUE)
    peak = jnp.maximum(
        jnp.max(scores, axis=1, keepdims=True), jnp.max(scores_new, axis=1, keepdims=True)
    )
    weights = jnp.exp(scores - peak).astype(bf16)
    weights_new = jnp.exp(scores_new - peak).astype(bf16)
    weights_ref[...] = weights
    total = jnp.sum(weights.astype(f32), axis=1, keepdims=True) + jnp.sum(
        weights_new.astype(f32), axis=1, keepdims=True
    )
    numerator = []
    for h in range(KV_HEADS):
        columns = slice(h * HEAD_DIM, (h + 1) * HEAD_DIM)
        rows = slice(h * count, (h + 1) * count)
        numerator.append(
            jnp.dot(weights_ref[rows, :], v_ref[0, :, columns], preferred_element_type=f32)
            + jnp.dot(weights_new[rows], shifted[h], preferred_element_type=f32)
        )
    grouped = (KV_HEADS, STEPS, SLOTS, LANES)
    part = (jnp.concatenate(numerator, axis=0) / total).reshape(grouped)
    slot = lax.broadcasted_iota(jnp.int32, grouped, 2)
    diagonal = slot == lax.broadcasted_iota(jnp.int32, grouped, 3)
    log_total = jnp.broadcast_to(peak + jnp.log(total), (shape[0], LANES)).reshape(grouped)
    log_row = jnp.sum(jnp.where(diagonal, log_total, 0.0), axis=2, keepdims=True)
    high = log_row.astype(bf16).astype(f32)
    middle = (log_row - high).astype(bf16).astype(f32)
    low = log_row - high - middle
    part = jnp.where(
        slot < GROUP,
        part,
        jnp.where(slot == GROUP, high, jnp.where(slot == GROUP + 1, middle, low)),
    )
    by_core = part.reshape(PER_CORE, 2, STEPS, SLOTS, LANES)
    for core in range(2):
        for s, (b, r) in enumerate(zip(blocks, rows_of)):
            out_ref[b + core, r] = by_core[:, core, s].reshape(HALF_ROWS, LANES).astype(bf16)


def attend(cache_len, gathered, kv_cache):
    chunk = kv_cache.shape[1]
    width = KV_HEADS * HEAD_DIM
    whole = pl.BlockSpec((N_TP, BLOCK, LANES), lambda r: (0, 0, 0))
    lines = KV_HEADS * STEPS * SLOTS
    return pl.pallas_call(
        attend_kernel,
        grid=(ROWS,),
        in_specs=[
            SMEM,
            whole,
            pl.BlockSpec((1, chunk, width), lambda r: (r, 0, 0)),
            pl.BlockSpec((1, chunk, width), lambda r: (r, 0, 1)),
        ],
        out_specs=whole,
        out_shape=jax.ShapeDtypeStruct((N_TP, BLOCK, LANES), bf16),
        scratch_shapes=[pltpu.VMEM((lines, chunk), f32), pltpu.VMEM((lines, chunk), bf16)],
        compiler_params=params(60, 1),
        name="attend",
    )(cache_len, gathered, kv_cache, kv_cache)


def merge_kernel(x_ref, out_ref):
    x = x_ref[...].astype(f32).reshape(N_TP, KV_HEADS, SLOTS, LANES)
    log_row = jnp.sum(x[:, :, GROUP:, :], axis=2, keepdims=True)
    slot = lax.broadcasted_iota(jnp.int32, x.shape, 2)
    lane = lax.broadcasted_iota(jnp.int32, x.shape, 3)
    log_total = jnp.sum(jnp.where(slot == lane, log_row, 0.0), axis=3, keepdims=True)
    share = jnp.exp(log_total - jnp.max(log_total, axis=0, keepdims=True))
    heads = jnp.sum(share * x, axis=0) / jnp.sum(share, axis=0)
    packed = jnp.concatenate([heads[h, :GROUP] for h in range(KV_HEADS)], axis=0)
    out_ref[...] = jnp.broadcast_to(packed.astype(bf16)[None], out_ref.shape)


def merge(received):
    return pl.pallas_call(
        merge_kernel,
        in_specs=[VMEM],
        out_specs=VMEM,
        out_shape=jax.ShapeDtypeStruct((N_TP, HEADS, LANES), bf16),
        compiler_params=params(16),
        name="merge",
    )(received)


def output_kernel(x_ref, old_ref, new_ref, out_ref, wide, heads, early_sum, late_sum):
    step = pl.program_id(0)

    @pl.when(step == 0)
    def _():
        wide[...] = x_ref[...].astype(f32).reshape(wide.shape)
        early_sum[...] = jnp.zeros_like(early_sum)
        late_sum[...] = jnp.zeros_like(late_sum)
        per_step = HEADS // heads.shape[0]
        for h in range(HEADS):
            kv = h // GROUP
            at = kv % 2 * HEADS + kv // 2 * GROUP + h % GROUP
            rows = [wide[pl.ds(at + el * HEADS // 2, HALF_TP, stride=2 * HEADS), :] for el in range(2)]
            at = h % per_step * HEAD_DIM
            heads[h // per_step, :, at : at + HEAD_DIM] = jnp.concatenate(rows, axis=0).astype(
                bf16
            )

    contract_last = (((1,), (1,)), ((), ()))
    both = heads[step]
    early_sum[...] += lax.dot_general(
        both[:HALF_TP], old_ref[...], contract_last, preferred_element_type=f32
    )
    late_sum[...] += lax.dot_general(
        both[HALF_TP:], new_ref[...], contract_last, preferred_element_type=f32
    )

    @pl.when(step == pl.num_programs(0) - 1)
    def _():
        for r in range(ROWS):
            for el, total in enumerate((early_sum, late_sum)):
                out_ref[r, el * 2 : el * 2 + 2, :] = total[r * 2 : r * 2 + 2, :].astype(bf16)


def output(gathered, old_out, fresh_out):
    blocks = 4
    depth = D // blocks
    return pl.pallas_call(
        output_kernel,
        grid=(blocks,),
        in_specs=[
            pl.BlockSpec((N_TP, HEADS, LANES), lambda i: (0, 0, 0)),
            pl.BlockSpec((FEAT, depth), lambda i: (0, i)),
            pl.BlockSpec((FEAT, depth), lambda i: (0, i)),
        ],
        out_specs=pl.BlockSpec((ROWS, STEPS, FEAT), lambda i: (0, 0, 0)),
        out_shape=jax.ShapeDtypeStruct((ROWS, STEPS, FEAT), bf16),
        scratch_shapes=[
            pltpu.VMEM((N_TP * HEADS, LANES), f32),
            pltpu.VMEM((blocks, N_TP, depth), bf16),
            pltpu.VMEM((HALF_TP, FEAT), f32),
            pltpu.VMEM((HALF_TP, FEAT), f32),
        ],
        compiler_params=params(60, 1),
        name="output",
    )(gathered, old_out.T, fresh_out)


def rotation(cache_len):
    tp = lax.axis_index("tp")
    half_dim = HEAD_DIM // 2
    inverse_freq = ROPE_BASE ** (-jnp.arange(half_dim, dtype=f32) * 2.0 / HEAD_DIM)
    positions = cache_len[tp >> 2] + ((tp >> 1) & 1) + 2 * jnp.arange(2, dtype=jnp.int32)
    angles = positions.astype(f32)[:, None] * inverse_freq[None, :]
    cosine, sine = jnp.cos(angles), jnp.sin(angles)
    return (
        jnp.concatenate([cosine, cosine], axis=1),
        jnp.concatenate([-sine, sine], axis=1),
    )


def body(
    token_ids, cache_len, embed_table, norm_gain, old_qkv, old_out, new_qkv, new_out, kv_cache
):
    fresh_out = lax.all_gather(new_out.T, "rep", axis=0, tiled=True)
    other_qkv = lax.ppermute(new_qkv, "rep", [(r, r ^ 1) for r in range(N_REP)])
    cosine, sine = rotation(cache_len)
    rows = lax.all_to_all(gather_rows(token_ids, embed_table), "rep", 0, 0)
    keep, send = project(rows, norm_gain, new_qkv, other_qkv, old_qkv)
    arrived = lax.ppermute(send, "tp", [(t, t ^ 1) for t in range(N_TP)])
    summed = add(keep, arrived).reshape(DESTS, SUMS, LANES)
    groups = [
        [(x * 2 + zh) * N_TP + k * 2 + core for x in range(N_X) for k in range(HALF_TP)]
        for zh in range(2)
        for core in range(2)
    ]
    partials = lax.all_to_all(summed, ("rep", "tp"), 0, 0, axis_index_groups=groups)
    projected = lax.all_to_all(finish(partials, cosine, sine), "tp", 0, 0)
    parts = lax.all_to_all(attend(cache_len, projected, kv_cache), "tp", 0, 0)
    heads = lax.all_to_all(merge(parts), "tp", 0, 0)
    return output(heads, old_out, fresh_out)


def solution(mesh):
    in_specs = (
        P(),
        P("rep"),
        P("rep", "tp"),
        P("tp"),
        P("tp", None),
        P(None, "tp"),
        P(("tp", "rep"), None),
        P(None, ("tp", "rep")),
        P("rep", "tp", None),
    )
    out_specs = P("rep", None, "tp")
    return jax.shard_map(body, mesh=mesh, in_specs=in_specs, out_specs=out_specs, check_vma=False)
```

time: 136 us -> 119 us (0.88)
  local copies, waits for them, and re-layouts: 11.6 us -> 3.78 us
  Pallas kernels: 30.9 us -> 24.7 us
  starting transfers between devices: 19.4 us -> 17.8 us
  waiting for transfers between devices: 26.2 us -> 24.6 us
    pallas_call x2 -> x3, Pallas kernels: 24.6 us -> 14.3 us  [the longest x1 6.88 us: gather_rows(): pl.pallas_call(gather_kernel, grid=(1,), in_specs=[SMEM, pl.BlockSpec((FE...]
    unnamed x18 -> x10, local copies, waits for them, and re-layouts: 11 us -> 2.63 us
    all_to_all x1, waiting for transfers between devices: 16.4 us -> 13.7 us  [body(): lax.all_to_all(summed, ('rep', 'tp'), 0, 0, axis_index_groups=groups)]
    all_to_all x1, starting transfers between devices: 6.47 us -> 3.99 us  [body(): rows = lax.all_to_all(gather_rows(token_ids, embed_table), 'rep', 0, 0)]
    pallas_call x1, Pallas kernels: 2.27 us -> 4.54 us  [project(): pl.pallas_call(project_kernel, in_specs=[VMEM, VMEM, VMEM, VMEM, ANY], ou...]
    pallas_call x1, Pallas kernels: 3.47 us -> 5.31 us  [output(): pl.pallas_call(output_kernel, grid=(blocks,), in_specs=[pl.BlockSpec((N_T...]
    all_to_all x1, waiting for transfers between devices: 6.73 us -> 8.24 us  [body(): rows = lax.all_to_all(gather_rows(token_ids, embed_table), 'rep', 0, 0)]
  transfers between devices with their start and end apart: 5 -> 5, of which waited for: 3 -> 3; matrix products, arithmetic and copies ran while one was open for 1% -> 1% of each run, Pallas kernels for 20% -> 16%
where the time goes in v2:
time: 119 us; the launch traced here: 118 us
  blocking collectives  32.9 us (28%)
  Pallas kernels  24.7 us (21%)
  waiting for transfers between devices  24.6 us (21%)
  starting transfers between devices  17.8 us (15%)
  between operations  14.1 us (12%)
  local copies, waits for them, and re-layouts  3.78 us (3%)
    all_to_all x1, waiting for transfers between devices, body(): lax.all_to_all(summed, ('rep', 'tp'), 0, 0, axis_index_groups=groups)  13.7 us
    all_to_all x1, blocking collectives, body(): projected = lax.all_to_all(finish(partials, cosine, sine), 'tp', 0, 0)  11.7 us
    all_to_all x1, blocking collectives, body(): parts = lax.all_to_all(attend(cache_len, projected, kv_cache), 'tp', 0, 0)  11.2 us
    all_to_all x1, blocking collectives, body(): heads = lax.all_to_all(merge(parts), 'tp', 0, 0)  10 us
    all_to_all x1, waiting for transfers between devices, body(): rows = lax.all_to_all(gather_rows(token_ids, embed_table), 'rep', 0, 0)  8.24 us
    pallas_call x1, Pallas kernels, gather_rows(): pl.pallas_call(gather_kernel, grid=(1,), in_specs=[SMEM, pl.BlockSpec((FE...  6.88 us
    all_to_all x1, starting transfers between devices, body(): lax.all_to_all(summed, ('rep', 'tp'), 0, 0, axis_index_groups=groups)  6.87 us
    pallas_call x1, Pallas kernels, attend(): pl.pallas_call(attend_kernel, grid=(ROWS,), in_specs=[SMEM, whole, pl.Blo...  6.55 us
  transfers between devices with their start and end apart: 5, of which 3 were waited for; matrix products, arithmetic and copies ran while one was open for 1% of the time, Pallas kernels for 16%

profile of v2, /device:TPU:1, one launch (start us, length us, event | category | flops | bytes accessed | tf_op | source)
XLA Modules:
  0.0 118.1 jit_solution(13268879165115882477)
XLA Ops:
  6.5 0.0 all-gather.2.cloned.1.call-start
  6.5 0.7 all-gather.2.cloned.1.call-update
  7.3 4.5 %collective-permute-start = (bf16[40,7168]{1,0:T(8,128)(2,1)}, bf16[40,7168]{1,0:T(8,128)(2,1)S(1)}, u32[]{:S(2)}, u32[]{:S(2)}) collective-permute-start(bf16[40,7168]{1,0:T(8,128)(2,1)} %new_ref.1), channel_id=1, source_target_pairs={{0,16},{16,0},{32,48},{48,32},{64,80},{80,64},{96,112},{112,96},{1... | collective-permute-start | bytes 1720328 | tf_op jit(solution)/shard_map/ppermute | solution.py:471
  11.8 0.0 copy-start.3
  11.8 6.9 %gather_rows.1 = bf16[8,128,128]{2,1,0:T(8,128)(2,1)} custom-call(s32[4,32]{1,0:T(4,128)} %bitcast.10, bf16[320,9504]{1,0:T(8,128)(2,1)} %bitcast.6, bf16[320,9504]{1,0:T(8,128)(2,1)} %bitcast.7), custom_call_target="tpu_custom_call" | custom-call | tf_op jit(solution)/shard_map/gather_rows/pallas_call | solution.py:127
  18.7 4.0 %all-to-all-start = ((bf16[8,128,128]{2,1,0:T(8,128)(2,1)}), bf16[8,128,128]{2,1,0:T(8,128)(2,1)S(1)}, u32[]{:S(2)}, u32[]{:S(2)}) async-start(bf16[8,128,128]{2,1,0:T(8,128)(2,1)} %gather_rows.1), calls=%async_computation | async-start | bytes 524288 | tf_op jit(solution)/shard_map/all_to_all | solution.py:473
  22.6 0.0 copy-done.3
  22.6 0.6 reshape.18.gain_ref
  23.2 0.0 copy-start.4
  23.2 8.2 %all-to-all-done.x_ref = bf16[8,128,128]{2,1,0:T(8,128)(2,1)S(1)} async-done(((bf16[8,128,128]{2,1,0:T(8,128)(2,1)}), bf16[8,128,128]{2,1,0:T(8,128)(2,1)S(1)}, u32[]{:S(2)}, u32[]{:S(2)}) %all-to-all-start) | async-done | bytes 262176 | tf_op jit(solution)/shard_map/all_to_all | solution.py:473
  31.5 0.0 copy-start.1
  31.5 0.0 collective-permute-done.other_ref
  31.5 0.7 copy-done.1
  32.2 0.0 copy-start.2
  32.2 0.8 copy-done.2
  33.0 4.5 %project.1 = (f32[1280,128]{1,0:T(8,128)}, f32[1280,128]{1,0:T(8,128)}) custom-call(bf16[8,128,128]{2,1,0:T(8,128)(2,1)} %copy-done.1, bf16[1,320]{1,0:T(2,128)(2,1)} %reshape.18.gain_ref, bf16[40,7168]{1,0:T(8,128)(2,1)} %new_ref.1, bf16[40,7168]{1,0:T(8,128)(2,1)} %copy-done.2, bf16[320,7168]{1,0:T(8,128)(2,1)} %old_ref.1), custom_call_target="tpu_custom_call" | custom-call | tf_op jit(solution)/shard_map/project/pallas_call | solution.py:216
  37.5 2.5 %collective-permute-start.1 = (f32[1280,128]{1,0:T(8,128)}, f32[1280,128]{1,0:T(8,128)S(1)}, u32[]{:S(2)}, u32[]{:S(2)}) collective-permute-start(f32[1280,128]{1,0:T(8,128)} %get-tuple-element.8), channel_id=1, source_target_pairs={{0,1},{1,0},{2,3},{3,2},{4,5},{5,4},{6,7},{7,6},{8,9},{9,8},{10,11... | collective-permute-start | bytes 1966088 | tf_op jit(solution)/shard_map/ppermute | solution.py:475
  40.0 1.9 %collective-permute-done.1.b_ref = f32[1280,128]{1,0:T(8,128)S(1)} collective-permute-done((f32[1280,128]{1,0:T(8,128)}, f32[1280,128]{1,0:T(8,128)S(1)}, u32[]{:S(2)}, u32[]{:S(2)}) %collective-permute-start.1) | collective-permute-done | bytes 655392 | tf_op jit(solution)/shard_map/ppermute | solution.py:475
  41.9 0.0 copy-start
  41.9 1.1 copy-done
  43.0 0.9 add.23
  43.9 6.9 %all-to-all-start.1 = ((f32[32,40,128]{2,1,0:T(8,128)}), f32[32,40,128]{2,1,0:T(8,128)S(1)}, u32[]{:S(2)}, u32[]{:S(2)}) async-start(f32[32,40,128]{2,1,0:T(8,128)} %bitcast.2), calls=%async_computation.1 | async-start | bytes 1310720 | tf_op jit(solution)/shard_map/all_to_all | solution.py:482
  50.8 0.0 copy-done.4
  50.8 0.6 dynamic_slice.3
  52.1 0.1 fusion
  52.2 0.1 pad_maximum_fusion
  52.3 13.7 %all-to-all-done.1.x_ref = f32[32,40,128]{2,1,0:T(8,128)S(1)} async-done(((f32[32,40,128]{2,1,0:T(8,128)}), f32[32,40,128]{2,1,0:T(8,128)S(1)}, u32[]{:S(2)}, u32[]{:S(2)}) %all-to-all-start.1) | async-done | bytes 655392 | tf_op jit(solution)/shard_map/all_to_all | solution.py:482
  66.0 0.1 finish.1
  66.1 11.7 %all_to_all.25.q_ref = bf16[16,64,128]{2,1,0:T(8,128)(2,1)} all-to-all(bf16[16,64,128]{2,1,0:T(8,128)(2,1)S(1)} %finish.1), channel_id=1, replica_groups=mesh['rep'=8,'tp'=16] {'tp'}, dimensions={0} | all-to-all | bytes 524288 | tf_op jit(solution)/shard_map/all_to_all | solution.py:483
  77.8 6.6 %attend.1 = bf16[16,64,128]{2,1,0:T(8,128)(2,1)} custom-call(s32[4]{0:T(128)} %len_ref.1, bf16[16,64,128]{2,1,0:T(8,128)(2,1)} %all_to_all.25.q_ref, bf16[4,512,2048]{2,1,0:T(8,128)(2,1)} %v_ref.1, bf16[4,512,2048]{2,1,0:T(8,128)(2,1)} %v_ref.1), custom_call_target="tpu_custom_call" | custom-call | tf_op jit(solution)/shard_map/attend/pallas_call | solution.py:356
  84.4 11.2 %all_to_all.26.x_ref = bf16[16,64,128]{2,1,0:T(8,128)(2,1)S(1)} all-to-all(bf16[16,64,128]{2,1,0:T(8,128)(2,1)} %attend.1), channel_id=1, replica_groups=mesh['rep'=8,'tp'=16] {'tp'}, dimensions={0} | all-to-all | bytes 524288 | tf_op jit(solution)/shard_map/all_to_all | solution.py:484
  95.6 0.4 merge.1
  95.9 10.0 %all_to_all.27.x_ref = bf16[16,40,128]{2,1,0:T(8,128)(2,1)} all-to-all(bf16[16,40,128]{2,1,0:T(8,128)(2,1)S(1)} %merge.1), channel_id=1, replica_groups=mesh['rep'=8,'tp'=16] {'tp'}, dimensions={0} | all-to-all | bytes 327680 | tf_op jit(solution)/shard_map/all_to_all | solution.py:485
  106.0 0.0 all-gather.2.cloned.1.call-done.new_ref
  106.0 5.3 %output.1 = bf16[4,4,320]{2,1,0:T(4,128)(2,1)} custom-call(bf16[16,40,128]{2,1,0:T(8,128)(2,1)} %all_to_all.27.x_ref, bf16[320,5120]{1,0:T(8,128)(2,1)} %bitcast.8, bf16[320,5120]{1,0:T(8,128)(2,1)} %all-gather.2.cloned.1.call-done.new_ref), custom_call_target="tpu_custom_call" | custom-call | tf_op jit(solution)/shard_map/output/pallas_call | solution.py:433
  (2 shorter events, 0.0 us)
Async XLA Ops:
  6.5 99.4 %all-gather.2.cloned.1.call-start = ((), (), s32[]{:S(2)}) async-start(), calls=%async_computation.5 | async-start | bytes 3686400 | tf_op jit(solution)/shard_map/all_gather | solution.py:470
  7.3 24.2 %collective-permute-start = (bf16[40,7168]{1,0:T(8,128)(2,1)}, bf16[40,7168]{1,0:T(8,128)(2,1)S(1)}, u32[]{:S(2)}, u32[]{:S(2)}) collective-permute-start(bf16[40,7168]{1,0:T(8,128)(2,1)} %new_ref.1), channel_id=1, source_target_pairs={{0,16},{16,0},{32,48},{48,32},{64,80},{80,64},{96,112},{112,96},{1... | collective-permute-start | bytes 1720328 | tf_op jit(solution)/shard_map/ppermute | solution.py:471
  11.8 10.9 %copy-start.3 = (bf16[320]{0:T(512)(128)(2,1)S(1)}, bf16[320]{0:T(512)(128)(2,1)}, u32[]{:S(2)}) copy-start(bf16[320]{0:T(512)(128)(2,1)} %param.12) | copy-start | bytes 1924
  18.7 12.8 %all-to-all-start = ((bf16[8,128,128]{2,1,0:T(8,128)(2,1)}), bf16[8,128,128]{2,1,0:T(8,128)(2,1)S(1)}, u32[]{:S(2)}, u32[]{:S(2)}) async-start(bf16[8,128,128]{2,1,0:T(8,128)(2,1)} %gather_rows.1), calls=%async_computation | async-start | bytes 524288 | tf_op jit(solution)/shard_map/all_to_all | solution.py:473
  23.2 27.6 %copy-start.4 = (s32[4]{0:T(128)S(1)}, s32[4]{0:T(128)}, u32[]{:S(2)}) copy-start(s32[4]{0:T(128)} %len_ref.1) | copy-start | bytes 52
  31.5 0.7 copy-start.1
  32.2 0.8 copy-start.2
  37.5 4.4 %collective-permute-start.1 = (f32[1280,128]{1,0:T(8,128)}, f32[1280,128]{1,0:T(8,128)S(1)}, u32[]{:S(2)}, u32[]{:S(2)}) collective-permute-start(f32[1280,128]{1,0:T(8,128)} %get-tuple-element.8), channel_id=1, source_target_pairs={{0,1},{1,0},{2,3},{3,2},{4,5},{5,4},{6,7},{7,6},{8,9},{9,8},{10,11... | collective-permute-start | bytes 1966088 | tf_op jit(solution)/shard_map/ppermute | solution.py:475
  41.9 1.1 copy-start
  43.9 22.0 %all-to-all-start.1 = ((f32[32,40,128]{2,1,0:T(8,128)}), f32[32,40,128]{2,1,0:T(8,128)S(1)}, u32[]{:S(2)}, u32[]{:S(2)}) async-start(f32[32,40,128]{2,1,0:T(8,128)} %bitcast.2), calls=%async_computation.1 | async-start | bytes 1310720 | tf_op jit(solution)/shard_map/all_to_all | solution.py:482
Sparse Core Ops, SparseCore 0:
  9.7 79.4 all-gather.1

commit v3 on v2

--- a/solution.py
+++ b/solution.py
@@ -136,14 +136,13 @@
             pltpu.SMEM((TOKENS,), jnp.int32),
             pltpu.SemaphoreType.DMA((TOKENS,)),
         ],
-        compiler_params=params(60),
+        compiler_params=params(55),
         name="gather_rows",
     )(token_ids.T, table, table)
 
 
-def project_kernel(x_ref, gain_ref, new_ref, other_ref, old_ref, keep_ref, send_ref, old, sems):
-    rep, core = lax.axis_index("rep"), lax.axis_index("tp") & 1
-    xx, zh = rep >> 1, rep & 1
+def old_columns_kernel(old_ref, out_ref, sems):
+    xx = lax.axis_index("rep") >> 1
     copies = []
     for n, (first, width, to) in enumerate(
         (
@@ -152,15 +151,38 @@
             (HEADS + KV_HEADS, 2, 2 * GROUP + 2),
         )
     ):
-        start = pl.multiple_of((first + xx * width) * HEAD_DIM, HEAD_DIM)
+        at = pl.multiple_of((first + xx * width) * HEAD_DIM, HEAD_DIM)
         copies.append(
             pltpu.make_async_copy(
-                old_ref.at[:, pl.ds(start, width * HEAD_DIM)],
-                old.at[:, pl.ds(to * HEAD_DIM, width * HEAD_DIM)],
+                old_ref.at[:, pl.ds(at, width * HEAD_DIM)],
+                out_ref.at[:, pl.ds(to * HEAD_DIM, width * HEAD_DIM)],
                 sems.at[n],
             )
         )
         copies[-1].start()
+    for copy in copies:
+        copy.wait()
+
+
+def take_old_columns(old_qkv):
+    shape = (FEAT, 2 * USED * HEAD_DIM)
+    return pl.pallas_call(
+        old_columns_kernel,
+        in_specs=[ANY],
+        out_specs=VMEM,
+        out_shape=jax.ShapeDtypeStruct(shape, bf16),
+        scratch_shapes=[pltpu.SemaphoreType.DMA((3,))],
+        compiler_params=params(8),
+        cost_estimate=pl.CostEstimate(
+            flops=0, bytes_accessed=4 * shape[0] * shape[1], transcendentals=0
+        ),
+        name="take_old_columns",
+    )(old_qkv)
+
+
+def project_kernel(x_ref, gain_ref, new_ref, other_ref, old, keep_ref, send_ref):
+    rep, core = lax.axis_index("rep"), lax.axis_index("tp") & 1
+    xx, zh = rep >> 1, rep & 1
     embedded = jnp.sum(x_ref[...].astype(f32), axis=0)
     early = jnp.concatenate(
         [embedded[n * DESTS : (n + 1) * DESTS] for n in range(WIDE // LANES)], axis=1
@@ -199,8 +221,6 @@
                 for g in range(width):
                     put(out_ref, j, slot + g, sums[:, g * HEAD_DIM : (g + 1) * HEAD_DIM])
             put(out_ref, j, SLOTS - 1, squares[0])
-    for copy in copies:
-        copy.wait()
     sums = jnp.dot(early, old[...], preferred_element_type=f32)
     for slot in range(USED):
         at = (slot, slot + GROUP) if slot < GROUP else (slot * 2, slot * 2 + 1)
@@ -211,20 +231,16 @@
         put(out_ref, PER_CORE, SLOTS - 1, squares[1])
 
 
-def project(received, norm_gain, new_qkv, other_qkv, old_qkv):
+def project(received, norm_gain, new_qkv, other_qkv, old_columns):
     out = jax.ShapeDtypeStruct((DESTS * SUMS, LANES), f32)
     return pl.pallas_call(
         project_kernel,
-        in_specs=[VMEM, VMEM, VMEM, VMEM, ANY],
+        in_specs=[VMEM] * 5,
         out_specs=[VMEM, VMEM],
         out_shape=[out, out],
-        scratch_shapes=[
-            pltpu.VMEM((FEAT, 2 * USED * HEAD_DIM), bf16),
-            pltpu.SemaphoreType.DMA((3,)),
-        ],
-        compiler_params=params(56),
+        compiler_params=params(16),
         name="project",
-    )(received, norm_gain.reshape(1, FEAT), new_qkv, other_qkv, old_qkv)
+    )(received, norm_gain.reshape(1, FEAT), new_qkv, other_qkv, old_columns)
 
 
 def add_kernel(a_ref, b_ref, out_ref):
@@ -269,14 +285,16 @@
         out_specs=VMEM,
         out_shape=jax.ShapeDtypeStruct((N_TP, BLOCK, LANES), bf16),
         compiler_params=params(16),
+        cost_estimate=pl.CostEstimate(flops=0, bytes_accessed=32 * MIB, transcendentals=0),
         name="finish",
     )(received, cosine, sine)
 
 
-def attend_kernel(len_ref, q_ref, k_ref, v_ref, out_ref, scores_ref, weights_ref):
+def attend_kernel(len_ref, q_ref, kv_ref, out_ref, scores_ref, weights_ref):
     row = pl.program_id(0)
     tp = lax.axis_index("tp")
-    chunk = k_ref.shape[1]
+    chunk = kv_ref.shape[1]
+    value_at = KV_HEADS * HEAD_DIM
     count = STEPS * SLOTS
     blocks = [(row * 2 + s % 2) * 2 for s in range(STEPS)]
     rows_of = [slice(s // 2 * HALF_ROWS, (s // 2 + 1) * HALF_ROWS) for s in range(STEPS)]
@@ -298,7 +316,7 @@
     for h in range(KV_HEADS):
         columns = slice(h * HEAD_DIM, (h + 1) * HEAD_DIM)
         scores_ref[h * count : (h + 1) * count, :] = lax.dot_general(
-            queries[h], k_ref[0, :, columns], contract_last, preferred_element_type=f32
+            queries[h], kv_ref[row, :, columns], contract_last, preferred_element_type=f32
         )
         new.append(
             lax.dot_general(queries[h], queries[h], contract_last, preferred_element_type=f32)
@@ -322,10 +340,10 @@
     )
     numerator = []
     for h in range(KV_HEADS):
-        columns = slice(h * HEAD_DIM, (h + 1) * HEAD_DIM)
+        columns = slice(value_at + h * HEAD_DIM, value_at + (h + 1) * HEAD_DIM)
         rows = slice(h * count, (h + 1) * count)
         numerator.append(
-            jnp.dot(weights_ref[rows, :], v_ref[0, :, columns], preferred_element_type=f32)
+            jnp.dot(weights_ref[rows, :], kv_ref[row, :, columns], preferred_element_type=f32)
             + jnp.dot(weights_new[rows], shifted[h], preferred_element_type=f32)
         )
     grouped = (KV_HEADS, STEPS, SLOTS, LANES)
@@ -350,7 +368,6 @@
 
 def attend(cache_len, gathered, kv_cache):
     chunk = kv_cache.shape[1]
-    width = KV_HEADS * HEAD_DIM
     whole = pl.BlockSpec((N_TP, BLOCK, LANES), lambda r: (0, 0, 0))
     lines = KV_HEADS * STEPS * SLOTS
     return pl.pallas_call(
@@ -359,15 +376,14 @@
         in_specs=[
             SMEM,
             whole,
-            pl.BlockSpec((1, chunk, width), lambda r: (r, 0, 0)),
-            pl.BlockSpec((1, chunk, width), lambda r: (r, 0, 1)),
+            VMEM,
         ],
         out_specs=whole,
         out_shape=jax.ShapeDtypeStruct((N_TP, BLOCK, LANES), bf16),
         scratch_shapes=[pltpu.VMEM((lines, chunk), f32), pltpu.VMEM((lines, chunk), bf16)],
-        compiler_params=params(60, 1),
+        compiler_params=params(16, 1),
         name="attend",
-    )(cache_len, gathered, kv_cache, kv_cache)
+    )(cache_len, gathered, kv_cache)
 
 
 def merge_kernel(x_ref, out_ref):
@@ -393,62 +409,48 @@
     )(received)
 
 
-def output_kernel(x_ref, old_ref, new_ref, out_ref, wide, heads, early_sum, late_sum):
-    step = pl.program_id(0)
-
-    @pl.when(step == 0)
-    def _():
-        wide[...] = x_ref[...].astype(f32).reshape(wide.shape)
-        early_sum[...] = jnp.zeros_like(early_sum)
-        late_sum[...] = jnp.zeros_like(late_sum)
-        per_step = HEADS // heads.shape[0]
-        for h in range(HEADS):
-            kv = h // GROUP
-            at = kv % 2 * HEADS + kv // 2 * GROUP + h % GROUP
-            rows = [wide[pl.ds(at + el * HEADS // 2, HALF_TP, stride=2 * HEADS), :] for el in range(2)]
-            at = h % per_step * HEAD_DIM
-            heads[h // per_step, :, at : at + HEAD_DIM] = jnp.concatenate(rows, axis=0).astype(
-                bf16
-            )
-
+def output_kernel(*refs):
+    x_ref, old_ref, *pieces, out_ref, wide, heads, late_parts = refs
+    rep = lax.axis_index("rep")
+    xx, zh = rep >> 1, rep & 1
+    wide[...] = x_ref[...].astype(f32).reshape(wide.shape)
+    for h in range(HEADS):
+        kv = h // GROUP
+        at = kv % 2 * HEADS + kv // 2 * GROUP + h % GROUP
+        rows = [
+            wide[pl.ds(at + el * HEADS // 2, HALF_TP, stride=2 * HEADS), :] for el in range(2)
+        ]
+        heads[:, h * HEAD_DIM : (h + 1) * HEAD_DIM] = jnp.concatenate(rows, axis=0).astype(bf16)
     contract_last = (((1,), (1,)), ((), ()))
-    both = heads[step]
-    early_sum[...] += lax.dot_general(
-        both[:HALF_TP], old_ref[...], contract_last, preferred_element_type=f32
-    )
-    late_sum[...] += lax.dot_general(
-        both[HALF_TP:], new_ref[...], contract_last, preferred_element_type=f32
-    )
-
-    @pl.when(step == pl.num_programs(0) - 1)
-    def _():
-        for r in range(ROWS):
-            for el, total in enumerate((early_sum, late_sum)):
-                out_ref[r, el * 2 : el * 2 + 2, :] = total[r * 2 : r * 2 + 2, :].astype(bf16)
-
-
-def output(gathered, old_out, fresh_out):
-    blocks = 4
-    depth = D // blocks
+    early_heads, late_heads = heads[:HALF_TP], heads[HALF_TP:]
+    for n, piece in enumerate(pieces):
+        place = ((xx + n // 2) & (N_X - 1)) * 2 + (zh ^ (n & 1))
+        late_parts[place, :, :SHARD] = lax.dot_general(
+            late_heads, piece[...], contract_last, preferred_element_type=f32
+        )
+    early = lax.dot_general(
+        early_heads, old_ref[...], contract_last, preferred_element_type=f32
+    )
+    late = jnp.concatenate([late_parts[r, :, :SHARD] for r in range(N_REP)], axis=1)
+    for r in range(ROWS):
+        for el, total in enumerate((early, late)):
+            out_ref[r, el * 2 : el * 2 + 2, :] = total[r * 2 : r * 2 + 2, :].astype(bf16)
+
+
+def output(gathered, old_out, pieces):
     return pl.pallas_call(
         output_kernel,
-        grid=(blocks,),
-        in_specs=[
-            pl.BlockSpec((N_TP, HEADS, LANES), lambda i: (0, 0, 0)),
-            pl.BlockSpec((FEAT, depth), lambda i: (0, i)),
-            pl.BlockSpec((FEAT, depth), lambda i: (0, i)),
-        ],
-        out_specs=pl.BlockSpec((ROWS, STEPS, FEAT), lambda i: (0, 0, 0)),
+        in_specs=[VMEM] * (2 + N_REP),
+        out_specs=VMEM,
         out_shape=jax.ShapeDtypeStruct((ROWS, STEPS, FEAT), bf16),
         scratch_shapes=[
             pltpu.VMEM((N_TP * HEADS, LANES), f32),
-            pltpu.VMEM((blocks, N_TP, depth), bf16),
-            pltpu.VMEM((HALF_TP, FEAT), f32),
-            pltpu.VMEM((HALF_TP, FEAT), f32),
+            pltpu.VMEM((N_TP, D), bf16),
+            pltpu.VMEM((N_REP, HALF_TP, LANES), f32),
         ],
-        compiler_params=params(60, 1),
+        compiler_params=params(16),
         name="output",
-    )(gathered, old_out.T, fresh_out)
+    )(gathered, old_out.T, *pieces)
 
 
 def rotation(cache_len):
@@ -467,11 +469,17 @@
 def body(
     token_ids, cache_len, embed_table, norm_gain, old_qkv, old_out, new_qkv, new_out, kv_cache
 ):
-    fresh_out = lax.all_gather(new_out.T, "rep", axis=0, tiled=True)
-    other_qkv = lax.ppermute(new_qkv, "rep", [(r, r ^ 1) for r in range(N_REP)])
+    turn = [(r, r ^ 1) for r in range(N_REP)]
+    ahead = [(r, (r + 2) % N_REP) for r in range(N_REP)]
+    back = [(r, (r - 2) % N_REP) for r in range(N_REP)]
+    other_qkv = lax.ppermute(new_qkv, "rep", turn)
     cosine, sine = rotation(cache_len)
-    rows = lax.all_to_all(gather_rows(token_ids, embed_table), "rep", 0, 0)
-    keep, send = project(rows, norm_gain, new_qkv, other_qkv, old_qkv)
+    rows = gather_rows(token_ids, embed_table)
+    rows, old_qkv = lax.optimization_barrier((rows, old_qkv))
+    old_columns = take_old_columns(old_qkv)
+    rows = lax.all_to_all(rows, "rep", 0, 0)
+    rows, old_columns, cosine, sine = lax.optimization_barrier((rows, old_columns, cosine, sine))
+    keep, send = project(rows, norm_gain, new_qkv, other_qkv, old_columns)
     arrived = lax.ppermute(send, "tp", [(t, t ^ 1) for t in range(N_TP)])
     summed = add(keep, arrived).reshape(DESTS, SUMS, LANES)
     groups = [
@@ -480,10 +488,30 @@
         for core in range(2)
     ]
     partials = lax.all_to_all(summed, ("rep", "tp"), 0, 0, axis_index_groups=groups)
+    partials, own = lax.optimization_barrier((partials, new_out.T))
+    other = lax.ppermute(own, "rep", turn)
+    behind_own = lax.ppermute(own, "rep", ahead)
+    front_own = lax.ppermute(own, "rep", back)
     projected = lax.all_to_all(finish(partials, cosine, sine), "tp", 0, 0)
+    projected, other, behind_own = lax.optimization_barrier((projected, other, behind_own))
+    far_own = lax.ppermute(behind_own, "rep", ahead)
+    front_other = lax.ppermute(other, "rep", back)
     parts = lax.all_to_all(attend(cache_len, projected, kv_cache), "tp", 0, 0)
+    parts, front_other, other = lax.optimization_barrier((parts, front_other, other))
+    far_other = lax.ppermute(front_other, "rep", back)
+    behind_other = lax.ppermute(other, "rep", ahead)
     heads = lax.all_to_all(merge(parts), "tp", 0, 0)
-    return output(heads, old_out, fresh_out)
+    pieces = (
+        own,
+        other,
+        front_own,
+        front_other,
+        far_own,
+        far_other,
+        behind_own,
+        behind_other,
+    )
+    return output(heads, old_out, pieces)
 
 
 def solution(mesh):

time: 119 us -> 106 us (0.89)
  between operations: 14.1 us -> 0.79 us
  starting transfers between devices: 17.8 us -> 29.9 us
  Pallas kernels: 24.7 us -> 16.3 us
  waiting for transfers between devices: 24.6 us -> 17.7 us
  local copies, waits for them, and re-layouts: 3.78 us -> 9.69 us
  blocking collectives: 32.9 us -> 30.9 us
    ppermute x1 -> x8, starting transfers between devices: 4.51 us -> 12.3 us  [the longest x1 4.43 us: body(): other_qkv = lax.ppermute(new_qkv, 'rep', turn)]
    unnamed x10 -> x22, local copies, waits for them, and re-layouts: 2.63 us -> 9.1 us
    pallas_call x3 -> x4, Pallas kernels: 16.4 us -> 10.1 us  [the longest x1 4.79 us: attend(): pl.pallas_call(attend_kernel, grid=(ROWS,), in_specs=[SMEM, whole, VMEM],...]
    all_to_all x2 -> x3, waiting for transfers between devices: 21.9 us -> 16 us  [the longest x1 6.52 us: body(): heads = lax.all_to_all(merge(parts), 'tp', 0, 0)]
    all_to_all x2 -> x3, starting transfers between devices: 10.9 us -> 15.2 us  [the longest x1 6.07 us: body(): rows = lax.all_to_all(rows, 'rep', 0, 0)]
    all_to_all x2 -> x1, blocking collectives: 21.2 us -> 18.4 us  [body(): lax.all_to_all(summed, ('rep', 'tp'), 0, 0, axis_index_groups=groups)]
  transfers between devices with their start and end apart: 5 -> 12, of which waited for: 3 -> 4; matrix products, arithmetic and copies ran while one was open for 1% -> 1% of each run, Pallas kernels for 16% -> 11%
where the time goes in v3:
time: 106 us
  blocking collectives  30.9 us (29%)
  starting transfers between devices  29.9 us (28%)
  waiting for transfers between devices  17.7 us (17%)
  Pallas kernels  16.3 us (15%)
  local copies, waits for them, and re-layouts  9.69 us (9%)
    all_to_all x1, blocking collectives, body(): lax.all_to_all(summed, ('rep', 'tp'), 0, 0, axis_index_groups=groups)  18.4 us
    all_to_all x1, blocking collectives, body(): projected = lax.all_to_all(finish(partials, cosine, sine), 'tp', 0, 0)  12.5 us
    unnamed x22, local copies, waits for them, and re-layouts  9.1 us
    all_to_all x1, waiting for transfers between devices, body(): heads = lax.all_to_all(merge(parts), 'tp', 0, 0)  6.52 us
    all_to_all x1, starting transfers between devices, body(): rows = lax.all_to_all(rows, 'rep', 0, 0)  6.07 us
    all_to_all x1, waiting for transfers between devices, body(): parts = lax.all_to_all(attend(cache_len, projected, kv_cache), 'tp', 0, 0)  5.99 us
    pallas_call x1, Pallas kernels, gather_rows(): pl.pallas_call(gather_kernel, grid=(1,), in_specs=[SMEM, pl.BlockSpec((FE...  5.7 us
    all_to_all x1, starting transfers between devices, body(): parts = lax.all_to_all(attend(cache_len, projected, kv_cache), 'tp', 0, 0)  4.87 us
  transfers between devices with their start and end apart: 12, of which 4 were waited for; matrix products, arithmetic and copies ran while one was open for 1% of the time, Pallas kernels for 11%

profile of v3, /device:TPU:1, one launch (start us, length us, event | category | flops | bytes accessed | tf_op | source)
XLA Modules:
  0.0 105.6 jit_solution(4018653992995466972)
XLA Ops:
  0.0 4.4 %collective-permute-start = (bf16[40,7168]{1,0:T(8,128)(2,1)}, bf16[40,7168]{1,0:T(8,128)(2,1)S(1)}, u32[]{:S(2)}, u32[]{:S(2)}) collective-permute-start(bf16[40,7168]{1,0:T(8,128)(2,1)} %new_ref.1), channel_id=1, source_target_pairs={{0,16},{16,0},{32,48},{48,32},{64,80},{80,64},{96,112},{112,96},{1... | collective-permute-start | bytes 1720328 | tf_op jit(solution)/shard_map/ppermute | solution.py:475
  4.4 5.7 %gather_rows.1 = bf16[8,128,128]{2,1,0:T(8,128)(2,1)} custom-call(s32[4,32]{1,0:T(4,128)} %bitcast.14, bf16[320,9504]{1,0:T(8,128)(2,1)} %bitcast.12, bf16[320,9504]{1,0:T(8,128)(2,1)} %bitcast.13), custom_call_target="tpu_custom_call" | custom-call | tf_op jit(solution)/shard_map/gather_rows/pallas_call | solution.py:127
  10.1 0.0 copy-start.9
  10.2 6.1 %all-to-all-start = ((bf16[8,128,128]{2,1,0:T(8,128)(2,1)}), bf16[8,128,128]{2,1,0:T(8,128)(2,1)S(1)}, u32[]{:S(2)}, u32[]{:S(2)}) async-start(bf16[8,128,128]{2,1,0:T(8,128)(2,1)} %gather_rows.1), calls=%async_computation | async-start | bytes 524288 | tf_op jit(solution)/shard_map/all_to_all | solution.py:480
  16.2 0.0 copy-done.10
  16.2 0.0 copy-start.1
  16.3 2.3 %copy-done.1 = bf16[320,7168]{1,0:T(8,128)(2,1)S(1)} copy-done((bf16[320,7168]{1,0:T(8,128)(2,1)S(1)}, bf16[320,7168]{1,0:T(8,128)(2,1)}, u32[]{:S(2)}) %copy-start.1) | copy-done | bytes 4587544
  18.5 0.1 take_old_columns.1.old
  18.7 0.6 dynamic_slice.3
  20.0 0.1 fusion
  20.1 0.1 pad_maximum_fusion
  20.2 3.5 %all-to-all-done.x_ref = bf16[8,128,128]{2,1,0:T(8,128)(2,1)S(1)} async-done(((bf16[8,128,128]{2,1,0:T(8,128)(2,1)}), bf16[8,128,128]{2,1,0:T(8,128)(2,1)S(1)}, u32[]{:S(2)}, u32[]{:S(2)}) %all-to-all-start) | async-done | bytes 262176 | tf_op jit(solution)/shard_map/all_to_all | solution.py:480
  23.7 0.0 collective-permute-done.other_ref
  23.7 0.0 copy-done.4
  23.7 0.9 project.1
  24.5 2.3 %collective-permute-start.1 = (f32[1280,128]{1,0:T(8,128)S(1)}, f32[1280,128]{1,0:T(8,128)S(1)}, u32[]{:S(2)}, u32[]{:S(2)}) collective-permute-start(f32[1280,128]{1,0:T(8,128)S(1)} %get-tuple-element.26), channel_id=1, source_target_pairs={{0,1},{1,0},{2,3},{3,2},{4,5},{5,4},{6,7},{7,6},{8,9},{9,8},{10,11... | collective-permute-start | bytes 1966088 | tf_op jit(solution)/shard_map/ppermute | solution.py:483
  26.8 1.7 %collective-permute-done.1.b_ref = f32[1280,128]{1,0:T(8,128)S(1)} collective-permute-done((f32[1280,128]{1,0:T(8,128)S(1)}, f32[1280,128]{1,0:T(8,128)S(1)}, u32[]{:S(2)}, u32[]{:S(2)}) %collective-permute-start.1) | collective-permute-done | bytes 655392 | tf_op jit(solution)/shard_map/ppermute | solution.py:483
  28.6 0.1 add.23
  28.6 18.4 %all_to_all.25.x_ref = f32[32,40,128]{2,1,0:T(8,128)S(1)} all-to-all(f32[32,40,128]{2,1,0:T(8,128)S(1)} %bitcast.7), channel_id=1, replica_groups={{0,2,4,6,8,10,12,14,32,34,36,38,40,42,44,46,64,66,68,70,72,74,76,78,96,..., dimensions={0} | all-to-all | bytes 1310720 | tf_op jit(solution)/shard_map/all_to_all | solution.py:490
  47.1 0.0 collective-permute-start.3
  47.1 1.2 %collective-permute-start.2 = (bf16[40,5120]{1,0:T(8,128)(2,1)S(1)}, bf16[40,5120]{1,0:T(8,128)(2,1)}, u32[]{:S(2)}, u32[]{:S(2)}) collective-permute-start(bf16[40,5120]{1,0:T(8,128)(2,1)S(1)} %bitcast.10), channel_id=1, source_target_pairs={{0,16},{16,0},{32,48},{48,32},{64,80},{80,64},{96,112},{112,96},{1... | collective-permute-start | bytes 1228808 | tf_op jit(solution)/shard_map/ppermute | solution.py:492
  48.3 0.1 finish.1
  48.4 12.5 %all_to_all.26.q_ref = bf16[16,64,128]{2,1,0:T(8,128)(2,1)S(1)} all-to-all(bf16[16,64,128]{2,1,0:T(8,128)(2,1)S(1)} %finish.1), channel_id=1, replica_groups=mesh['rep'=8,'tp'=16] {'tp'}, dimensions={0} | all-to-all | bytes 524288 | tf_op jit(solution)/shard_map/all_to_all | solution.py:495
  60.9 0.0 collective-permute-done.3.refs_8_
  61.0 0.0 collective-permute-done.2.refs_3_
  61.0 0.8 copy-done.7
  61.7 2.5 %collective-permute-start.4 = (bf16[40,5120]{1,0:T(8,128)(2,1)}, bf16[40,5120]{1,0:T(8,128)(2,1)}, u32[]{:S(2)}, u32[]{:S(2)}) collective-permute-start(bf16[40,5120]{1,0:T(8,128)(2,1)} %collective-permute-done.2.refs_3_), channel_id=1, source_target_pairs={{0,96},{16,112},{32,0},{48,16},{64,32},{80,48},{96,64},{112,80},{1... | collective-permute-start | bytes 1228808 | tf_op jit(solution)/shard_map/ppermute | solution.py:498
  64.2 3.4 %copy-done = bf16[4,512,2048]{2,1,0:T(8,128)(2,1)S(1)} copy-done((bf16[4,512,2048]{2,1,0:T(8,128)(2,1)S(1)}, bf16[4,512,2048]{2,1,0:T(8,128)(2,1)}, u32[]{:S(2)}) %copy-start) | copy-done | bytes 8388632
  67.6 4.8 %attend.1 = bf16[16,64,128]{2,1,0:T(8,128)(2,1)} custom-call(s32[4]{0:T(128)S(1)} %copy-done.9, bf16[16,64,128]{2,1,0:T(8,128)(2,1)S(1)} %all_to_all.26.q_ref, bf16[4,512,2048]{2,1,0:T(8,128)(2,1)S(1)} %copy-done), custom_call_target="tpu_custom_call" | custom-call | tf_op jit(solution)/shard_map/attend/pallas_call | solution.py:373
  72.4 4.9 %all-to-all-start.3 = ((bf16[16,64,128]{2,1,0:T(8,128)(2,1)}), bf16[16,64,128]{2,1,0:T(8,128)(2,1)S(1)}, u32[]{:S(2)}, u32[]{:S(2)}) async-start(bf16[16,64,128]{2,1,0:T(8,128)(2,1)} %attend.1), calls=%async_computation.3 | async-start | bytes 524288 | tf_op jit(solution)/shard_map/all_to_all | solution.py:499
  77.3 0.1 collective-permute-start.5
  77.4 1.4 %collective-permute-start.6 = (bf16[40,5120]{1,0:T(8,128)(2,1)}, bf16[40,5120]{1,0:T(8,128)(2,1)}, u32[]{:S(2)}, u32[]{:S(2)}) collective-permute-start(bf16[40,5120]{1,0:T(8,128)(2,1)} %copy-done.7), channel_id=1, source_target_pairs={{0,32},{16,48},{32,64},{48,80},{64,96},{80,112},{96,0},{112,16},{1... | collective-permute-start | bytes 1228808 | tf_op jit(solution)/shard_map/ppermute | solution.py:497
  78.8 6.0 %all-to-all-done.3.x_ref = bf16[16,64,128]{2,1,0:T(8,128)(2,1)S(1)} async-done(((bf16[16,64,128]{2,1,0:T(8,128)(2,1)}), bf16[16,64,128]{2,1,0:T(8,128)(2,1)S(1)}, u32[]{:S(2)}, u32[]{:S(2)}) %all-to-all-start.3) | async-done | bytes 262176 | tf_op jit(solution)/shard_map/all_to_all | solution.py:499
  84.7 0.0 collective-permute-done.4.refs_5_
  84.7 0.0 collective-permute-start.8
  84.7 2.7 %collective-permute-start.7 = (bf16[40,5120]{1,0:T(8,128)(2,1)}, bf16[40,5120]{1,0:T(8,128)(2,1)}, u32[]{:S(2)}, u32[]{:S(2)}) collective-permute-start(bf16[40,5120]{1,0:T(8,128)(2,1)} %collective-permute-done.4.refs_5_), channel_id=1, source_target_pairs={{0,96},{16,112},{32,0},{48,16},{64,32},{80,48},{96,64},{112,80},{1... | collective-permute-start | bytes 1228808 | tf_op jit(solution)/shard_map/ppermute | solution.py:501
  87.4 0.4 merge.1
  87.8 0.6 copy-done.3
  88.4 4.3 %all-to-all-start.4 = ((bf16[16,40,128]{2,1,0:T(8,128)(2,1)}), bf16[16,40,128]{2,1,0:T(8,128)(2,1)S(1)}, u32[]{:S(2)}, u32[]{:S(2)}) async-start(bf16[16,40,128]{2,1,0:T(8,128)(2,1)} %copy-done.3), calls=%async_computation.4 | async-start | bytes 327680 | tf_op jit(solution)/shard_map/all_to_all | solution.py:503
  92.7 0.0 collective-permute-done.5.refs_4_
  92.7 0.0 collective-permute-done.6.refs_6_
  92.7 6.5 %all-to-all-done.4.refs_0_ = bf16[16,40,128]{2,1,0:T(8,128)(2,1)S(1)} async-done(((bf16[16,40,128]{2,1,0:T(8,128)(2,1)}), bf16[16,40,128]{2,1,0:T(8,128)(2,1)S(1)}, u32[]{:S(2)}, u32[]{:S(2)}) %all-to-all-start.4) | async-done | bytes 163872 | tf_op jit(solution)/shard_map/all_to_all | solution.py:503
  99.3 0.0 collective-permute-done.8.refs_9_
  99.3 0.0 collective-permute-done.7.refs_7_
  99.3 0.0 copy-start.6
  99.3 1.0 copy-done.6
  100.3 1.0 copy-done.8
  101.3 4.3 %output.1 = bf16[4,4,320]{2,1,0:T(4,128)(2,1)} custom-call(bf16[16,40,128]{2,1,0:T(8,128)(2,1)S(1)} %all-to-all-done.4.refs_0_, bf16[320,5120]{1,0:T(8,128)(2,1)S(1)} %bitcast.6, bf16[40,5120]{1,0:T(8,128)(2,1)S(1)} %bitcast.11, bf16[40,5120]{1,0:T(8,128)(2,1)} %collective-permute-done.2.refs_3_, bf16[40,5120]{1,0:T(8,128)(2,1)} %collective-permute-done.5.refs_4_, ...), custom_call_target="tpu_custom_call" | custom-call | tf_op jit(solution)/shard_map/output/pallas_call | solution.py:441
  (14 shorter events, 0.0 us)
Async XLA Ops:
  0.0 23.7 %collective-permute-start = (bf16[40,7168]{1,0:T(8,128)(2,1)}, bf16[40,7168]{1,0:T(8,128)(2,1)S(1)}, u32[]{:S(2)}, u32[]{:S(2)}) collective-permute-start(bf16[40,7168]{1,0:T(8,128)(2,1)} %new_ref.1), channel_id=1, source_target_pairs={{0,16},{16,0},{32,48},{48,32},{64,80},{80,64},{96,112},{112,96},{1... | collective-permute-start | bytes 1720328 | tf_op jit(solution)/shard_map/ppermute | solution.py:475
  4.4 11.8 %copy-start.10 = (bf16[320]{0:T(512)(128)(2,1)S(1)}, bf16[320]{0:T(512)(128)(2,1)}, u32[]{:S(2)}) copy-start(bf16[320]{0:T(512)(128)(2,1)} %param.12) | copy-start | bytes 1924
  4.4 19.2 %copy-start.4 = (bf16[40,7168]{1,0:T(8,128)(2,1)S(1)}, bf16[40,7168]{1,0:T(8,128)(2,1)}, u32[]{:S(2)}) copy-start(bf16[40,7168]{1,0:T(8,128)(2,1)} %new_ref.1) | copy-start | bytes 1720324
  10.1 8.6 %copy-start.9 = (s32[4]{0:T(128)S(1)}, s32[4]{0:T(128)}, u32[]{:S(2)}) copy-start(s32[4]{0:T(128)} %len_ref.1) | copy-start | bytes 52
  10.2 13.5 %all-to-all-start = ((bf16[8,128,128]{2,1,0:T(8,128)(2,1)}), bf16[8,128,128]{2,1,0:T(8,128)(2,1)S(1)}, u32[]{:S(2)}, u32[]{:S(2)}) async-start(bf16[8,128,128]{2,1,0:T(8,128)(2,1)} %gather_rows.1), calls=%async_computation | async-start | bytes 524288 | tf_op jit(solution)/shard_map/all_to_all | solution.py:480
  16.2 2.3 %copy-start.1 = (bf16[320,7168]{1,0:T(8,128)(2,1)S(1)}, bf16[320,7168]{1,0:T(8,128)(2,1)}, u32[]{:S(2)}) copy-start(bf16[320,7168]{1,0:T(8,128)(2,1)} %old_ref) | copy-start | bytes 13762564
  18.5 28.5 %copy-start.5 = (bf16[5120,40]{0,1:T(8,128)(2,1)S(1)}, bf16[5120,40]{0,1:T(8,128)(2,1)}, u32[]{:S(2)}) copy-start(bf16[5120,40]{0,1:T(8,128)(2,1)} %param.16) | copy-start | bytes 1228804
  24.5 4.0 %collective-permute-start.1 = (f32[1280,128]{1,0:T(8,128)S(1)}, f32[1280,128]{1,0:T(8,128)S(1)}, u32[]{:S(2)}, u32[]{:S(2)}) collective-permute-start(f32[1280,128]{1,0:T(8,128)S(1)} %get-tuple-element.26), channel_id=1, source_target_pairs={{0,1},{1,0},{2,3},{3,2},{4,5},{5,4},{6,7},{7,6},{8,9},{9,8},{10,11... | collective-permute-start | bytes 1966088 | tf_op jit(solution)/shard_map/ppermute | solution.py:483
  47.1 13.9 %collective-permute-start.3 = (bf16[40,5120]{1,0:T(8,128)(2,1)S(1)}, bf16[40,5120]{1,0:T(8,128)(2,1)S(1)}, u32[]{:S(2)}, u32[]{:S(2)}) collective-permute-start(bf16[40,5120]{1,0:T(8,128)(2,1)S(1)} %bitcast.9), channel_id=1, source_target_pairs={{0,32},{16,48},{32,64},{48,80},{64,96},{80,112},{96,0},{112,16},{1... | collective-permute-start | bytes 1228808 | tf_op jit(solution)/shard_map/ppermute | solution.py:493
  47.1 13.9 %collective-permute-start.2 = (bf16[40,5120]{1,0:T(8,128)(2,1)S(1)}, bf16[40,5120]{1,0:T(8,128)(2,1)}, u32[]{:S(2)}, u32[]{:S(2)}) collective-permute-start(bf16[40,5120]{1,0:T(8,128)(2,1)S(1)} %bitcast.10), channel_id=1, source_target_pairs={{0,16},{16,0},{32,48},{48,32},{64,80},{80,64},{96,112},{112,96},{1... | collective-permute-start | bytes 1228808 | tf_op jit(solution)/shard_map/ppermute | solution.py:492
  61.0 0.8 copy-start.7
  61.7 23.0 %collective-permute-start.4 = (bf16[40,5120]{1,0:T(8,128)(2,1)}, bf16[40,5120]{1,0:T(8,128)(2,1)}, u32[]{:S(2)}, u32[]{:S(2)}) collective-permute-start(bf16[40,5120]{1,0:T(8,128)(2,1)} %collective-permute-done.2.refs_3_), channel_id=1, source_target_pairs={{0,96},{16,112},{32,0},{48,16},{64,32},{80,48},{96,64},{112,80},{1... | collective-permute-start | bytes 1228808 | tf_op jit(solution)/shard_map/ppermute | solution.py:498
  64.2 3.4 %copy-start = (bf16[4,512,2048]{2,1,0:T(8,128)(2,1)S(1)}, bf16[4,512,2048]{2,1,0:T(8,128)(2,1)}, u32[]{:S(2)}) copy-start(bf16[4,512,2048]{2,1,0:T(8,128)(2,1)} %kv_ref.1) | copy-start | bytes 25165828
  67.6 31.7 %copy-start.2 = (bf16[5120,320]{0,1:T(8,128)(2,1)S(1)}, bf16[5120,320]{0,1:T(8,128)(2,1)}, u32[]{:S(2)}) copy-start(bf16[5120,320]{0,1:T(8,128)(2,1)} %param.14) | copy-start | bytes 9830404
  72.4 12.3 %all-to-all-start.3 = ((bf16[16,64,128]{2,1,0:T(8,128)(2,1)}), bf16[16,64,128]{2,1,0:T(8,128)(2,1)S(1)}, u32[]{:S(2)}, u32[]{:S(2)}) async-start(bf16[16,64,128]{2,1,0:T(8,128)(2,1)} %attend.1), calls=%async_computation.3 | async-start | bytes 524288 | tf_op jit(solution)/shard_map/all_to_all | solution.py:499
  77.3 15.5 %collective-permute-start.5 = (bf16[40,5120]{1,0:T(8,128)(2,1)}, bf16[40,5120]{1,0:T(8,128)(2,1)}, u32[]{:S(2)}, u32[]{:S(2)}) collective-permute-start(bf16[40,5120]{1,0:T(8,128)(2,1)} %bitcast.8), channel_id=1, source_target_pairs={{0,96},{16,112},{32,0},{48,16},{64,32},{80,48},{96,64},{112,80},{1... | collective-permute-start | bytes 1228808 | tf_op jit(solution)/shard_map/ppermute | solution.py:494
  77.4 15.3 %collective-permute-start.6 = (bf16[40,5120]{1,0:T(8,128)(2,1)}, bf16[40,5120]{1,0:T(8,128)(2,1)}, u32[]{:S(2)}, u32[]{:S(2)}) collective-permute-start(bf16[40,5120]{1,0:T(8,128)(2,1)} %copy-done.7), channel_id=1, source_target_pairs={{0,32},{16,48},{32,64},{48,80},{64,96},{80,112},{96,0},{112,16},{1... | collective-permute-start | bytes 1228808 | tf_op jit(solution)/shard_map/ppermute | solution.py:497
  84.7 14.5 %collective-permute-start.8 = (bf16[40,5120]{1,0:T(8,128)(2,1)}, bf16[40,5120]{1,0:T(8,128)(2,1)}, u32[]{:S(2)}, u32[]{:S(2)}) collective-permute-start(bf16[40,5120]{1,0:T(8,128)(2,1)} %collective-permute-done.2.refs_3_), channel_id=1, source_target_pairs={{0,32},{16,48},{32,64},{48,80},{64,96},{80,112},{96,0},{112,16},{1... | collective-permute-start | bytes 1228808 | tf_op jit(solution)/shard_map/ppermute | solution.py:502
  84.7 14.5 %collective-permute-start.7 = (bf16[40,5120]{1,0:T(8,128)(2,1)}, bf16[40,5120]{1,0:T(8,128)(2,1)}, u32[]{:S(2)}, u32[]{:S(2)}) collective-permute-start(bf16[40,5120]{1,0:T(8,128)(2,1)} %collective-permute-done.4.refs_5_), channel_id=1, source_target_pairs={{0,96},{16,112},{32,0},{48,16},{64,32},{80,48},{96,64},{112,80},{1... | collective-permute-start | bytes 1228808 | tf_op jit(solution)/shard_map/ppermute | solution.py:501
  87.8 0.7 copy-start.3
  88.4 10.8 %all-to-all-start.4 = ((bf16[16,40,128]{2,1,0:T(8,128)(2,1)}), bf16[16,40,128]{2,1,0:T(8,128)(2,1)S(1)}, u32[]{:S(2)}, u32[]{:S(2)}) async-start(bf16[16,40,128]{2,1,0:T(8,128)(2,1)} %copy-done.3), calls=%async_computation.4 | async-start | bytes 327680 | tf_op jit(solution)/shard_map/all_to_all | solution.py:503
  99.3 1.0 copy-start.6
  100.3 1.0 copy-start.8

commit v4 on v3

--- a/solution.py
+++ b/solution.py
@@ -50,7 +50,7 @@
 
 def params(mib, grid=False):
     kwargs = dict(dimension_semantics=("arbitrary",) * grid) if grid else {}
-    return pltpu.CompilerParams(vmem_limit_bytes=mib * MIB, **kwargs)
+    return pltpu.CompilerParams(vmem_limit_bytes=int(mib * MIB), **kwargs)
 
 def gather_kernel(ids_ref, tail_ref, table_ref, out_ref, buf, cols, found, sems):
     window = table_ref.shape[1]
@@ -258,7 +258,8 @@
     )(a, b)
 
 
-def finish_kernel(x_ref, cos_ref, sin_ref, out_ref):
+def finish_kernel(x_ref, cos_ref, sin_ref, *refs):
+    out_ref = refs[-1]
     parts = x_ref[...].reshape(N_X, HALF_TP, SUMS, LANES)
     late = jnp.sum(jnp.sum(parts[:, :, :HALF_ROWS], axis=1), axis=0)
     early = jnp.sum(parts[:, :, HALF_ROWS:], axis=1)
@@ -278,16 +279,15 @@
     )
 
 
-def finish(received, cosine, sine):
+def finish(received, cosine, sine, *far):
     return pl.pallas_call(
         finish_kernel,
-        in_specs=[VMEM, VMEM, VMEM],
+        in_specs=[VMEM, VMEM, VMEM] + [ANY] * len(far),
         out_specs=VMEM,
         out_shape=jax.ShapeDtypeStruct((N_TP, BLOCK, LANES), bf16),
-        compiler_params=params(16),
-        cost_estimate=pl.CostEstimate(flops=0, bytes_accessed=32 * MIB, transcendentals=0),
+        compiler_params=params(53.5),
         name="finish",
-    )(received, cosine, sine)
+    )(received, cosine, sine, *far)
 
 
 def attend_kernel(len_ref, q_ref, kv_ref, out_ref, scores_ref, weights_ref):
@@ -492,7 +492,7 @@
     other = lax.ppermute(own, "rep", turn)
     behind_own = lax.ppermute(own, "rep", ahead)
     front_own = lax.ppermute(own, "rep", back)
-    projected = lax.all_to_all(finish(partials, cosine, sine), "tp", 0, 0)
+    projected = lax.all_to_all(finish(partials, cosine, sine, embed_table.T, embed_table.T, old_qkv), "tp", 0, 0)
     projected, other, behind_own = lax.optimization_barrier((projected, other, behind_own))
     far_own = lax.ppermute(behind_own, "rep", ahead)
     front_other = lax.ppermute(other, "rep", back)

time: 106 us -> 102 us (0.962); the launches traced: 106 us -> 100 us
  local copies, waits for them, and re-layouts: 9.69 us -> 4.84 us
  Pallas kernels: 16.3 us -> 19.6 us
  starting transfers between devices: 29.9 us -> 26.8 us
    unnamed x22 -> x16, local copies, waits for them, and re-layouts: 9.1 us -> 4.25 us
    all_to_all x1, starting transfers between devices: 6.07 us -> 3.47 us  [body(): rows = lax.all_to_all(rows, 'rep', 0, 0)]
    pallas_call x1, Pallas kernels: 0.12 us -> 1.95 us  [finish(): pl.pallas_call(finish_kernel, in_specs=[VMEM, VMEM, VMEM] + [ANY] * len(f...]
    pallas_call x1, Pallas kernels: 5.7 us -> 7.14 us  [gather_rows(): pl.pallas_call(gather_kernel, grid=(1,), in_specs=[SMEM, pl.BlockSpec((FE...]
  transfers between devices with their start and end apart: 12 -> 12, of which waited for: 4 -> 4; matrix products, arithmetic and copies ran while one was open for 1% -> 1% of each run, Pallas kernels for 11% -> 15%
where the time goes in v4:
time: 102 us; the launch traced here: 100 us
  blocking collectives  30.3 us (30%)
  starting transfers between devices  26.8 us (26%)
  Pallas kernels  19.6 us (19%)
  waiting for transfers between devices  17.6 us (17%)
  local copies, waits for them, and re-layouts  4.84 us (5%)
    all_to_all x1, blocking collectives, body(): lax.all_to_all(summed, ('rep', 'tp'), 0, 0, axis_index_groups=groups)  18.5 us
    all_to_all x1, blocking collectives, body(): lax.all_to_all(finish(partials, cosine, sine, embed_table.T, embed_table....  11.9 us
    pallas_call x1, Pallas kernels, gather_rows(): pl.pallas_call(gather_kernel, grid=(1,), in_specs=[SMEM, pl.BlockSpec((FE...  7.14 us
    all_to_all x1, waiting for transfers between devices, body(): heads = lax.all_to_all(merge(parts), 'tp', 0, 0)  6.52 us
    all_to_all x1, waiting for transfers between devices, body(): parts = lax.all_to_all(attend(cache_len, projected, kv_cache), 'tp', 0, 0)  5.99 us
    pallas_call x1, Pallas kernels, attend(): pl.pallas_call(attend_kernel, grid=(ROWS,), in_specs=[SMEM, whole, VMEM],...  4.75 us
    ppermute x1, starting transfers between devices, body(): other_qkv = lax.ppermute(new_qkv, 'rep', turn)  4.43 us
    all_to_all x1, starting transfers between devices, body(): heads = lax.all_to_all(merge(parts), 'tp', 0, 0)  4.29 us
  transfers between devices with their start and end apart: 12, of which 4 were waited for; matrix products, arithmetic and copies ran while one was open for 1% of the time, Pallas kernels for 15%

profile of v4, /device:TPU:1, one launch (start us, length us, event | category | flops | bytes accessed | tf_op | source)
XLA Modules:
  0.0 100.1 jit_solution(18232643351770255128)
XLA Ops:
  0.0 4.4 %collective-permute-start = (bf16[40,7168]{1,0:T(8,128)(2,1)}, bf16[40,7168]{1,0:T(8,128)(2,1)S(1)}, u32[]{:S(2)}, u32[]{:S(2)}) collective-permute-start(bf16[40,7168]{1,0:T(8,128)(2,1)} %new_ref.1), channel_id=1, source_target_pairs={{0,16},{16,0},{32,48},{48,32},{64,80},{80,64},{96,112},{112,96},{1... | collective-permute-start | bytes 1720328 | tf_op jit(solution)/shard_map/ppermute | solution.py:475
  4.4 0.0 copy-start.5
  4.4 7.1 %gather_rows.1 = bf16[8,128,128]{2,1,0:T(8,128)(2,1)} custom-call(s32[4,32]{1,0:T(4,128)} %bitcast.18, bf16[320,9504]{1,0:T(8,128)(2,1)} %bitcast.14, bf16[320,9504]{1,0:T(8,128)(2,1)} %bitcast.15), custom_call_target="tpu_custom_call" | custom-call | tf_op jit(solution)/shard_map/gather_rows/pallas_call | solution.py:127
  11.6 0.0 copy-start.4
  11.6 3.5 %all-to-all-start = ((bf16[8,128,128]{2,1,0:T(8,128)(2,1)}), bf16[8,128,128]{2,1,0:T(8,128)(2,1)S(1)}, u32[]{:S(2)}, u32[]{:S(2)}) async-start(bf16[8,128,128]{2,1,0:T(8,128)(2,1)} %gather_rows.1), calls=%async_computation | async-start | bytes 524288 | tf_op jit(solution)/shard_map/all_to_all | solution.py:480
  15.1 0.0 copy-done.5
  15.1 0.0 copy-start
  15.1 2.3 %copy-done = bf16[320,7168]{1,0:T(8,128)(2,1)S(1)} copy-done((bf16[320,7168]{1,0:T(8,128)(2,1)S(1)}, bf16[320,7168]{1,0:T(8,128)(2,1)}, u32[]{:S(2)}) %copy-start) | copy-done | bytes 4587544
  17.4 0.1 take_old_columns.1.old
  17.5 0.0 copy-done.4
  17.5 0.6 dynamic_slice.3
  18.8 0.1 fusion
  18.9 0.1 pad_maximum_fusion
  19.0 3.3 %all-to-all-done.x_ref = bf16[8,128,128]{2,1,0:T(8,128)(2,1)S(1)} async-done(((bf16[8,128,128]{2,1,0:T(8,128)(2,1)}), bf16[8,128,128]{2,1,0:T(8,128)(2,1)S(1)}, u32[]{:S(2)}, u32[]{:S(2)}) %all-to-all-start) | async-done | bytes 262176 | tf_op jit(solution)/shard_map/all_to_all | solution.py:480
  22.4 0.0 collective-permute-done.other_ref
  22.4 0.0 copy-done.2
  22.4 0.8 project.1
  23.2 2.5 %collective-permute-start.1 = (f32[1280,128]{1,0:T(8,128)S(1)}, f32[1280,128]{1,0:T(8,128)S(1)}, u32[]{:S(2)}, u32[]{:S(2)}) collective-permute-start(f32[1280,128]{1,0:T(8,128)S(1)} %get-tuple-element.26), channel_id=1, source_target_pairs={{0,1},{1,0},{2,3},{3,2},{4,5},{5,4},{6,7},{7,6},{8,9},{9,8},{10,11... | collective-permute-start | bytes 1966088 | tf_op jit(solution)/shard_map/ppermute | solution.py:483
  25.7 1.7 %collective-permute-done.1.b_ref = f32[1280,128]{1,0:T(8,128)S(1)} collective-permute-done((f32[1280,128]{1,0:T(8,128)S(1)}, f32[1280,128]{1,0:T(8,128)S(1)}, u32[]{:S(2)}, u32[]{:S(2)}) %collective-permute-start.1) | collective-permute-done | bytes 655392 | tf_op jit(solution)/shard_map/ppermute | solution.py:483
  27.4 0.1 add.23
  27.5 18.5 %all_to_all.25.x_ref = f32[32,40,128]{2,1,0:T(8,128)} all-to-all(f32[32,40,128]{2,1,0:T(8,128)S(1)} %bitcast.9), channel_id=1, replica_groups={{0,2,4,6,8,10,12,14,32,34,36,38,40,42,44,46,64,66,68,70,72,74,76,78,96,..., dimensions={0} | all-to-all | bytes 1310720 | tf_op jit(solution)/shard_map/all_to_all | solution.py:490
  46.0 0.0 copy-done.3
  46.0 0.0 collective-permute-start.3
  46.0 1.6 %collective-permute-start.2 = (bf16[40,5120]{1,0:T(8,128)(2,1)S(1)}, bf16[40,5120]{1,0:T(8,128)(2,1)S(1)}, u32[]{:S(2)}, u32[]{:S(2)}) collective-permute-start(bf16[40,5120]{1,0:T(8,128)(2,1)S(1)} %bitcast.11), channel_id=1, source_target_pairs={{0,16},{16,0},{32,48},{48,32},{64,80},{80,64},{96,112},{112,96},{1... | collective-permute-start | bytes 1228808 | tf_op jit(solution)/shard_map/ppermute | solution.py:492
  47.6 2.0 %finish.1 = bf16[16,64,128]{2,1,0:T(8,128)(2,1)S(1)} custom-call(f32[32,40,128]{2,1,0:T(8,128)} %all_to_all.25.x_ref, f32[2,128]{1,0:T(2,128)S(1)} %get-tuple-element.28.cos_ref, f32[2,128]{1,0:T(2,128)S(1)} %get-tuple-element.29.sin_ref, bf16[320,9504]{1,0:T(8,128)(2,1)} %bitcast.16, bf16[320,9504]{1,0:T(8,128)(2,1)} %bitcast.17, bf16[320,7168]{1,0:T(8,128)(2,1)} %refs_2_), custom_call_target="tpu_custom_call" | custom-call | tf_op jit(solution)/shard_map/finish/pallas_call | solution.py:283
  49.6 11.9 %all_to_all.26.q_ref = bf16[16,64,128]{2,1,0:T(8,128)(2,1)S(1)} all-to-all(bf16[16,64,128]{2,1,0:T(8,128)(2,1)S(1)} %finish.1), channel_id=1, replica_groups=mesh['rep'=8,'tp'=16] {'tp'}, dimensions={0} | all-to-all | bytes 524288 | tf_op jit(solution)/shard_map/all_to_all | solution.py:495
  61.4 0.0 collective-permute-done.3.refs_8_
  61.4 0.0 collective-permute-done.2.refs_3_
  61.4 2.4 %collective-permute-start.4 = (bf16[40,5120]{1,0:T(8,128)(2,1)S(1)}, bf16[40,5120]{1,0:T(8,128)(2,1)S(1)}, u32[]{:S(2)}, u32[]{:S(2)}) collective-permute-start(bf16[40,5120]{1,0:T(8,128)(2,1)S(1)} %collective-permute-done.2.refs_3_), channel_id=1, source_target_pairs={{0,96},{16,112},{32,0},{48,16},{64,32},{80,48},{96,64},{112,80},{1... | collective-permute-start | bytes 1228808 | tf_op jit(solution)/shard_map/ppermute | solution.py:498
  63.8 0.0 slice-done
  63.8 0.0 slice-done.1
  63.8 4.7 %attend.1 = bf16[16,64,128]{2,1,0:T(8,128)(2,1)} custom-call(s32[4]{0:T(128)S(1)} %copy-done.4, bf16[16,64,128]{2,1,0:T(8,128)(2,1)S(1)} %all_to_all.26.q_ref, bf16[4,512,2048]{2,1,0:T(8,128)(2,1)S(1)} %bitcast.7), custom_call_target="tpu_custom_call" | custom-call | tf_op jit(solution)/shard_map/attend/pallas_call | solution.py:373
  68.5 4.0 %all-to-all-start.3 = ((bf16[16,64,128]{2,1,0:T(8,128)(2,1)}), bf16[16,64,128]{2,1,0:T(8,128)(2,1)S(1)}, u32[]{:S(2)}, u32[]{:S(2)}) async-start(bf16[16,64,128]{2,1,0:T(8,128)(2,1)} %attend.1), calls=%async_computation.3 | async-start | bytes 524288 | tf_op jit(solution)/shard_map/all_to_all | solution.py:499
  72.6 0.0 collective-permute-start.5
  72.6 1.5 %collective-permute-start.6 = (bf16[40,5120]{1,0:T(8,128)(2,1)S(1)}, bf16[40,5120]{1,0:T(8,128)(2,1)S(1)}, u32[]{:S(2)}, u32[]{:S(2)}) collective-permute-start(bf16[40,5120]{1,0:T(8,128)(2,1)S(1)} %collective-permute-done.3.refs_8_), channel_id=1, source_target_pairs={{0,32},{16,48},{32,64},{48,80},{64,96},{80,112},{96,0},{112,16},{1... | collective-permute-start | bytes 1228808 | tf_op jit(solution)/shard_map/ppermute | solution.py:497
  74.0 6.0 %all-to-all-done.3.x_ref = bf16[16,64,128]{2,1,0:T(8,128)(2,1)S(1)} async-done(((bf16[16,64,128]{2,1,0:T(8,128)(2,1)}), bf16[16,64,128]{2,1,0:T(8,128)(2,1)S(1)}, u32[]{:S(2)}, u32[]{:S(2)}) %all-to-all-start.3) | async-done | bytes 262176 | tf_op jit(solution)/shard_map/all_to_all | solution.py:499
  80.0 0.0 collective-permute-done.4.refs_5_
  80.0 0.0 collective-permute-start.8
  80.0 2.7 %collective-permute-start.7 = (bf16[40,5120]{1,0:T(8,128)(2,1)S(1)}, bf16[40,5120]{1,0:T(8,128)(2,1)}, u32[]{:S(2)}, u32[]{:S(2)}) collective-permute-start(bf16[40,5120]{1,0:T(8,128)(2,1)S(1)} %collective-permute-done.4.refs_5_), channel_id=1, source_target_pairs={{0,96},{16,112},{32,0},{48,16},{64,32},{80,48},{96,64},{112,80},{1... | collective-permute-start | bytes 1228808 | tf_op jit(solution)/shard_map/ppermute | solution.py:501
  82.7 1.0 %merge.1 = bf16[16,40,128]{2,1,0:T(8,128)(2,1)} custom-call(bf16[16,64,128]{2,1,0:T(8,128)(2,1)S(1)} %all-to-all-done.3.x_ref), custom_call_target="tpu_custom_call" | custom-call | tf_op jit(solution)/shard_map/merge/pallas_call | solution.py:402
  83.7 4.3 %all-to-all-start.4 = ((bf16[16,40,128]{2,1,0:T(8,128)(2,1)}), bf16[16,40,128]{2,1,0:T(8,128)(2,1)S(1)}, u32[]{:S(2)}, u32[]{:S(2)}) async-start(bf16[16,40,128]{2,1,0:T(8,128)(2,1)} %merge.1), calls=%async_computation.4 | async-start | bytes 327680 | tf_op jit(solution)/shard_map/all_to_all | solution.py:503
  88.0 0.0 collective-permute-done.5.refs_4_
  88.0 0.0 collective-permute-done.6.refs_6_
  88.0 6.5 %all-to-all-done.4.refs_0_ = bf16[16,40,128]{2,1,0:T(8,128)(2,1)S(1)} async-done(((bf16[16,40,128]{2,1,0:T(8,128)(2,1)}), bf16[16,40,128]{2,1,0:T(8,128)(2,1)S(1)}, u32[]{:S(2)}, u32[]{:S(2)}) %all-to-all-start.4) | async-done | bytes 163872 | tf_op jit(solution)/shard_map/all_to_all | solution.py:503
  94.6 0.0 collective-permute-done.8.refs_9_
  94.6 0.0 collective-permute-done.7.refs_7_
  94.6 1.9 %copy-done.1 = bf16[5120,320]{0,1:T(8,128)(2,1)S(1)} copy-done((bf16[5120,320]{0,1:T(8,128)(2,1)S(1)}, bf16[5120,320]{0,1:T(8,128)(2,1)}, u32[]{:S(2)}) %copy-start.1) | copy-done | bytes 3276824
  96.5 3.6 %output.1 = bf16[4,4,320]{2,1,0:T(4,128)(2,1)} custom-call(bf16[16,40,128]{2,1,0:T(8,128)(2,1)S(1)} %all-to-all-done.4.refs_0_, bf16[320,5120]{1,0:T(8,128)(2,1)S(1)} %bitcast.8, bf16[40,5120]{1,0:T(8,128)(2,1)S(1)} %bitcast.13, bf16[40,5120]{1,0:T(8,128)(2,1)S(1)} %collective-permute-done.2.refs_3_, bf16[40,5120]{1,0:T(8,128)(2,1)S(1)} %collective-permute-done.5.refs_4_, ...), custom_call_target="tpu_custom_call" | custom-call | tf_op jit(solution)/shard_map/output/pallas_call | solution.py:441
  (9 shorter events, 0.0 us)
Async XLA Ops:
  0.0 22.4 %collective-permute-start = (bf16[40,7168]{1,0:T(8,128)(2,1)}, bf16[40,7168]{1,0:T(8,128)(2,1)S(1)}, u32[]{:S(2)}, u32[]{:S(2)}) collective-permute-start(bf16[40,7168]{1,0:T(8,128)(2,1)} %new_ref.1), channel_id=1, source_target_pairs={{0,16},{16,0},{32,48},{48,32},{64,80},{80,64},{96,112},{112,96},{1... | collective-permute-start | bytes 1720328 | tf_op jit(solution)/shard_map/ppermute | solution.py:475
  4.4 10.6 %copy-start.5 = (bf16[320]{0:T(512)(128)(2,1)S(1)}, bf16[320]{0:T(512)(128)(2,1)}, u32[]{:S(2)}) copy-start(bf16[320]{0:T(512)(128)(2,1)} %param.12) | copy-start | bytes 1924
  4.4 17.9 %copy-start.2 = (bf16[40,7168]{1,0:T(8,128)(2,1)S(1)}, bf16[40,7168]{1,0:T(8,128)(2,1)}, u32[]{:S(2)}) copy-start(bf16[40,7168]{1,0:T(8,128)(2,1)} %new_ref.1) | copy-start | bytes 1720324
  11.6 6.0 %copy-start.4 = (s32[4]{0:T(128)S(1)}, s32[4]{0:T(128)}, u32[]{:S(2)}) copy-start(s32[4]{0:T(128)} %len_ref.1) | copy-start | bytes 52
  11.6 10.8 %all-to-all-start = ((bf16[8,128,128]{2,1,0:T(8,128)(2,1)}), bf16[8,128,128]{2,1,0:T(8,128)(2,1)S(1)}, u32[]{:S(2)}, u32[]{:S(2)}) async-start(bf16[8,128,128]{2,1,0:T(8,128)(2,1)} %gather_rows.1), calls=%async_computation | async-start | bytes 524288 | tf_op jit(solution)/shard_map/all_to_all | solution.py:480
  15.1 2.3 %copy-start = (bf16[320,7168]{1,0:T(8,128)(2,1)S(1)}, bf16[320,7168]{1,0:T(8,128)(2,1)}, u32[]{:S(2)}) copy-start(bf16[320,7168]{1,0:T(8,128)(2,1)} %refs_2_) | copy-start | bytes 13762564
  17.4 28.6 %copy-start.3 = (bf16[5120,40]{0,1:T(8,128)(2,1)S(1)}, bf16[5120,40]{0,1:T(8,128)(2,1)}, u32[]{:S(2)}) copy-start(bf16[5120,40]{0,1:T(8,128)(2,1)} %param.16) | copy-start | bytes 1228804
  23.2 4.2 %collective-permute-start.1 = (f32[1280,128]{1,0:T(8,128)S(1)}, f32[1280,128]{1,0:T(8,128)S(1)}, u32[]{:S(2)}, u32[]{:S(2)}) collective-permute-start(f32[1280,128]{1,0:T(8,128)S(1)} %get-tuple-element.26), channel_id=1, source_target_pairs={{0,1},{1,0},{2,3},{3,2},{4,5},{5,4},{6,7},{7,6},{8,9},{9,8},{10,11... | collective-permute-start | bytes 1966088 | tf_op jit(solution)/shard_map/ppermute | solution.py:483
  46.0 17.8 %slice-start = ((s8[8388608]{0:T(1024)(128)(4,1)}), s8[4194304]{0:T(1024)(128)(4,1)S(1)}, s32[]{:S(2)}) async-start(s8[8388608]{0:T(1024)(128)(4,1)} %bitcast.6), calls=%async_computation.5 | async-start | bytes 8388608
  46.0 17.8 %slice-start.1 = ((s8[8388608]{0:T(1024)(128)(4,1)}), s8[4194304]{0:T(1024)(128)(4,1)S(1)}, s32[]{:S(2)}) async-start(s8[8388608]{0:T(1024)(128)(4,1)} %bitcast.6), calls=%async_computation.6 | async-start | bytes 8388608
  46.0 15.5 %collective-permute-start.3 = (bf16[40,5120]{1,0:T(8,128)(2,1)S(1)}, bf16[40,5120]{1,0:T(8,128)(2,1)S(1)}, u32[]{:S(2)}, u32[]{:S(2)}) collective-permute-start(bf16[40,5120]{1,0:T(8,128)(2,1)S(1)} %bitcast.10), channel_id=1, source_target_pairs={{0,32},{16,48},{32,64},{48,80},{64,96},{80,112},{96,0},{112,16},{1... | collective-permute-start | bytes 1228808 | tf_op jit(solution)/shard_map/ppermute | solution.py:493
  46.0 15.5 %collective-permute-start.2 = (bf16[40,5120]{1,0:T(8,128)(2,1)S(1)}, bf16[40,5120]{1,0:T(8,128)(2,1)S(1)}, u32[]{:S(2)}, u32[]{:S(2)}) collective-permute-start(bf16[40,5120]{1,0:T(8,128)(2,1)S(1)} %bitcast.11), channel_id=1, source_target_pairs={{0,16},{16,0},{32,48},{48,32},{64,80},{80,64},{96,112},{112,96},{1... | collective-permute-start | bytes 1228808 | tf_op jit(solution)/shard_map/ppermute | solution.py:492
  61.4 18.6 %collective-permute-start.4 = (bf16[40,5120]{1,0:T(8,128)(2,1)S(1)}, bf16[40,5120]{1,0:T(8,128)(2,1)S(1)}, u32[]{:S(2)}, u32[]{:S(2)}) collective-permute-start(bf16[40,5120]{1,0:T(8,128)(2,1)S(1)} %collective-permute-done.2.refs_3_), channel_id=1, source_target_pairs={{0,96},{16,112},{32,0},{48,16},{64,32},{80,48},{96,64},{112,80},{1... | collective-permute-start | bytes 1228808 | tf_op jit(solution)/shard_map/ppermute | solution.py:498
  68.5 11.5 %all-to-all-start.3 = ((bf16[16,64,128]{2,1,0:T(8,128)(2,1)}), bf16[16,64,128]{2,1,0:T(8,128)(2,1)S(1)}, u32[]{:S(2)}, u32[]{:S(2)}) async-start(bf16[16,64,128]{2,1,0:T(8,128)(2,1)} %attend.1), calls=%async_computation.3 | async-start | bytes 524288 | tf_op jit(solution)/shard_map/all_to_all | solution.py:499
  72.6 15.5 %collective-permute-start.5 = (bf16[40,5120]{1,0:T(8,128)(2,1)S(1)}, bf16[40,5120]{1,0:T(8,128)(2,1)S(1)}, u32[]{:S(2)}, u32[]{:S(2)}) collective-permute-start(bf16[40,5120]{1,0:T(8,128)(2,1)S(1)} %bitcast.12), channel_id=1, source_target_pairs={{0,96},{16,112},{32,0},{48,16},{64,32},{80,48},{96,64},{112,80},{1... | collective-permute-start | bytes 1228808 | tf_op jit(solution)/shard_map/ppermute | solution.py:494
  72.6 15.5 %collective-permute-start.6 = (bf16[40,5120]{1,0:T(8,128)(2,1)S(1)}, bf16[40,5120]{1,0:T(8,128)(2,1)S(1)}, u32[]{:S(2)}, u32[]{:S(2)}) collective-permute-start(bf16[40,5120]{1,0:T(8,128)(2,1)S(1)} %collective-permute-done.3.refs_8_), channel_id=1, source_target_pairs={{0,32},{16,48},{32,64},{48,80},{64,96},{80,112},{96,0},{112,16},{1... | collective-permute-start | bytes 1228808 | tf_op jit(solution)/shard_map/ppermute | solution.py:497
  80.0 14.5 %collective-permute-start.8 = (bf16[40,5120]{1,0:T(8,128)(2,1)S(1)}, bf16[40,5120]{1,0:T(8,128)(2,1)S(1)}, u32[]{:S(2)}, u32[]{:S(2)}) collective-permute-start(bf16[40,5120]{1,0:T(8,128)(2,1)S(1)} %collective-permute-done.2.refs_3_), channel_id=1, source_target_pairs={{0,32},{16,48},{32,64},{48,80},{64,96},{80,112},{96,0},{112,16},{1... | collective-permute-start | bytes 1228808 | tf_op jit(solution)/shard_map/ppermute | solution.py:502
  80.0 14.5 %collective-permute-start.7 = (bf16[40,5120]{1,0:T(8,128)(2,1)S(1)}, bf16[40,5120]{1,0:T(8,128)(2,1)}, u32[]{:S(2)}, u32[]{:S(2)}) collective-permute-start(bf16[40,5120]{1,0:T(8,128)(2,1)S(1)} %collective-permute-done.4.refs_5_), channel_id=1, source_target_pairs={{0,96},{16,112},{32,0},{48,16},{64,32},{80,48},{96,64},{112,80},{1... | collective-permute-start | bytes 1228808 | tf_op jit(solution)/shard_map/ppermute | solution.py:501
  83.7 10.8 %all-to-all-start.4 = ((bf16[16,40,128]{2,1,0:T(8,128)(2,1)}), bf16[16,40,128]{2,1,0:T(8,128)(2,1)S(1)}, u32[]{:S(2)}, u32[]{:S(2)}) async-start(bf16[16,40,128]{2,1,0:T(8,128)(2,1)} %merge.1), calls=%async_computation.4 | async-start | bytes 327680 | tf_op jit(solution)/shard_map/all_to_all | solution.py:503
  94.6 1.9 %copy-start.1 = (bf16[5120,320]{0,1:T(8,128)(2,1)S(1)}, bf16[5120,320]{0,1:T(8,128)(2,1)}, u32[]{:S(2)}) copy-start(bf16[5120,320]{0,1:T(8,128)(2,1)} %param.14) | copy-start | bytes 9830404

commit v5 on v4

--- a/solution.py
+++ b/solution.py
@@ -285,7 +285,7 @@
         in_specs=[VMEM, VMEM, VMEM] + [ANY] * len(far),
         out_specs=VMEM,
         out_shape=jax.ShapeDtypeStruct((N_TP, BLOCK, LANES), bf16),
-        compiler_params=params(53.5),
+        compiler_params=params(52),
         name="finish",
     )(received, cosine, sine, *far)
 
@@ -493,11 +493,15 @@
     behind_own = lax.ppermute(own, "rep", ahead)
     front_own = lax.ppermute(own, "rep", back)
     projected = lax.all_to_all(finish(partials, cosine, sine, embed_table.T, embed_table.T, old_qkv), "tp", 0, 0)
-    projected, other, behind_own = lax.optimization_barrier((projected, other, behind_own))
+    projected, other, behind_own, front_own = lax.optimization_barrier(
+        (projected, other, behind_own, front_own)
+    )
     far_own = lax.ppermute(behind_own, "rep", ahead)
     front_other = lax.ppermute(other, "rep", back)
     parts = lax.all_to_all(attend(cache_len, projected, kv_cache), "tp", 0, 0)
-    parts, front_other, other = lax.optimization_barrier((parts, front_other, other))
+    parts, front_other, other, far_own = lax.optimization_barrier(
+        (parts, front_other, other, far_own)
+    )
     far_other = lax.ppermute(front_other, "rep", back)
     behind_other = lax.ppermute(other, "rep", ahead)
     heads = lax.all_to_all(merge(parts), "tp", 0, 0)

time: 102 us -> 96.9 us (0.950); the launches traced: 100 us -> 97.1 us
  blocking collectives: 30.3 us -> 53.1 us
  waiting for transfers between devices: 17.6 us -> 5.24 us
  starting transfers between devices: 26.8 us -> 19.7 us
  Pallas kernels: 19.6 us -> 15.2 us
  local copies, waits for them, and re-layouts: 4.84 us -> 2.92 us
    all_to_all x0 -> x2, blocking collectives: none -> 22 us  [the longest x1 12.4 us: body(): parts = lax.all_to_all(attend(cache_len, projected, kv_cache), 'tp', 0, 0)]
    all_to_all x2 -> x0, waiting for transfers between devices: 12.5 us -> none  [the longest x1 6.52 us: body(): heads = lax.all_to_all(merge(parts), 'tp', 0, 0)]
    all_to_all x2 -> x0, starting transfers between devices: 8.31 us -> none  [the longest x1 4.29 us: body(): heads = lax.all_to_all(merge(parts), 'tp', 0, 0)]
    unnamed x16, local copies, waits for them, and re-layouts: 4.25 us -> 2.32 us
    pallas_call x1, Pallas kernels: 1.95 us -> 0.12 us  [finish(): pl.pallas_call(finish_kernel, in_specs=[VMEM, VMEM, VMEM] + [ANY] * len(f...]
    all_to_all x1, starting transfers between devices: 3.47 us -> 5.11 us  [body(): rows = lax.all_to_all(rows, 'rep', 0, 0)]
    ppermute x1, starting transfers between devices: 1.46 us -> 0.01 us  [body(): far_own = lax.ppermute(behind_own, 'rep', ahead)]
  transfers between devices with their start and end apart: 12 -> 10, of which waited for: 4 -> 2; matrix products, arithmetic and copies ran while one was open for 1% -> 1% of each run, Pallas kernels for 15% -> 12%
where the time goes in v5:
time: 96.9 us; the launch traced here: 97.1 us
  blocking collectives  53.1 us (55%)
  starting transfers between devices  19.7 us (20%)
  Pallas kernels  15.2 us (16%)
  waiting for transfers between devices  5.24 us (5%)
  local copies, waits for them, and re-layouts  2.92 us (3%)
    all_to_all x1, blocking collectives, body(): lax.all_to_all(summed, ('rep', 'tp'), 0, 0, axis_index_groups=groups)  18.4 us
    all_to_all x1, blocking collectives, body(): lax.all_to_all(finish(partials, cosine, sine, embed_table.T, embed_table....  12.6 us
    all_to_all x1, blocking collectives, body(): parts = lax.all_to_all(attend(cache_len, projected, kv_cache), 'tp', 0, 0)  12.4 us
    all_to_all x1, blocking collectives, body(): heads = lax.all_to_all(merge(parts), 'tp', 0, 0)  9.63 us
    pallas_call x1, Pallas kernels, gather_rows(): pl.pallas_call(gather_kernel, grid=(1,), in_specs=[SMEM, pl.BlockSpec((FE...  6.92 us
    all_to_all x1, starting transfers between devices, body(): rows = lax.all_to_all(rows, 'rep', 0, 0)  5.11 us
    ppermute x1, starting transfers between devices, body(): other_qkv = lax.ppermute(new_qkv, 'rep', turn)  4.43 us
    pallas_call x1, Pallas kernels, attend(): pl.pallas_call(attend_kernel, grid=(ROWS,), in_specs=[SMEM, whole, VMEM],...  4.07 us
  transfers between devices with their start and end apart: 10, of which 2 were waited for; matrix products, arithmetic and copies ran while one was open for 1% of the time, Pallas kernels for 12%

profile of v5, /device:TPU:1, one launch (start us, length us, event | category | flops | bytes accessed | tf_op | source)
XLA Modules:
  0.0 97.1 jit_solution(16206919074750878672)
XLA Ops:
  0.0 4.4 %collective-permute-start = (bf16[40,7168]{1,0:T(8,128)(2,1)}, bf16[40,7168]{1,0:T(8,128)(2,1)S(1)}, u32[]{:S(2)}, u32[]{:S(2)}) collective-permute-start(bf16[40,7168]{1,0:T(8,128)(2,1)} %new_ref.1), channel_id=1, source_target_pairs={{0,16},{16,0},{32,48},{48,32},{64,80},{80,64},{96,112},{112,96},{1... | collective-permute-start | bytes 1720328 | tf_op jit(solution)/shard_map/ppermute | solution.py:475
  4.4 0.0 copy-start.5
  4.4 0.0 copy-start.2
  4.4 6.9 %gather_rows.1 = bf16[8,128,128]{2,1,0:T(8,128)(2,1)} custom-call(s32[4,32]{1,0:T(4,128)} %bitcast.18, bf16[320,9504]{1,0:T(8,128)(2,1)} %bitcast.14, bf16[320,9504]{1,0:T(8,128)(2,1)} %bitcast.15), custom_call_target="tpu_custom_call" | custom-call | tf_op jit(solution)/shard_map/gather_rows/pallas_call | solution.py:127
  11.4 0.0 copy-start.4
  11.4 5.1 %all-to-all-start = ((bf16[8,128,128]{2,1,0:T(8,128)(2,1)}), bf16[8,128,128]{2,1,0:T(8,128)(2,1)S(1)}, u32[]{:S(2)}, u32[]{:S(2)}) async-start(bf16[8,128,128]{2,1,0:T(8,128)(2,1)} %gather_rows.1), calls=%async_computation | async-start | bytes 524288 | tf_op jit(solution)/shard_map/all_to_all | solution.py:480
  16.5 0.0 copy-done.5
  16.5 0.0 copy-start
  16.5 2.3 %copy-done = bf16[320,7168]{1,0:T(8,128)(2,1)S(1)} copy-done((bf16[320,7168]{1,0:T(8,128)(2,1)S(1)}, bf16[320,7168]{1,0:T(8,128)(2,1)}, u32[]{:S(2)}) %copy-start) | copy-done | bytes 4587544
  18.8 0.0 copy-start.3
  18.8 0.1 take_old_columns.1.old
  18.9 0.0 copy-done.4
  19.0 0.6 dynamic_slice.3
  20.2 0.1 fusion
  20.3 0.1 pad_maximum_fusion
  20.4 3.5 %all-to-all-done.x_ref = bf16[8,128,128]{2,1,0:T(8,128)(2,1)S(1)} async-done(((bf16[8,128,128]{2,1,0:T(8,128)(2,1)}), bf16[8,128,128]{2,1,0:T(8,128)(2,1)S(1)}, u32[]{:S(2)}, u32[]{:S(2)}) %all-to-all-start) | async-done | bytes 262176 | tf_op jit(solution)/shard_map/all_to_all | solution.py:480
  23.9 0.0 collective-permute-done.other_ref
  23.9 0.0 copy-done.2
  23.9 0.8 project.1
  24.8 2.3 %collective-permute-start.1 = (f32[1280,128]{1,0:T(8,128)S(1)}, f32[1280,128]{1,0:T(8,128)S(1)}, u32[]{:S(2)}, u32[]{:S(2)}) collective-permute-start(f32[1280,128]{1,0:T(8,128)S(1)} %get-tuple-element.28), channel_id=1, source_target_pairs={{0,1},{1,0},{2,3},{3,2},{4,5},{5,4},{6,7},{7,6},{8,9},{9,8},{10,11... | collective-permute-start | bytes 1966088 | tf_op jit(solution)/shard_map/ppermute | solution.py:483
  27.1 1.7 %collective-permute-done.1.b_ref = f32[1280,128]{1,0:T(8,128)S(1)} collective-permute-done((f32[1280,128]{1,0:T(8,128)S(1)}, f32[1280,128]{1,0:T(8,128)S(1)}, u32[]{:S(2)}, u32[]{:S(2)}) %collective-permute-start.1) | collective-permute-done | bytes 655392 | tf_op jit(solution)/shard_map/ppermute | solution.py:483
  28.8 0.1 add.23
  28.9 18.4 %all_to_all.25.x_ref = f32[32,40,128]{2,1,0:T(8,128)S(1)} all-to-all(f32[32,40,128]{2,1,0:T(8,128)S(1)} %bitcast.9), channel_id=1, replica_groups={{0,2,4,6,8,10,12,14,32,34,36,38,40,42,44,46,64,66,68,70,72,74,76,78,96,..., dimensions={0} | all-to-all | bytes 1310720 | tf_op jit(solution)/shard_map/all_to_all | solution.py:490
  47.3 0.0 copy-done.3
  47.3 0.7 collective-permute-start.4
  48.0 0.8 collective-permute-start.3
  48.8 1.2 %collective-permute-start.2 = (bf16[40,5120]{1,0:T(8,128)(2,1)S(1)}, bf16[40,5120]{1,0:T(8,128)(2,1)S(1)}, u32[]{:S(2)}, u32[]{:S(2)}) collective-permute-start(bf16[40,5120]{1,0:T(8,128)(2,1)S(1)} %bitcast.12), channel_id=1, source_target_pairs={{0,16},{16,0},{32,48},{48,32},{64,80},{80,64},{96,112},{112,96},{1... | collective-permute-start | bytes 1228808 | tf_op jit(solution)/shard_map/ppermute | solution.py:492
  50.0 0.1 finish.1
  50.1 12.6 %all_to_all.26.q_ref = bf16[16,64,128]{2,1,0:T(8,128)(2,1)S(1)} all-to-all(bf16[16,64,128]{2,1,0:T(8,128)(2,1)S(1)} %finish.1), channel_id=1, replica_groups=mesh['rep'=8,'tp'=16] {'tp'}, dimensions={0} | all-to-all | bytes 524288 | tf_op jit(solution)/shard_map/all_to_all | solution.py:495
  62.8 0.0 collective-permute-done.4.refs_4_
  62.8 0.0 collective-permute-done.3.refs_8_
  62.8 0.0 collective-permute-done.2.refs_3_
  62.8 2.1 %collective-permute-start.5 = (bf16[40,5120]{1,0:T(8,128)(2,1)S(1)}, bf16[40,5120]{1,0:T(8,128)(2,1)S(1)}, u32[]{:S(2)}, u32[]{:S(2)}) collective-permute-start(bf16[40,5120]{1,0:T(8,128)(2,1)S(1)} %collective-permute-done.2.refs_3_), channel_id=1, source_target_pairs={{0,96},{16,112},{32,0},{48,16},{64,32},{80,48},{96,64},{112,80},{1... | collective-permute-start | bytes 1228808 | tf_op jit(solution)/shard_map/ppermute | solution.py:500
  64.9 0.0 collective-permute-start.6
  64.9 0.0 slice-done
  64.9 0.0 slice-done.1
  64.9 4.1 %attend.1 = bf16[16,64,128]{2,1,0:T(8,128)(2,1)S(1)} custom-call(s32[4]{0:T(128)S(1)} %copy-done.4, bf16[16,64,128]{2,1,0:T(8,128)(2,1)S(1)} %all_to_all.26.q_ref, bf16[4,512,2048]{2,1,0:T(8,128)(2,1)S(1)} %bitcast.7), custom_call_target="tpu_custom_call" | custom-call | tf_op jit(solution)/shard_map/attend/pallas_call | solution.py:373
  69.0 12.4 %all_to_all.27.x_ref = bf16[16,64,128]{2,1,0:T(8,128)(2,1)S(1)} all-to-all(bf16[16,64,128]{2,1,0:T(8,128)(2,1)S(1)} %attend.1), channel_id=1, replica_groups=mesh['rep'=8,'tp'=16] {'tp'}, dimensions={0} | all-to-all | bytes 524288 | tf_op jit(solution)/shard_map/all_to_all | solution.py:501
  81.4 0.0 collective-permute-done.5.refs_5_
  81.4 0.0 collective-permute-done.6.refs_6_
  81.4 0.0 collective-permute-start.8
  81.4 3.0 %collective-permute-start.7 = (bf16[40,5120]{1,0:T(8,128)(2,1)S(1)}, bf16[40,5120]{1,0:T(8,128)(2,1)S(1)}, u32[]{:S(2)}, u32[]{:S(2)}) collective-permute-start(bf16[40,5120]{1,0:T(8,128)(2,1)S(1)} %collective-permute-done.5.refs_5_), channel_id=1, source_target_pairs={{0,96},{16,112},{32,0},{48,16},{64,32},{80,48},{96,64},{112,80},{1... | collective-permute-start | bytes 1228808 | tf_op jit(solution)/shard_map/ppermute | solution.py:505
  84.4 0.4 merge.1
  84.8 9.6 %all_to_all.28.refs_0_ = bf16[16,40,128]{2,1,0:T(8,128)(2,1)S(1)} all-to-all(bf16[16,40,128]{2,1,0:T(8,128)(2,1)S(1)} %merge.1), channel_id=1, replica_groups=mesh['rep'=8,'tp'=16] {'tp'}, dimensions={0} | all-to-all | bytes 327680 | tf_op jit(solution)/shard_map/all_to_all | solution.py:507
  94.4 0.0 collective-permute-done.8.refs_9_
  94.4 0.0 collective-permute-done.7.refs_7_
  94.4 0.0 copy-done.1
  94.4 2.7 %output.1 = bf16[4,4,320]{2,1,0:T(4,128)(2,1)} custom-call(bf16[16,40,128]{2,1,0:T(8,128)(2,1)S(1)} %all_to_all.28.refs_0_, bf16[320,5120]{1,0:T(8,128)(2,1)S(1)} %bitcast.8, bf16[40,5120]{1,0:T(8,128)(2,1)S(1)} %bitcast.13, bf16[40,5120]{1,0:T(8,128)(2,1)S(1)} %collective-permute-done.2.refs_3_, bf16[40,5120]{1,0:T(8,128)(2,1)S(1)} %collective-permute-done.4.refs_4_, ...), custom_call_target="tpu_custom_call" | custom-call | tf_op jit(solution)/shard_map/output/pallas_call | solution.py:441
  (7 shorter events, 0.0 us)
Async XLA Ops:
  0.0 23.9 %collective-permute-start = (bf16[40,7168]{1,0:T(8,128)(2,1)}, bf16[40,7168]{1,0:T(8,128)(2,1)S(1)}, u32[]{:S(2)}, u32[]{:S(2)}) collective-permute-start(bf16[40,7168]{1,0:T(8,128)(2,1)} %new_ref.1), channel_id=1, source_target_pairs={{0,16},{16,0},{32,48},{48,32},{64,80},{80,64},{96,112},{112,96},{1... | collective-permute-start | bytes 1720328 | tf_op jit(solution)/shard_map/ppermute | solution.py:475
  4.4 12.1 %copy-start.5 = (bf16[320]{0:T(512)(128)(2,1)S(1)}, bf16[320]{0:T(512)(128)(2,1)}, u32[]{:S(2)}) copy-start(bf16[320]{0:T(512)(128)(2,1)} %param.12) | copy-start | bytes 1924
  4.4 19.5 %copy-start.2 = (bf16[40,7168]{1,0:T(8,128)(2,1)S(1)}, bf16[40,7168]{1,0:T(8,128)(2,1)}, u32[]{:S(2)}) copy-start(bf16[40,7168]{1,0:T(8,128)(2,1)} %new_ref.1) | copy-start | bytes 1720324
  11.4 7.6 %copy-start.4 = (s32[4]{0:T(128)S(1)}, s32[4]{0:T(128)}, u32[]{:S(2)}) copy-start(s32[4]{0:T(128)} %len_ref.1) | copy-start | bytes 52
  11.4 12.5 %all-to-all-start = ((bf16[8,128,128]{2,1,0:T(8,128)(2,1)}), bf16[8,128,128]{2,1,0:T(8,128)(2,1)S(1)}, u32[]{:S(2)}, u32[]{:S(2)}) async-start(bf16[8,128,128]{2,1,0:T(8,128)(2,1)} %gather_rows.1), calls=%async_computation | async-start | bytes 524288 | tf_op jit(solution)/shard_map/all_to_all | solution.py:480
  16.5 2.3 %copy-start = (bf16[320,7168]{1,0:T(8,128)(2,1)S(1)}, bf16[320,7168]{1,0:T(8,128)(2,1)}, u32[]{:S(2)}) copy-start(bf16[320,7168]{1,0:T(8,128)(2,1)} %refs_2_) | copy-start | bytes 13762564
  18.8 28.5 %copy-start.3 = (bf16[5120,40]{0,1:T(8,128)(2,1)S(1)}, bf16[5120,40]{0,1:T(8,128)(2,1)}, u32[]{:S(2)}) copy-start(bf16[5120,40]{0,1:T(8,128)(2,1)} %param.16) | copy-start | bytes 1228804
  24.8 4.1 %collective-permute-start.1 = (f32[1280,128]{1,0:T(8,128)S(1)}, f32[1280,128]{1,0:T(8,128)S(1)}, u32[]{:S(2)}, u32[]{:S(2)}) collective-permute-start(f32[1280,128]{1,0:T(8,128)S(1)} %get-tuple-element.28), channel_id=1, source_target_pairs={{0,1},{1,0},{2,3},{3,2},{4,5},{5,4},{6,7},{7,6},{8,9},{9,8},{10,11... | collective-permute-start | bytes 1966088 | tf_op jit(solution)/shard_map/ppermute | solution.py:483
  47.3 17.6 %slice-start = ((s8[8388608]{0:T(1024)(128)(4,1)}), s8[4194304]{0:T(1024)(128)(4,1)S(1)}, s32[]{:S(2)}) async-start(s8[8388608]{0:T(1024)(128)(4,1)} %bitcast.6), calls=%async_computation.5 | async-start | bytes 8388608
  47.3 17.6 %slice-start.1 = ((s8[8388608]{0:T(1024)(128)(4,1)}), s8[4194304]{0:T(1024)(128)(4,1)S(1)}, s32[]{:S(2)}) async-start(s8[8388608]{0:T(1024)(128)(4,1)} %bitcast.6), calls=%async_computation.6 | async-start | bytes 8388608
  47.3 15.5 %collective-permute-start.4 = (bf16[40,5120]{1,0:T(8,128)(2,1)S(1)}, bf16[40,5120]{1,0:T(8,128)(2,1)S(1)}, u32[]{:S(2)}, u32[]{:S(2)}) collective-permute-start(bf16[40,5120]{1,0:T(8,128)(2,1)S(1)} %bitcast.10), channel_id=1, source_target_pairs={{0,96},{16,112},{32,0},{48,16},{64,32},{80,48},{96,64},{112,80},{1... | collective-permute-start | bytes 1228808 | tf_op jit(solution)/shard_map/ppermute | solution.py:494
  48.0 14.8 %collective-permute-start.3 = (bf16[40,5120]{1,0:T(8,128)(2,1)S(1)}, bf16[40,5120]{1,0:T(8,128)(2,1)S(1)}, u32[]{:S(2)}, u32[]{:S(2)}) collective-permute-start(bf16[40,5120]{1,0:T(8,128)(2,1)S(1)} %bitcast.11), channel_id=1, source_target_pairs={{0,32},{16,48},{32,64},{48,80},{64,96},{80,112},{96,0},{112,16},{1... | collective-permute-start | bytes 1228808 | tf_op jit(solution)/shard_map/ppermute | solution.py:493
  48.8 14.0 %collective-permute-start.2 = (bf16[40,5120]{1,0:T(8,128)(2,1)S(1)}, bf16[40,5120]{1,0:T(8,128)(2,1)S(1)}, u32[]{:S(2)}, u32[]{:S(2)}) collective-permute-start(bf16[40,5120]{1,0:T(8,128)(2,1)S(1)} %bitcast.12), channel_id=1, source_target_pairs={{0,16},{16,0},{32,48},{48,32},{64,80},{80,64},{96,112},{112,96},{1... | collective-permute-start | bytes 1228808 | tf_op jit(solution)/shard_map/ppermute | solution.py:492
  62.8 31.6 %copy-start.1 = (bf16[5120,320]{0,1:T(8,128)(2,1)S(1)}, bf16[5120,320]{0,1:T(8,128)(2,1)}, u32[]{:S(2)}) copy-start(bf16[5120,320]{0,1:T(8,128)(2,1)} %param.14) | copy-start | bytes 9830404
  62.8 18.6 %collective-permute-start.5 = (bf16[40,5120]{1,0:T(8,128)(2,1)S(1)}, bf16[40,5120]{1,0:T(8,128)(2,1)S(1)}, u32[]{:S(2)}, u32[]{:S(2)}) collective-permute-start(bf16[40,5120]{1,0:T(8,128)(2,1)S(1)} %collective-permute-done.2.refs_3_), channel_id=1, source_target_pairs={{0,96},{16,112},{32,0},{48,16},{64,32},{80,48},{96,64},{112,80},{1... | collective-permute-start | bytes 1228808 | tf_op jit(solution)/shard_map/ppermute | solution.py:500
  64.9 16.5 %collective-permute-start.6 = (bf16[40,5120]{1,0:T(8,128)(2,1)S(1)}, bf16[40,5120]{1,0:T(8,128)(2,1)S(1)}, u32[]{:S(2)}, u32[]{:S(2)}) collective-permute-start(bf16[40,5120]{1,0:T(8,128)(2,1)S(1)} %collective-permute-done.3.refs_8_), channel_id=1, source_target_pairs={{0,32},{16,48},{32,64},{48,80},{64,96},{80,112},{96,0},{112,16},{1... | collective-permute-start | bytes 1228808 | tf_op jit(solution)/shard_map/ppermute | solution.py:499
  81.4 13.0 %collective-permute-start.8 = (bf16[40,5120]{1,0:T(8,128)(2,1)S(1)}, bf16[40,5120]{1,0:T(8,128)(2,1)S(1)}, u32[]{:S(2)}, u32[]{:S(2)}) collective-permute-start(bf16[40,5120]{1,0:T(8,128)(2,1)S(1)} %collective-permute-done.2.refs_3_), channel_id=1, source_target_pairs={{0,32},{16,48},{32,64},{48,80},{64,96},{80,112},{96,0},{112,16},{1... | collective-permute-start | bytes 1228808 | tf_op jit(solution)/shard_map/ppermute | solution.py:506
  81.4 13.0 %collective-permute-start.7 = (bf16[40,5120]{1,0:T(8,128)(2,1)S(1)}, bf16[40,5120]{1,0:T(8,128)(2,1)S(1)}, u32[]{:S(2)}, u32[]{:S(2)}) collective-permute-start(bf16[40,5120]{1,0:T(8,128)(2,1)S(1)} %collective-permute-done.5.refs_5_), channel_id=1, source_target_pairs={{0,96},{16,112},{32,0},{48,16},{64,32},{80,48},{96,64},{112,80},{1... | collective-permute-start | bytes 1228808 | tf_op jit(solution)/shard_map/ppermute | solution.py:505

commit v6 on v5

--- a/solution.py
+++ b/solution.py
@@ -52,22 +52,19 @@
     kwargs = dict(dimension_semantics=("arbitrary",) * grid) if grid else {}
     return pltpu.CompilerParams(vmem_limit_bytes=int(mib * MIB), **kwargs)
 
-def gather_kernel(ids_ref, tail_ref, table_ref, out_ref, buf, cols, found, sems):
+def gather_kernel(ids_ref, tail_ref, table_ref, out_ref, buf, cols, found, places, sems):
     window = table_ref.shape[1]
     tail_start = window // LANES * LANES
     start = lax.axis_index("rep") * window
 
-    def local_id(i):
+    count = jnp.int32(0)
+    for i in range(TOKENS):
         step = ((i >> 5) & 1) * 2 + (i & 1)
         row = ((i >> 3) & 3) * 8 + (i >> 6) * 4 + ((i >> 1) & 3)
-        return ids_ref[step, row] - start
-
-    def note(i, count):
-        local = local_id(i)
+        local = ids_ref[step, row] - start
         found[count] = i
-        return count + ((local >= 0) & (local < window)).astype(jnp.int32)
-
-    count = lax.fori_loop(0, TOKENS, note, jnp.int32(0), unroll=32)
+        places[count] = local
+        count = count + ((local >= 0) & (local < window)).astype(jnp.int32)
 
     def copy(j, local):
         base = pl.multiple_of((local >> 7) << 7, LANES)
@@ -76,7 +73,7 @@
         )
 
     def begin(j, carry):
-        local = local_id(found[j])
+        local = places[j]
 
         @pl.when(local < tail_start)
         def _():
@@ -94,8 +91,7 @@
         cols[:FEAT] = jnp.where(lane == i, moved, cols[:FEAT])
 
     def end(j, carry):
-        i = found[j]
-        local = local_id(i)
+        i, local = found[j], places[j]
 
         @pl.when(local < tail_start)
         def _():
@@ -133,6 +129,7 @@
         scratch_shapes=[
             pltpu.VMEM((TOKENS, FEAT, LANES), bf16),
             pltpu.VMEM((WIDE, LANES), f32),
+            pltpu.SMEM((TOKENS,), jnp.int32),
             pltpu.SMEM((TOKENS,), jnp.int32),
             pltpu.SemaphoreType.DMA((TOKENS,)),
         ],

time: 96.9 us -> 96.3 us (level)
    all_to_all x1, starting transfers between devices: 5.11 us -> 3.62 us  [body(): rows = lax.all_to_all(rows, 'rep', 0, 0)]
    ppermute x1, starting transfers between devices: 1.24 us -> 2.21 us  [body(): other = lax.ppermute(own, 'rep', turn)]
where the time goes in v6:
time: 96.3 us; the launch traced here: 95.8 us
  blocking collectives  52.9 us (55%)
  starting transfers between devices  19.2 us (20%)
  Pallas kernels  14.7 us (15%)
  waiting for transfers between devices  5.09 us (5%)
  local copies, waits for them, and re-layouts  2.92 us (3%)
    all_to_all x1, blocking collectives, body(): lax.all_to_all(summed, ('rep', 'tp'), 0, 0, axis_index_groups=groups)  18.2 us
    all_to_all x1, blocking collectives, body(): lax.all_to_all(finish(partials, cosine, sine, embed_table.T, embed_table....  12.6 us
    all_to_all x1, blocking collectives, body(): parts = lax.all_to_all(attend(cache_len, projected, kv_cache), 'tp', 0, 0)  12.4 us
    all_to_all x1, blocking collectives, body(): heads = lax.all_to_all(merge(parts), 'tp', 0, 0)  9.63 us
    pallas_call x1, Pallas kernels, gather_rows(): pl.pallas_call(gather_kernel, grid=(1,), in_specs=[SMEM, pl.BlockSpec((FE...  6.46 us
    ppermute x1, starting transfers between devices, body(): other_qkv = lax.ppermute(new_qkv, 'rep', turn)  4.43 us
    pallas_call x1, Pallas kernels, attend(): pl.pallas_call(attend_kernel, grid=(ROWS,), in_specs=[SMEM, whole, VMEM],...  4.07 us
    all_to_all x1, starting transfers between devices, body(): rows = lax.all_to_all(rows, 'rep', 0, 0)  3.62 us
  transfers between devices with their start and end apart: 10, of which 2 were waited for; matrix products, arithmetic and copies ran while one was open for 1% of the time, Pallas kernels for 12%

profile of v6, /device:TPU:1, one launch (start us, length us, event | category | flops | bytes accessed | tf_op | source)
XLA Modules:
  0.0 95.8 jit_solution(5162895889102252655)
XLA Ops:
  0.0 4.4 %collective-permute-start = (bf16[40,7168]{1,0:T(8,128)(2,1)}, bf16[40,7168]{1,0:T(8,128)(2,1)S(1)}, u32[]{:S(2)}, u32[]{:S(2)}) collective-permute-start(bf16[40,7168]{1,0:T(8,128)(2,1)} %new_ref.1), channel_id=1, source_target_pairs={{0,16},{16,0},{32,48},{48,32},{64,80},{80,64},{96,112},{112,96},{1... | collective-permute-start | bytes 1720328 | tf_op jit(solution)/shard_map/ppermute | solution.py:472
  4.4 0.0 copy-start.5
  4.4 0.0 copy-start.2
  4.4 6.5 %gather_rows.1 = bf16[8,128,128]{2,1,0:T(8,128)(2,1)} custom-call(s32[4,32]{1,0:T(4,128)} %bitcast.18, bf16[320,9504]{1,0:T(8,128)(2,1)} %bitcast.14, bf16[320,9504]{1,0:T(8,128)(2,1)} %bitcast.15), custom_call_target="tpu_custom_call" | custom-call | tf_op jit(solution)/shard_map/gather_rows/pallas_call | solution.py:123
  10.9 0.0 copy-start.4
  10.9 3.6 %all-to-all-start = ((bf16[8,128,128]{2,1,0:T(8,128)(2,1)}), bf16[8,128,128]{2,1,0:T(8,128)(2,1)S(1)}, u32[]{:S(2)}, u32[]{:S(2)}) async-start(bf16[8,128,128]{2,1,0:T(8,128)(2,1)} %gather_rows.1), calls=%async_computation | async-start | bytes 524288 | tf_op jit(solution)/shard_map/all_to_all | solution.py:477
  14.5 0.0 copy-done.5
  14.5 0.0 copy-start
  14.6 2.3 %copy-done = bf16[320,7168]{1,0:T(8,128)(2,1)S(1)} copy-done((bf16[320,7168]{1,0:T(8,128)(2,1)S(1)}, bf16[320,7168]{1,0:T(8,128)(2,1)}, u32[]{:S(2)}) %copy-start) | copy-done | bytes 4587544
  16.8 0.0 copy-start.3
  16.9 0.1 take_old_columns.1.old
  17.0 0.0 copy-done.4
  17.0 0.6 dynamic_slice.3
  18.3 0.1 fusion
  18.4 0.1 pad_maximum_fusion
  18.5 3.3 %all-to-all-done.x_ref = bf16[8,128,128]{2,1,0:T(8,128)(2,1)S(1)} async-done(((bf16[8,128,128]{2,1,0:T(8,128)(2,1)}), bf16[8,128,128]{2,1,0:T(8,128)(2,1)S(1)}, u32[]{:S(2)}, u32[]{:S(2)}) %all-to-all-start) | async-done | bytes 262176 | tf_op jit(solution)/shard_map/all_to_all | solution.py:477
  21.8 0.0 collective-permute-done.other_ref
  21.8 0.0 copy-done.2
  21.8 0.8 project.1
  22.7 2.5 %collective-permute-start.1 = (f32[1280,128]{1,0:T(8,128)S(1)}, f32[1280,128]{1,0:T(8,128)S(1)}, u32[]{:S(2)}, u32[]{:S(2)}) collective-permute-start(f32[1280,128]{1,0:T(8,128)S(1)} %get-tuple-element.28), channel_id=1, source_target_pairs={{0,1},{1,0},{2,3},{3,2},{4,5},{5,4},{6,7},{7,6},{8,9},{9,8},{10,11... | collective-permute-start | bytes 1966088 | tf_op jit(solution)/shard_map/ppermute | solution.py:480
  25.1 1.7 %collective-permute-done.1.b_ref = f32[1280,128]{1,0:T(8,128)S(1)} collective-permute-done((f32[1280,128]{1,0:T(8,128)S(1)}, f32[1280,128]{1,0:T(8,128)S(1)}, u32[]{:S(2)}, u32[]{:S(2)}) %collective-permute-start.1) | collective-permute-done | bytes 655392 | tf_op jit(solution)/shard_map/ppermute | solution.py:480
  26.9 0.1 add.23
  26.9 18.2 %all_to_all.25.x_ref = f32[32,40,128]{2,1,0:T(8,128)S(1)} all-to-all(f32[32,40,128]{2,1,0:T(8,128)S(1)} %bitcast.9), channel_id=1, replica_groups={{0,2,4,6,8,10,12,14,32,34,36,38,40,42,44,46,64,66,68,70,72,74,76,78,96,..., dimensions={0} | all-to-all | bytes 1310720 | tf_op jit(solution)/shard_map/all_to_all | solution.py:487
  45.2 0.0 copy-done.3
  45.2 0.7 collective-permute-start.4
  45.9 0.8 collective-permute-start.3
  46.7 2.2 %collective-permute-start.2 = (bf16[40,5120]{1,0:T(8,128)(2,1)S(1)}, bf16[40,5120]{1,0:T(8,128)(2,1)S(1)}, u32[]{:S(2)}, u32[]{:S(2)}) collective-permute-start(bf16[40,5120]{1,0:T(8,128)(2,1)S(1)} %bitcast.12), channel_id=1, source_target_pairs={{0,16},{16,0},{32,48},{48,32},{64,80},{80,64},{96,112},{112,96},{1... | collective-permute-start | bytes 1228808 | tf_op jit(solution)/shard_map/ppermute | solution.py:489
  48.9 0.1 finish.1
  49.0 12.6 %all_to_all.26.q_ref = bf16[16,64,128]{2,1,0:T(8,128)(2,1)S(1)} all-to-all(bf16[16,64,128]{2,1,0:T(8,128)(2,1)S(1)} %finish.1), channel_id=1, replica_groups=mesh['rep'=8,'tp'=16] {'tp'}, dimensions={0} | all-to-all | bytes 524288 | tf_op jit(solution)/shard_map/all_to_all | solution.py:492
  61.7 0.0 collective-permute-done.4.refs_4_
  61.7 0.0 collective-permute-done.3.refs_8_
  61.7 0.0 collective-permute-done.2.refs_3_
  61.7 2.0 %collective-permute-start.5 = (bf16[40,5120]{1,0:T(8,128)(2,1)S(1)}, bf16[40,5120]{1,0:T(8,128)(2,1)S(1)}, u32[]{:S(2)}, u32[]{:S(2)}) collective-permute-start(bf16[40,5120]{1,0:T(8,128)(2,1)S(1)} %collective-permute-done.2.refs_3_), channel_id=1, source_target_pairs={{0,96},{16,112},{32,0},{48,16},{64,32},{80,48},{96,64},{112,80},{1... | collective-permute-start | bytes 1228808 | tf_op jit(solution)/shard_map/ppermute | solution.py:497
  63.7 0.0 collective-permute-start.6
  63.7 0.0 slice-done
  63.7 0.0 slice-done.1
  63.7 4.1 %attend.1 = bf16[16,64,128]{2,1,0:T(8,128)(2,1)S(1)} custom-call(s32[4]{0:T(128)S(1)} %copy-done.4, bf16[16,64,128]{2,1,0:T(8,128)(2,1)S(1)} %all_to_all.26.q_ref, bf16[4,512,2048]{2,1,0:T(8,128)(2,1)S(1)} %bitcast.7), custom_call_target="tpu_custom_call" | custom-call | tf_op jit(solution)/shard_map/attend/pallas_call | solution.py:370
  67.8 12.4 %all_to_all.27.x_ref = bf16[16,64,128]{2,1,0:T(8,128)(2,1)S(1)} all-to-all(bf16[16,64,128]{2,1,0:T(8,128)(2,1)S(1)} %attend.1), channel_id=1, replica_groups=mesh['rep'=8,'tp'=16] {'tp'}, dimensions={0} | all-to-all | bytes 524288 | tf_op jit(solution)/shard_map/all_to_all | solution.py:498
  80.2 0.0 collective-permute-done.5.refs_5_
  80.2 0.0 collective-permute-done.6.refs_6_
  80.2 0.0 collective-permute-start.8
  80.2 3.0 %collective-permute-start.7 = (bf16[40,5120]{1,0:T(8,128)(2,1)S(1)}, bf16[40,5120]{1,0:T(8,128)(2,1)S(1)}, u32[]{:S(2)}, u32[]{:S(2)}) collective-permute-start(bf16[40,5120]{1,0:T(8,128)(2,1)S(1)} %collective-permute-done.5.refs_5_), channel_id=1, source_target_pairs={{0,96},{16,112},{32,0},{48,16},{64,32},{80,48},{96,64},{112,80},{1... | collective-permute-start | bytes 1228808 | tf_op jit(solution)/shard_map/ppermute | solution.py:502
  83.2 0.4 merge.1
  83.5 9.6 %all_to_all.28.refs_0_ = bf16[16,40,128]{2,1,0:T(8,128)(2,1)S(1)} all-to-all(bf16[16,40,128]{2,1,0:T(8,128)(2,1)S(1)} %merge.1), channel_id=1, replica_groups=mesh['rep'=8,'tp'=16] {'tp'}, dimensions={0} | all-to-all | bytes 327680 | tf_op jit(solution)/shard_map/all_to_all | solution.py:504
  93.2 0.0 collective-permute-done.8.refs_9_
  93.2 0.0 collective-permute-done.7.refs_7_
  93.2 0.0 copy-done.1
  93.2 2.7 %output.1 = bf16[4,4,320]{2,1,0:T(4,128)(2,1)} custom-call(bf16[16,40,128]{2,1,0:T(8,128)(2,1)S(1)} %all_to_all.28.refs_0_, bf16[320,5120]{1,0:T(8,128)(2,1)S(1)} %bitcast.8, bf16[40,5120]{1,0:T(8,128)(2,1)S(1)} %bitcast.13, bf16[40,5120]{1,0:T(8,128)(2,1)S(1)} %collective-permute-done.2.refs_3_, bf16[40,5120]{1,0:T(8,128)(2,1)S(1)} %collective-permute-done.4.refs_4_, ...), custom_call_target="tpu_custom_call" | custom-call | tf_op jit(solution)/shard_map/output/pallas_call | solution.py:438
  (7 shorter events, 0.0 us)
Async XLA Ops:
  0.0 21.8 %collective-permute-start = (bf16[40,7168]{1,0:T(8,128)(2,1)}, bf16[40,7168]{1,0:T(8,128)(2,1)S(1)}, u32[]{:S(2)}, u32[]{:S(2)}) collective-permute-start(bf16[40,7168]{1,0:T(8,128)(2,1)} %new_ref.1), channel_id=1, source_target_pairs={{0,16},{16,0},{32,48},{48,32},{64,80},{80,64},{96,112},{112,96},{1... | collective-permute-start | bytes 1720328 | tf_op jit(solution)/shard_map/ppermute | solution.py:472
  4.4 10.1 %copy-start.5 = (bf16[320]{0:T(512)(128)(2,1)S(1)}, bf16[320]{0:T(512)(128)(2,1)}, u32[]{:S(2)}) copy-start(bf16[320]{0:T(512)(128)(2,1)} %param.12) | copy-start | bytes 1924
  4.4 17.4 %copy-start.2 = (bf16[40,7168]{1,0:T(8,128)(2,1)S(1)}, bf16[40,7168]{1,0:T(8,128)(2,1)}, u32[]{:S(2)}) copy-start(bf16[40,7168]{1,0:T(8,128)(2,1)} %new_ref.1) | copy-start | bytes 1720324
  10.9 6.1 %copy-start.4 = (s32[4]{0:T(128)S(1)}, s32[4]{0:T(128)}, u32[]{:S(2)}) copy-start(s32[4]{0:T(128)} %len_ref.1) | copy-start | bytes 52
  10.9 10.9 %all-to-all-start = ((bf16[8,128,128]{2,1,0:T(8,128)(2,1)}), bf16[8,128,128]{2,1,0:T(8,128)(2,1)S(1)}, u32[]{:S(2)}, u32[]{:S(2)}) async-start(bf16[8,128,128]{2,1,0:T(8,128)(2,1)} %gather_rows.1), calls=%async_computation | async-start | bytes 524288 | tf_op jit(solution)/shard_map/all_to_all | solution.py:477
  14.5 2.3 %copy-start = (bf16[320,7168]{1,0:T(8,128)(2,1)S(1)}, bf16[320,7168]{1,0:T(8,128)(2,1)}, u32[]{:S(2)}) copy-start(bf16[320,7168]{1,0:T(8,128)(2,1)} %refs_2_) | copy-start | bytes 13762564
  16.8 28.3 %copy-start.3 = (bf16[5120,40]{0,1:T(8,128)(2,1)S(1)}, bf16[5120,40]{0,1:T(8,128)(2,1)}, u32[]{:S(2)}) copy-start(bf16[5120,40]{0,1:T(8,128)(2,1)} %param.16) | copy-start | bytes 1228804
  22.7 4.2 %collective-permute-start.1 = (f32[1280,128]{1,0:T(8,128)S(1)}, f32[1280,128]{1,0:T(8,128)S(1)}, u32[]{:S(2)}, u32[]{:S(2)}) collective-permute-start(f32[1280,128]{1,0:T(8,128)S(1)} %get-tuple-element.28), channel_id=1, source_target_pairs={{0,1},{1,0},{2,3},{3,2},{4,5},{5,4},{6,7},{7,6},{8,9},{9,8},{10,11... | collective-permute-start | bytes 1966088 | tf_op jit(solution)/shard_map/ppermute | solution.py:480
  45.2 18.5 %slice-start = ((s8[8388608]{0:T(1024)(128)(4,1)}), s8[4194304]{0:T(1024)(128)(4,1)S(1)}, s32[]{:S(2)}) async-start(s8[8388608]{0:T(1024)(128)(4,1)} %bitcast.6), calls=%async_computation.5 | async-start | bytes 8388608
  45.2 18.5 %slice-start.1 = ((s8[8388608]{0:T(1024)(128)(4,1)}), s8[4194304]{0:T(1024)(128)(4,1)S(1)}, s32[]{:S(2)}) async-start(s8[8388608]{0:T(1024)(128)(4,1)} %bitcast.6), calls=%async_computation.6 | async-start | bytes 8388608
  45.2 16.5 %collective-permute-start.4 = (bf16[40,5120]{1,0:T(8,128)(2,1)S(1)}, bf16[40,5120]{1,0:T(8,128)(2,1)S(1)}, u32[]{:S(2)}, u32[]{:S(2)}) collective-permute-start(bf16[40,5120]{1,0:T(8,128)(2,1)S(1)} %bitcast.10), channel_id=1, source_target_pairs={{0,96},{16,112},{32,0},{48,16},{64,32},{80,48},{96,64},{112,80},{1... | collective-permute-start | bytes 1228808 | tf_op jit(solution)/shard_map/ppermute | solution.py:491
  45.9 15.8 %collective-permute-start.3 = (bf16[40,5120]{1,0:T(8,128)(2,1)S(1)}, bf16[40,5120]{1,0:T(8,128)(2,1)S(1)}, u32[]{:S(2)}, u32[]{:S(2)}) collective-permute-start(bf16[40,5120]{1,0:T(8,128)(2,1)S(1)} %bitcast.11), channel_id=1, source_target_pairs={{0,32},{16,48},{32,64},{48,80},{64,96},{80,112},{96,0},{112,16},{1... | collective-permute-start | bytes 1228808 | tf_op jit(solution)/shard_map/ppermute | solution.py:490
  46.7 15.0 %collective-permute-start.2 = (bf16[40,5120]{1,0:T(8,128)(2,1)S(1)}, bf16[40,5120]{1,0:T(8,128)(2,1)S(1)}, u32[]{:S(2)}, u32[]{:S(2)}) collective-permute-start(bf16[40,5120]{1,0:T(8,128)(2,1)S(1)} %bitcast.12), channel_id=1, source_target_pairs={{0,16},{16,0},{32,48},{48,32},{64,80},{80,64},{96,112},{112,96},{1... | collective-permute-start | bytes 1228808 | tf_op jit(solution)/shard_map/ppermute | solution.py:489
  61.7 31.5 %copy-start.1 = (bf16[5120,320]{0,1:T(8,128)(2,1)S(1)}, bf16[5120,320]{0,1:T(8,128)(2,1)}, u32[]{:S(2)}) copy-start(bf16[5120,320]{0,1:T(8,128)(2,1)} %param.14) | copy-start | bytes 9830404
  61.7 18.5 %collective-permute-start.5 = (bf16[40,5120]{1,0:T(8,128)(2,1)S(1)}, bf16[40,5120]{1,0:T(8,128)(2,1)S(1)}, u32[]{:S(2)}, u32[]{:S(2)}) collective-permute-start(bf16[40,5120]{1,0:T(8,128)(2,1)S(1)} %collective-permute-done.2.refs_3_), channel_id=1, source_target_pairs={{0,96},{16,112},{32,0},{48,16},{64,32},{80,48},{96,64},{112,80},{1... | collective-permute-start | bytes 1228808 | tf_op jit(solution)/shard_map/ppermute | solution.py:497
  63.7 16.5 %collective-permute-start.6 = (bf16[40,5120]{1,0:T(8,128)(2,1)S(1)}, bf16[40,5120]{1,0:T(8,128)(2,1)S(1)}, u32[]{:S(2)}, u32[]{:S(2)}) collective-permute-start(bf16[40,5120]{1,0:T(8,128)(2,1)S(1)} %collective-permute-done.3.refs_8_), channel_id=1, source_target_pairs={{0,32},{16,48},{32,64},{48,80},{64,96},{80,112},{96,0},{112,16},{1... | collective-permute-start | bytes 1228808 | tf_op jit(solution)/shard_map/ppermute | solution.py:496
  80.2 13.0 %collective-permute-start.8 = (bf16[40,5120]{1,0:T(8,128)(2,1)S(1)}, bf16[40,5120]{1,0:T(8,128)(2,1)S(1)}, u32[]{:S(2)}, u32[]{:S(2)}) collective-permute-start(bf16[40,5120]{1,0:T(8,128)(2,1)S(1)} %collective-permute-done.2.refs_3_), channel_id=1, source_target_pairs={{0,32},{16,48},{32,64},{48,80},{64,96},{80,112},{96,0},{112,16},{1... | collective-permute-start | bytes 1228808 | tf_op jit(solution)/shard_map/ppermute | solution.py:503
  80.2 13.0 %collective-permute-start.7 = (bf16[40,5120]{1,0:T(8,128)(2,1)S(1)}, bf16[40,5120]{1,0:T(8,128)(2,1)S(1)}, u32[]{:S(2)}, u32[]{:S(2)}) collective-permute-start(bf16[40,5120]{1,0:T(8,128)(2,1)S(1)} %collective-permute-done.5.refs_5_), channel_id=1, source_target_pairs={{0,96},{16,112},{32,0},{48,16},{64,32},{80,48},{96,64},{112,80},{1... | collective-permute-start | bytes 1228808 | tf_op jit(solution)/shard_map/ppermute | solution.py:502

commit v7 on v6

--- a/solution.py
+++ b/solution.py
@@ -336,13 +336,16 @@
         weights_new.astype(f32), axis=1, keepdims=True
     )
     numerator = []
-    for h in range(KV_HEADS):
-        columns = slice(value_at + h * HEAD_DIM, value_at + (h + 1) * HEAD_DIM)
-        rows = slice(h * count, (h + 1) * count)
-        numerator.append(
-            jnp.dot(weights_ref[rows, :], kv_ref[row, :, columns], preferred_element_type=f32)
-            + jnp.dot(weights_new[rows], shifted[h], preferred_element_type=f32)
-        )
+    for h in range(0, KV_HEADS, 2):
+        columns = slice(value_at + h * HEAD_DIM, value_at + (h + 2) * HEAD_DIM)
+        rows = slice(h * count, (h + 2) * count)
+        both = jnp.dot(weights_ref[rows, :], kv_ref[row, :, columns], preferred_element_type=f32)
+        for n in range(2):
+            at = slice((h + n) * count, (h + n + 1) * count)
+            numerator.append(
+                both[n * count : (n + 1) * count, n * LANES : (n + 1) * LANES]
+                + jnp.dot(weights_new[at], shifted[h + n], preferred_element_type=f32)
+            )
     grouped = (KV_HEADS, STEPS, SLOTS, LANES)
     part = (jnp.concatenate(numerator, axis=0) / total).reshape(grouped)
     slot = lax.broadcasted_iota(jnp.int32, grouped, 2)

time: 96.3 us -> 95.7 us (level)
  Pallas kernels: 14.7 us -> 13.3 us
  starting transfers between devices: 19.2 us -> 20.2 us
    all_to_all x1, starting transfers between devices: 3.62 us -> 5.16 us  [body(): rows = lax.all_to_all(rows, 'rep', 0, 0)]
  transfers between devices with their start and end apart: 10 -> 10, of which waited for: 2 -> 2; matrix products, arithmetic and copies ran while one was open for 1% -> 1% of each run, Pallas kernels for 12% -> 10%
where the time goes in v7:
time: 95.7 us; the launch traced here: 95.3 us
  blocking collectives  52.7 us (55%)
  starting transfers between devices  20.2 us (21%)
  Pallas kernels  13.3 us (14%)
  waiting for transfers between devices  5.09 us (5%)
  local copies, waits for them, and re-layouts  2.92 us (3%)
    all_to_all x1, blocking collectives, body(): lax.all_to_all(summed, ('rep', 'tp'), 0, 0, axis_index_groups=groups)  18.2 us
    all_to_all x1, blocking collectives, body(): lax.all_to_all(finish(partials, cosine, sine, embed_table.T, embed_table....  12.6 us
    all_to_all x1, blocking collectives, body(): parts = lax.all_to_all(attend(cache_len, projected, kv_cache), 'tp', 0, 0)  12.3 us
    all_to_all x1, blocking collectives, body(): heads = lax.all_to_all(merge(parts), 'tp', 0, 0)  9.63 us
    pallas_call x1, Pallas kernels, gather_rows(): pl.pallas_call(gather_kernel, grid=(1,), in_specs=[SMEM, pl.BlockSpec((FE...  5.64 us
    all_to_all x1, starting transfers between devices, body(): rows = lax.all_to_all(rows, 'rep', 0, 0)  5.16 us
    ppermute x1, starting transfers between devices, body(): other_qkv = lax.ppermute(new_qkv, 'rep', turn)  4.43 us
    pallas_call x1, Pallas kernels, attend(): pl.pallas_call(attend_kernel, grid=(ROWS,), in_specs=[SMEM, whole, VMEM],...  3.49 us
  transfers between devices with their start and end apart: 10, of which 2 were waited for; matrix products, arithmetic and copies ran while one was open for 1% of the time, Pallas kernels for 10%

profile of v7, /device:TPU:1, one launch (start us, length us, event | category | flops | bytes accessed | tf_op | source)
XLA Modules:
  0.0 95.3 jit_solution(9692973539241977139)
XLA Ops:
  0.0 4.4 %collective-permute-start = (bf16[40,7168]{1,0:T(8,128)(2,1)}, bf16[40,7168]{1,0:T(8,128)(2,1)S(1)}, u32[]{:S(2)}, u32[]{:S(2)}) collective-permute-start(bf16[40,7168]{1,0:T(8,128)(2,1)} %new_ref.1), channel_id=1, source_target_pairs={{0,16},{16,0},{32,48},{48,32},{64,80},{80,64},{96,112},{112,96},{1... | collective-permute-start | bytes 1720328 | tf_op jit(solution)/shard_map/ppermute | solution.py:475
  4.4 0.0 copy-start.5
  4.4 0.0 copy-start.2
  4.4 5.6 %gather_rows.1 = bf16[8,128,128]{2,1,0:T(8,128)(2,1)} custom-call(s32[4,32]{1,0:T(4,128)} %bitcast.18, bf16[320,9504]{1,0:T(8,128)(2,1)} %bitcast.14, bf16[320,9504]{1,0:T(8,128)(2,1)} %bitcast.15), custom_call_target="tpu_custom_call" | custom-call | tf_op jit(solution)/shard_map/gather_rows/pallas_call | solution.py:123
  10.1 0.0 copy-start.4
  10.1 5.2 %all-to-all-start = ((bf16[8,128,128]{2,1,0:T(8,128)(2,1)}), bf16[8,128,128]{2,1,0:T(8,128)(2,1)S(1)}, u32[]{:S(2)}, u32[]{:S(2)}) async-start(bf16[8,128,128]{2,1,0:T(8,128)(2,1)} %gather_rows.1), calls=%async_computation | async-start | bytes 524288 | tf_op jit(solution)/shard_map/all_to_all | solution.py:480
  15.3 0.0 copy-done.5
  15.3 0.0 copy-start
  15.3 2.3 %copy-done = bf16[320,7168]{1,0:T(8,128)(2,1)S(1)} copy-done((bf16[320,7168]{1,0:T(8,128)(2,1)S(1)}, bf16[320,7168]{1,0:T(8,128)(2,1)}, u32[]{:S(2)}) %copy-start) | copy-done | bytes 4587544
  17.6 0.0 copy-start.3
  17.6 0.1 take_old_columns.1.old
  17.7 0.0 copy-done.4
  17.7 0.6 dynamic_slice.3
  19.0 0.1 fusion
  19.1 0.1 pad_maximum_fusion
  19.2 3.3 %all-to-all-done.x_ref = bf16[8,128,128]{2,1,0:T(8,128)(2,1)S(1)} async-done(((bf16[8,128,128]{2,1,0:T(8,128)(2,1)}), bf16[8,128,128]{2,1,0:T(8,128)(2,1)S(1)}, u32[]{:S(2)}, u32[]{:S(2)}) %all-to-all-start) | async-done | bytes 262176 | tf_op jit(solution)/shard_map/all_to_all | solution.py:480
  22.5 0.0 collective-permute-done.other_ref
  22.5 0.0 copy-done.2
  22.5 0.8 project.1
  23.4 2.5 %collective-permute-start.1 = (f32[1280,128]{1,0:T(8,128)S(1)}, f32[1280,128]{1,0:T(8,128)S(1)}, u32[]{:S(2)}, u32[]{:S(2)}) collective-permute-start(f32[1280,128]{1,0:T(8,128)S(1)} %get-tuple-element.28), channel_id=1, source_target_pairs={{0,1},{1,0},{2,3},{3,2},{4,5},{5,4},{6,7},{7,6},{8,9},{9,8},{10,11... | collective-permute-start | bytes 1966088 | tf_op jit(solution)/shard_map/ppermute | solution.py:483
  25.9 1.7 %collective-permute-done.1.b_ref = f32[1280,128]{1,0:T(8,128)S(1)} collective-permute-done((f32[1280,128]{1,0:T(8,128)S(1)}, f32[1280,128]{1,0:T(8,128)S(1)}, u32[]{:S(2)}, u32[]{:S(2)}) %collective-permute-start.1) | collective-permute-done | bytes 655392 | tf_op jit(solution)/shard_map/ppermute | solution.py:483
  27.6 0.1 add.23
  27.7 18.2 %all_to_all.25.x_ref = f32[32,40,128]{2,1,0:T(8,128)S(1)} all-to-all(f32[32,40,128]{2,1,0:T(8,128)S(1)} %bitcast.9), channel_id=1, replica_groups={{0,2,4,6,8,10,12,14,32,34,36,38,40,42,44,46,64,66,68,70,72,74,76,78,96,..., dimensions={0} | all-to-all | bytes 1310720 | tf_op jit(solution)/shard_map/all_to_all | solution.py:490
  45.8 0.0 copy-done.3
  45.8 0.7 collective-permute-start.4
  46.5 0.8 collective-permute-start.3
  47.3 1.6 %collective-permute-start.2 = (bf16[40,5120]{1,0:T(8,128)(2,1)S(1)}, bf16[40,5120]{1,0:T(8,128)(2,1)S(1)}, u32[]{:S(2)}, u32[]{:S(2)}) collective-permute-start(bf16[40,5120]{1,0:T(8,128)(2,1)S(1)} %bitcast.12), channel_id=1, source_target_pairs={{0,16},{16,0},{32,48},{48,32},{64,80},{80,64},{96,112},{112,96},{1... | collective-permute-start | bytes 1228808 | tf_op jit(solution)/shard_map/ppermute | solution.py:492
  48.9 0.1 finish.1
  49.0 12.6 %all_to_all.26.q_ref = bf16[16,64,128]{2,1,0:T(8,128)(2,1)S(1)} all-to-all(bf16[16,64,128]{2,1,0:T(8,128)(2,1)S(1)} %finish.1), channel_id=1, replica_groups=mesh['rep'=8,'tp'=16] {'tp'}, dimensions={0} | all-to-all | bytes 524288 | tf_op jit(solution)/shard_map/all_to_all | solution.py:495
  61.7 0.0 collective-permute-done.4.refs_4_
  61.7 0.0 collective-permute-done.3.refs_8_
  61.7 0.0 collective-permute-done.2.refs_3_
  61.7 2.1 %collective-permute-start.5 = (bf16[40,5120]{1,0:T(8,128)(2,1)S(1)}, bf16[40,5120]{1,0:T(8,128)(2,1)S(1)}, u32[]{:S(2)}, u32[]{:S(2)}) collective-permute-start(bf16[40,5120]{1,0:T(8,128)(2,1)S(1)} %collective-permute-done.2.refs_3_), channel_id=1, source_target_pairs={{0,96},{16,112},{32,0},{48,16},{64,32},{80,48},{96,64},{112,80},{1... | collective-permute-start | bytes 1228808 | tf_op jit(solution)/shard_map/ppermute | solution.py:500
  63.8 0.0 collective-permute-start.6
  63.8 0.0 slice-done
  63.8 0.0 slice-done.1
  63.8 3.5 %attend.1 = bf16[16,64,128]{2,1,0:T(8,128)(2,1)S(1)} custom-call(s32[4]{0:T(128)S(1)} %copy-done.4, bf16[16,64,128]{2,1,0:T(8,128)(2,1)S(1)} %all_to_all.26.q_ref, bf16[4,512,2048]{2,1,0:T(8,128)(2,1)S(1)} %bitcast.7), custom_call_target="tpu_custom_call" | custom-call | tf_op jit(solution)/shard_map/attend/pallas_call | solution.py:373
  67.3 12.3 %all_to_all.27.x_ref = bf16[16,64,128]{2,1,0:T(8,128)(2,1)S(1)} all-to-all(bf16[16,64,128]{2,1,0:T(8,128)(2,1)S(1)} %attend.1), channel_id=1, replica_groups=mesh['rep'=8,'tp'=16] {'tp'}, dimensions={0} | all-to-all | bytes 524288 | tf_op jit(solution)/shard_map/all_to_all | solution.py:501
  79.6 0.0 collective-permute-done.5.refs_5_
  79.6 0.0 collective-permute-done.6.refs_6_
  79.6 0.0 collective-permute-start.8
  79.6 3.0 %collective-permute-start.7 = (bf16[40,5120]{1,0:T(8,128)(2,1)S(1)}, bf16[40,5120]{1,0:T(8,128)(2,1)S(1)}, u32[]{:S(2)}, u32[]{:S(2)}) collective-permute-start(bf16[40,5120]{1,0:T(8,128)(2,1)S(1)} %collective-permute-done.5.refs_5_), channel_id=1, source_target_pairs={{0,96},{16,112},{32,0},{48,16},{64,32},{80,48},{96,64},{112,80},{1... | collective-permute-start | bytes 1228808 | tf_op jit(solution)/shard_map/ppermute | solution.py:505
  82.6 0.4 merge.1
  83.0 9.6 %all_to_all.28.refs_0_ = bf16[16,40,128]{2,1,0:T(8,128)(2,1)S(1)} all-to-all(bf16[16,40,128]{2,1,0:T(8,128)(2,1)S(1)} %merge.1), channel_id=1, replica_groups=mesh['rep'=8,'tp'=16] {'tp'}, dimensions={0} | all-to-all | bytes 327680 | tf_op jit(solution)/shard_map/all_to_all | solution.py:507
  92.6 0.0 collective-permute-done.8.refs_9_
  92.6 0.0 collective-permute-done.7.refs_7_
  92.6 0.0 copy-done.1
  92.6 2.7 %output.1 = bf16[4,4,320]{2,1,0:T(4,128)(2,1)} custom-call(bf16[16,40,128]{2,1,0:T(8,128)(2,1)S(1)} %all_to_all.28.refs_0_, bf16[320,5120]{1,0:T(8,128)(2,1)S(1)} %bitcast.8, bf16[40,5120]{1,0:T(8,128)(2,1)S(1)} %bitcast.13, bf16[40,5120]{1,0:T(8,128)(2,1)S(1)} %collective-permute-done.2.refs_3_, bf16[40,5120]{1,0:T(8,128)(2,1)S(1)} %collective-permute-done.4.refs_4_, ...), custom_call_target="tpu_custom_call" | custom-call | tf_op jit(solution)/shard_map/output/pallas_call | solution.py:441
  (7 shorter events, 0.0 us)
Async XLA Ops:
  0.0 22.5 %collective-permute-start = (bf16[40,7168]{1,0:T(8,128)(2,1)}, bf16[40,7168]{1,0:T(8,128)(2,1)S(1)}, u32[]{:S(2)}, u32[]{:S(2)}) collective-permute-start(bf16[40,7168]{1,0:T(8,128)(2,1)} %new_ref.1), channel_id=1, source_target_pairs={{0,16},{16,0},{32,48},{48,32},{64,80},{80,64},{96,112},{112,96},{1... | collective-permute-start | bytes 1720328 | tf_op jit(solution)/shard_map/ppermute | solution.py:475
  4.4 10.8 %copy-start.5 = (bf16[320]{0:T(512)(128)(2,1)S(1)}, bf16[320]{0:T(512)(128)(2,1)}, u32[]{:S(2)}) copy-start(bf16[320]{0:T(512)(128)(2,1)} %param.12) | copy-start | bytes 1924
  4.4 18.1 %copy-start.2 = (bf16[40,7168]{1,0:T(8,128)(2,1)S(1)}, bf16[40,7168]{1,0:T(8,128)(2,1)}, u32[]{:S(2)}) copy-start(bf16[40,7168]{1,0:T(8,128)(2,1)} %new_ref.1) | copy-start | bytes 1720324
  10.1 7.6 %copy-start.4 = (s32[4]{0:T(128)S(1)}, s32[4]{0:T(128)}, u32[]{:S(2)}) copy-start(s32[4]{0:T(128)} %len_ref.1) | copy-start | bytes 52
  10.1 12.4 %all-to-all-start = ((bf16[8,128,128]{2,1,0:T(8,128)(2,1)}), bf16[8,128,128]{2,1,0:T(8,128)(2,1)S(1)}, u32[]{:S(2)}, u32[]{:S(2)}) async-start(bf16[8,128,128]{2,1,0:T(8,128)(2,1)} %gather_rows.1), calls=%async_computation | async-start | bytes 524288 | tf_op jit(solution)/shard_map/all_to_all | solution.py:480
  15.3 2.3 %copy-start = (bf16[320,7168]{1,0:T(8,128)(2,1)S(1)}, bf16[320,7168]{1,0:T(8,128)(2,1)}, u32[]{:S(2)}) copy-start(bf16[320,7168]{1,0:T(8,128)(2,1)} %refs_2_) | copy-start | bytes 13762564
  17.6 28.3 %copy-start.3 = (bf16[5120,40]{0,1:T(8,128)(2,1)S(1)}, bf16[5120,40]{0,1:T(8,128)(2,1)}, u32[]{:S(2)}) copy-start(bf16[5120,40]{0,1:T(8,128)(2,1)} %param.16) | copy-start | bytes 1228804
  23.4 4.2 %collective-permute-start.1 = (f32[1280,128]{1,0:T(8,128)S(1)}, f32[1280,128]{1,0:T(8,128)S(1)}, u32[]{:S(2)}, u32[]{:S(2)}) collective-permute-start(f32[1280,128]{1,0:T(8,128)S(1)} %get-tuple-element.28), channel_id=1, source_target_pairs={{0,1},{1,0},{2,3},{3,2},{4,5},{5,4},{6,7},{7,6},{8,9},{9,8},{10,11... | collective-permute-start | bytes 1966088 | tf_op jit(solution)/shard_map/ppermute | solution.py:483
  45.8 18.0 %slice-start = ((s8[8388608]{0:T(1024)(128)(4,1)}), s8[4194304]{0:T(1024)(128)(4,1)S(1)}, s32[]{:S(2)}) async-start(s8[8388608]{0:T(1024)(128)(4,1)} %bitcast.6), calls=%async_computation.5 | async-start | bytes 8388608
  45.8 18.0 %slice-start.1 = ((s8[8388608]{0:T(1024)(128)(4,1)}), s8[4194304]{0:T(1024)(128)(4,1)S(1)}, s32[]{:S(2)}) async-start(s8[8388608]{0:T(1024)(128)(4,1)} %bitcast.6), calls=%async_computation.6 | async-start | bytes 8388608
  45.8 15.8 %collective-permute-start.4 = (bf16[40,5120]{1,0:T(8,128)(2,1)S(1)}, bf16[40,5120]{1,0:T(8,128)(2,1)S(1)}, u32[]{:S(2)}, u32[]{:S(2)}) collective-permute-start(bf16[40,5120]{1,0:T(8,128)(2,1)S(1)} %bitcast.10), channel_id=1, source_target_pairs={{0,96},{16,112},{32,0},{48,16},{64,32},{80,48},{96,64},{112,80},{1... | collective-permute-start | bytes 1228808 | tf_op jit(solution)/shard_map/ppermute | solution.py:494
  46.5 15.1 %collective-permute-start.3 = (bf16[40,5120]{1,0:T(8,128)(2,1)S(1)}, bf16[40,5120]{1,0:T(8,128)(2,1)S(1)}, u32[]{:S(2)}, u32[]{:S(2)}) collective-permute-start(bf16[40,5120]{1,0:T(8,128)(2,1)S(1)} %bitcast.11), channel_id=1, source_target_pairs={{0,32},{16,48},{32,64},{48,80},{64,96},{80,112},{96,0},{112,16},{1... | collective-permute-start | bytes 1228808 | tf_op jit(solution)/shard_map/ppermute | solution.py:493
  47.3 14.4 %collective-permute-start.2 = (bf16[40,5120]{1,0:T(8,128)(2,1)S(1)}, bf16[40,5120]{1,0:T(8,128)(2,1)S(1)}, u32[]{:S(2)}, u32[]{:S(2)}) collective-permute-start(bf16[40,5120]{1,0:T(8,128)(2,1)S(1)} %bitcast.12), channel_id=1, source_target_pairs={{0,16},{16,0},{32,48},{48,32},{64,80},{80,64},{96,112},{112,96},{1... | collective-permute-start | bytes 1228808 | tf_op jit(solution)/shard_map/ppermute | solution.py:492
  61.7 30.9 %copy-start.1 = (bf16[5120,320]{0,1:T(8,128)(2,1)S(1)}, bf16[5120,320]{0,1:T(8,128)(2,1)}, u32[]{:S(2)}) copy-start(bf16[5120,320]{0,1:T(8,128)(2,1)} %param.14) | copy-start | bytes 9830404
  61.7 17.9 %collective-permute-start.5 = (bf16[40,5120]{1,0:T(8,128)(2,1)S(1)}, bf16[40,5120]{1,0:T(8,128)(2,1)S(1)}, u32[]{:S(2)}, u32[]{:S(2)}) collective-permute-start(bf16[40,5120]{1,0:T(8,128)(2,1)S(1)} %collective-permute-done.2.refs_3_), channel_id=1, source_target_pairs={{0,96},{16,112},{32,0},{48,16},{64,32},{80,48},{96,64},{112,80},{1... | collective-permute-start | bytes 1228808 | tf_op jit(solution)/shard_map/ppermute | solution.py:500
  63.8 15.8 %collective-permute-start.6 = (bf16[40,5120]{1,0:T(8,128)(2,1)S(1)}, bf16[40,5120]{1,0:T(8,128)(2,1)S(1)}, u32[]{:S(2)}, u32[]{:S(2)}) collective-permute-start(bf16[40,5120]{1,0:T(8,128)(2,1)S(1)} %collective-permute-done.3.refs_8_), channel_id=1, source_target_pairs={{0,32},{16,48},{32,64},{48,80},{64,96},{80,112},{96,0},{112,16},{1... | collective-permute-start | bytes 1228808 | tf_op jit(solution)/shard_map/ppermute | solution.py:499
  79.6 13.0 %collective-permute-start.8 = (bf16[40,5120]{1,0:T(8,128)(2,1)S(1)}, bf16[40,5120]{1,0:T(8,128)(2,1)S(1)}, u32[]{:S(2)}, u32[]{:S(2)}) collective-permute-start(bf16[40,5120]{1,0:T(8,128)(2,1)S(1)} %collective-permute-done.2.refs_3_), channel_id=1, source_target_pairs={{0,32},{16,48},{32,64},{48,80},{64,96},{80,112},{96,0},{112,16},{1... | collective-permute-start | bytes 1228808 | tf_op jit(solution)/shard_map/ppermute | solution.py:506
  79.6 13.0 %collective-permute-start.7 = (bf16[40,5120]{1,0:T(8,128)(2,1)S(1)}, bf16[40,5120]{1,0:T(8,128)(2,1)S(1)}, u32[]{:S(2)}, u32[]{:S(2)}) collective-permute-start(bf16[40,5120]{1,0:T(8,128)(2,1)S(1)} %collective-permute-done.5.refs_5_), channel_id=1, source_target_pairs={{0,96},{16,112},{32,0},{48,16},{64,32},{80,48},{96,64},{112,80},{1... | collective-permute-start | bytes 1228808 | tf_op jit(solution)/shard_map/ppermute | solution.py:505

commit v8 on v7

--- a/solution.py
+++ b/solution.py
@@ -177,7 +177,7 @@
     )(old_qkv)
 
 
-def project_kernel(x_ref, gain_ref, new_ref, other_ref, old, keep_ref, send_ref):
+def project_kernel(own, x_ref, gain_ref, new_ref, other_ref, old, out_ref):
     rep, core = lax.axis_index("rep"), lax.axis_index("tp") & 1
     xx, zh = rep >> 1, rep & 1
     embedded = jnp.sum(x_ref[...].astype(f32), axis=0)
@@ -202,7 +202,7 @@
     def put(out_ref, group, slot, value):
         out_ref[pl.ds(group * SLOTS + slot, DESTS, stride=SUMS), :] = value
 
-    for out_ref, side in ((keep_ref, core), (send_ref, 1 - core)):
+    for side in (core if own else 1 - core,):
         for j in range(PER_CORE):
             head = j * 2 + side
             starts = (
@@ -222,20 +222,18 @@
     for slot in range(USED):
         at = (slot, slot + GROUP) if slot < GROUP else (slot * 2, slot * 2 + 1)
         both = [sums[:, a * HEAD_DIM : (a + 1) * HEAD_DIM] for a in at]
-        put(keep_ref, PER_CORE, slot, jnp.where(core == 0, both[0], both[1]))
-        put(send_ref, PER_CORE, slot, jnp.where(core == 0, both[1], both[0]))
-    for out_ref in (keep_ref, send_ref):
-        put(out_ref, PER_CORE, SLOTS - 1, squares[1])
-
-
-def project(received, norm_gain, new_qkv, other_qkv, old_columns):
-    out = jax.ShapeDtypeStruct((DESTS * SUMS, LANES), f32)
-    return pl.pallas_call(
-        project_kernel,
+        put(out_ref, PER_CORE, slot, jnp.where(core == (0 if own else 1), both[0], both[1]))
+    put(out_ref, PER_CORE, SLOTS - 1, squares[1])
+
+
+def project(own, received, norm_gain, new_qkv, other_qkv, old_columns):
+    return pl.pallas_call(
+        functools.partial(project_kernel, own),
         in_specs=[VMEM] * 5,
-        out_specs=[VMEM, VMEM],
-        out_shape=[out, out],
+        out_specs=VMEM,
+        out_shape=jax.ShapeDtypeStruct((DESTS * SUMS, LANES), f32),
         compiler_params=params(16),
+        cost_estimate=pl.CostEstimate(flops=0, bytes_accessed=4 * MIB, transcendentals=0),
         name="project",
     )(received, norm_gain.reshape(1, FEAT), new_qkv, other_qkv, old_columns)
 
@@ -479,7 +477,9 @@
     old_columns = take_old_columns(old_qkv)
     rows = lax.all_to_all(rows, "rep", 0, 0)
     rows, old_columns, cosine, sine = lax.optimization_barrier((rows, old_columns, cosine, sine))
-    keep, send = project(rows, norm_gain, new_qkv, other_qkv, old_columns)
+    send, keep = (
+        project(own, rows, norm_gain, new_qkv, other_qkv, old_columns) for own in (False, True)
+    )
     arrived = lax.ppermute(send, "tp", [(t, t ^ 1) for t in range(N_TP)])
     summed = add(keep, arrived).reshape(DESTS, SUMS, LANES)
     groups = [

time: 95.7 us -> 95.5 us (level)
    all_to_all x1, starting transfers between devices: 5.16 us -> 4.17 us  [body(): rows = lax.all_to_all(rows, 'rep', 0, 0)]
  transfers between devices with their start and end apart: 10 -> 10, of which waited for: 2 -> 2; matrix products, arithmetic and copies ran while one was open for 1% -> 1% of each run, Pallas kernels for 10% -> 11%
where the time goes in v8:
time: 95.5 us; the launch traced here: 95.1 us
  blocking collectives  53 us (55%)
  starting transfers between devices  19.5 us (20%)
  Pallas kernels  14.2 us (15%)
  waiting for transfers between devices  4.48 us (5%)
  local copies, waits for them, and re-layouts  2.92 us (3%)
    all_to_all x1, blocking collectives, body(): lax.all_to_all(summed, ('rep', 'tp'), 0, 0, axis_index_groups=groups)  18.4 us
    all_to_all x1, blocking collectives, body(): lax.all_to_all(finish(partials, cosine, sine, embed_table.T, embed_table....  12.6 us
    all_to_all x1, blocking collectives, body(): parts = lax.all_to_all(attend(cache_len, projected, kv_cache), 'tp', 0, 0)  12.3 us
    all_to_all x1, blocking collectives, body(): heads = lax.all_to_all(merge(parts), 'tp', 0, 0)  9.63 us
    pallas_call x1, Pallas kernels, gather_rows(): pl.pallas_call(gather_kernel, grid=(1,), in_specs=[SMEM, pl.BlockSpec((FE...  6.05 us
    ppermute x1, starting transfers between devices, body(): other_qkv = lax.ppermute(new_qkv, 'rep', turn)  4.43 us
    all_to_all x1, starting transfers between devices, body(): rows = lax.all_to_all(rows, 'rep', 0, 0)  4.17 us
    pallas_call x1, Pallas kernels, attend(): pl.pallas_call(attend_kernel, grid=(ROWS,), in_specs=[SMEM, whole, VMEM],...  3.49 us
  transfers between devices with their start and end apart: 10, of which 2 were waited for; matrix products, arithmetic and copies ran while one was open for 1% of the time, Pallas kernels for 11%

profile of v8, /device:TPU:1, one launch (start us, length us, event | category | flops | bytes accessed | tf_op | source)
XLA Modules:
  0.0 95.1 jit_solution(12998351422317169853)
XLA Ops:
  0.0 4.4 %collective-permute-start = (bf16[40,7168]{1,0:T(8,128)(2,1)}, bf16[40,7168]{1,0:T(8,128)(2,1)S(1)}, u32[]{:S(2)}, u32[]{:S(2)}) collective-permute-start(bf16[40,7168]{1,0:T(8,128)(2,1)} %new_ref.3), channel_id=1, source_target_pairs={{0,16},{16,0},{32,48},{48,32},{64,80},{80,64},{96,112},{112,96},{1... | collective-permute-start | bytes 1720328 | tf_op jit(solution)/shard_map/ppermute | solution.py:473
  4.4 0.0 copy-start.5
  4.4 0.0 copy-start.2
  4.4 6.0 %gather_rows.1 = bf16[8,128,128]{2,1,0:T(8,128)(2,1)} custom-call(s32[4,32]{1,0:T(4,128)} %bitcast.18, bf16[320,9504]{1,0:T(8,128)(2,1)} %bitcast.14, bf16[320,9504]{1,0:T(8,128)(2,1)} %bitcast.15), custom_call_target="tpu_custom_call" | custom-call | tf_op jit(solution)/shard_map/gather_rows/pallas_call | solution.py:123
  10.5 0.0 copy-start.4
  10.5 4.2 %all-to-all-start = ((bf16[8,128,128]{2,1,0:T(8,128)(2,1)}), bf16[8,128,128]{2,1,0:T(8,128)(2,1)S(1)}, u32[]{:S(2)}, u32[]{:S(2)}) async-start(bf16[8,128,128]{2,1,0:T(8,128)(2,1)} %gather_rows.1), calls=%async_computation | async-start | bytes 524288 | tf_op jit(solution)/shard_map/all_to_all | solution.py:478
  14.7 0.0 copy-done.5
  14.7 0.0 copy-start
  14.7 2.3 %copy-done = bf16[320,7168]{1,0:T(8,128)(2,1)S(1)} copy-done((bf16[320,7168]{1,0:T(8,128)(2,1)S(1)}, bf16[320,7168]{1,0:T(8,128)(2,1)}, u32[]{:S(2)}) %copy-start) | copy-done | bytes 4587544
  17.0 0.1 take_old_columns.1.old
  17.1 0.0 copy-done.4
  17.2 0.6 dynamic_slice.3
  18.4 0.1 fusion
  18.5 0.1 pad_maximum_fusion
  18.6 3.4 %all-to-all-done.x_ref = bf16[8,128,128]{2,1,0:T(8,128)(2,1)S(1)} async-done(((bf16[8,128,128]{2,1,0:T(8,128)(2,1)}), bf16[8,128,128]{2,1,0:T(8,128)(2,1)S(1)}, u32[]{:S(2)}, u32[]{:S(2)}) %all-to-all-start) | async-done | bytes 262176 | tf_op jit(solution)/shard_map/all_to_all | solution.py:478
  22.0 0.0 collective-permute-done.other_ref
  22.0 0.0 copy-done.2
  22.0 0.7 project.3
  22.7 2.4 %collective-permute-start.1 = (f32[1280,128]{1,0:T(8,128)S(1)}, f32[1280,128]{1,0:T(8,128)S(1)}, u32[]{:S(2)}, u32[]{:S(2)}) collective-permute-start(f32[1280,128]{1,0:T(8,128)S(1)} %project.3), channel_id=1, source_target_pairs={{0,1},{1,0},{2,3},{3,2},{4,5},{5,4},{6,7},{7,6},{8,9},{9,8},{10,11... | collective-permute-start | bytes 1966088 | tf_op jit(solution)/shard_map/ppermute | solution.py:483
  25.1 0.7 project.2.a_ref
  25.8 1.0 %collective-permute-done.1.b_ref = f32[1280,128]{1,0:T(8,128)S(1)} collective-permute-done((f32[1280,128]{1,0:T(8,128)S(1)}, f32[1280,128]{1,0:T(8,128)S(1)}, u32[]{:S(2)}, u32[]{:S(2)}) %collective-permute-start.1) | collective-permute-done | bytes 655392 | tf_op jit(solution)/shard_map/ppermute | solution.py:483
  26.8 0.1 add.23
  26.9 18.4 %all_to_all.25.x_ref = f32[32,40,128]{2,1,0:T(8,128)S(1)} all-to-all(f32[32,40,128]{2,1,0:T(8,128)S(1)} %bitcast.9), channel_id=1, replica_groups={{0,2,4,6,8,10,12,14,32,34,36,38,40,42,44,46,64,66,68,70,72,74,76,78,96,..., dimensions={0} | all-to-all | bytes 1310720 | tf_op jit(solution)/shard_map/all_to_all | solution.py:490
  45.3 0.0 copy-done.3
  45.3 0.7 collective-permute-start.4
  46.0 0.8 collective-permute-start.3
  46.8 1.9 %collective-permute-start.2 = (bf16[40,5120]{1,0:T(8,128)(2,1)S(1)}, bf16[40,5120]{1,0:T(8,128)(2,1)S(1)}, u32[]{:S(2)}, u32[]{:S(2)}) collective-permute-start(bf16[40,5120]{1,0:T(8,128)(2,1)S(1)} %bitcast.12), channel_id=1, source_target_pairs={{0,16},{16,0},{32,48},{48,32},{64,80},{80,64},{96,112},{112,96},{1... | collective-permute-start | bytes 1228808 | tf_op jit(solution)/shard_map/ppermute | solution.py:492
  48.7 0.1 finish.1
  48.8 12.6 %all_to_all.26.q_ref = bf16[16,64,128]{2,1,0:T(8,128)(2,1)S(1)} all-to-all(bf16[16,64,128]{2,1,0:T(8,128)(2,1)S(1)} %finish.1), channel_id=1, replica_groups=mesh['rep'=8,'tp'=16] {'tp'}, dimensions={0} | all-to-all | bytes 524288 | tf_op jit(solution)/shard_map/all_to_all | solution.py:495
  61.5 0.0 collective-permute-done.4.refs_4_
  61.5 0.0 collective-permute-done.3.refs_8_
  61.5 0.0 collective-permute-done.2.refs_3_
  61.5 2.1 %collective-permute-start.5 = (bf16[40,5120]{1,0:T(8,128)(2,1)S(1)}, bf16[40,5120]{1,0:T(8,128)(2,1)S(1)}, u32[]{:S(2)}, u32[]{:S(2)}) collective-permute-start(bf16[40,5120]{1,0:T(8,128)(2,1)S(1)} %collective-permute-done.2.refs_3_), channel_id=1, source_target_pairs={{0,96},{16,112},{32,0},{48,16},{64,32},{80,48},{96,64},{112,80},{1... | collective-permute-start | bytes 1228808 | tf_op jit(solution)/shard_map/ppermute | solution.py:500
  63.6 0.0 collective-permute-start.6
  63.6 0.0 slice-done
  63.6 0.0 slice-done.1
  63.6 3.5 %attend.1 = bf16[16,64,128]{2,1,0:T(8,128)(2,1)S(1)} custom-call(s32[4]{0:T(128)S(1)} %copy-done.4, bf16[16,64,128]{2,1,0:T(8,128)(2,1)S(1)} %all_to_all.26.q_ref, bf16[4,512,2048]{2,1,0:T(8,128)(2,1)S(1)} %bitcast.7), custom_call_target="tpu_custom_call" | custom-call | tf_op jit(solution)/shard_map/attend/pallas_call | solution.py:371
  67.1 12.3 %all_to_all.27.x_ref = bf16[16,64,128]{2,1,0:T(8,128)(2,1)S(1)} all-to-all(bf16[16,64,128]{2,1,0:T(8,128)(2,1)S(1)} %attend.1), channel_id=1, replica_groups=mesh['rep'=8,'tp'=16] {'tp'}, dimensions={0} | all-to-all | bytes 524288 | tf_op jit(solution)/shard_map/all_to_all | solution.py:501
  79.4 0.0 collective-permute-done.5.refs_5_
  79.4 0.0 collective-permute-done.6.refs_6_
  79.4 0.0 collective-permute-start.8
  79.4 3.0 %collective-permute-start.7 = (bf16[40,5120]{1,0:T(8,128)(2,1)S(1)}, bf16[40,5120]{1,0:T(8,128)(2,1)S(1)}, u32[]{:S(2)}, u32[]{:S(2)}) collective-permute-start(bf16[40,5120]{1,0:T(8,128)(2,1)S(1)} %collective-permute-done.5.refs_5_), channel_id=1, source_target_pairs={{0,96},{16,112},{32,0},{48,16},{64,32},{80,48},{96,64},{112,80},{1... | collective-permute-start | bytes 1228808 | tf_op jit(solution)/shard_map/ppermute | solution.py:505
  82.4 0.4 merge.1
  82.8 9.6 %all_to_all.28.refs_0_ = bf16[16,40,128]{2,1,0:T(8,128)(2,1)S(1)} all-to-all(bf16[16,40,128]{2,1,0:T(8,128)(2,1)S(1)} %merge.1), channel_id=1, replica_groups=mesh['rep'=8,'tp'=16] {'tp'}, dimensions={0} | all-to-all | bytes 327680 | tf_op jit(solution)/shard_map/all_to_all | solution.py:507
  92.4 0.0 collective-permute-done.8.refs_9_
  92.4 0.0 collective-permute-done.7.refs_7_
  92.4 0.0 copy-done.1
  92.4 2.7 %output.1 = bf16[4,4,320]{2,1,0:T(4,128)(2,1)} custom-call(bf16[16,40,128]{2,1,0:T(8,128)(2,1)S(1)} %all_to_all.28.refs_0_, bf16[320,5120]{1,0:T(8,128)(2,1)S(1)} %bitcast.8, bf16[40,5120]{1,0:T(8,128)(2,1)S(1)} %bitcast.13, bf16[40,5120]{1,0:T(8,128)(2,1)S(1)} %collective-permute-done.2.refs_3_, bf16[40,5120]{1,0:T(8,128)(2,1)S(1)} %collective-permute-done.4.refs_4_, ...), custom_call_target="tpu_custom_call" | custom-call | tf_op jit(solution)/shard_map/output/pallas_call | solution.py:439
  (8 shorter events, 0.0 us)
Async XLA Ops:
  0.0 22.0 %collective-permute-start = (bf16[40,7168]{1,0:T(8,128)(2,1)}, bf16[40,7168]{1,0:T(8,128)(2,1)S(1)}, u32[]{:S(2)}, u32[]{:S(2)}) collective-permute-start(bf16[40,7168]{1,0:T(8,128)(2,1)} %new_ref.3), channel_id=1, source_target_pairs={{0,16},{16,0},{32,48},{48,32},{64,80},{80,64},{96,112},{112,96},{1... | collective-permute-start | bytes 1720328 | tf_op jit(solution)/shard_map/ppermute | solution.py:473
  4.4 10.2 %copy-start.5 = (bf16[320]{0:T(512)(128)(2,1)S(1)}, bf16[320]{0:T(512)(128)(2,1)}, u32[]{:S(2)}) copy-start(bf16[320]{0:T(512)(128)(2,1)} %param.12) | copy-start | bytes 1924
  4.4 17.6 %copy-start.2 = (bf16[40,7168]{1,0:T(8,128)(2,1)S(1)}, bf16[40,7168]{1,0:T(8,128)(2,1)}, u32[]{:S(2)}) copy-start(bf16[40,7168]{1,0:T(8,128)(2,1)} %new_ref.3) | copy-start | bytes 1720324
  10.5 6.7 %copy-start.4 = (s32[4]{0:T(128)S(1)}, s32[4]{0:T(128)}, u32[]{:S(2)}) copy-start(s32[4]{0:T(128)} %len_ref.1) | copy-start | bytes 52
  10.5 11.5 %all-to-all-start = ((bf16[8,128,128]{2,1,0:T(8,128)(2,1)}), bf16[8,128,128]{2,1,0:T(8,128)(2,1)S(1)}, u32[]{:S(2)}, u32[]{:S(2)}) async-start(bf16[8,128,128]{2,1,0:T(8,128)(2,1)} %gather_rows.1), calls=%async_computation | async-start | bytes 524288 | tf_op jit(solution)/shard_map/all_to_all | solution.py:478
  14.7 2.3 %copy-start = (bf16[320,7168]{1,0:T(8,128)(2,1)S(1)}, bf16[320,7168]{1,0:T(8,128)(2,1)}, u32[]{:S(2)}) copy-start(bf16[320,7168]{1,0:T(8,128)(2,1)} %refs_2_) | copy-start | bytes 13762564
  22.0 23.3 %copy-start.3 = (bf16[5120,40]{0,1:T(8,128)(2,1)S(1)}, bf16[5120,40]{0,1:T(8,128)(2,1)}, u32[]{:S(2)}) copy-start(bf16[5120,40]{0,1:T(8,128)(2,1)} %param.16) | copy-start | bytes 1228804
  22.7 4.1 %collective-permute-start.1 = (f32[1280,128]{1,0:T(8,128)S(1)}, f32[1280,128]{1,0:T(8,128)S(1)}, u32[]{:S(2)}, u32[]{:S(2)}) collective-permute-start(f32[1280,128]{1,0:T(8,128)S(1)} %project.3), channel_id=1, source_target_pairs={{0,1},{1,0},{2,3},{3,2},{4,5},{5,4},{6,7},{7,6},{8,9},{9,8},{10,11... | collective-permute-start | bytes 1966088 | tf_op jit(solution)/shard_map/ppermute | solution.py:483
  45.3 18.3 %slice-start = ((s8[8388608]{0:T(1024)(128)(4,1)}), s8[4194304]{0:T(1024)(128)(4,1)S(1)}, s32[]{:S(2)}) async-start(s8[8388608]{0:T(1024)(128)(4,1)} %bitcast.6), calls=%async_computation.5 | async-start | bytes 8388608
  45.3 18.3 %slice-start.1 = ((s8[8388608]{0:T(1024)(128)(4,1)}), s8[4194304]{0:T(1024)(128)(4,1)S(1)}, s32[]{:S(2)}) async-start(s8[8388608]{0:T(1024)(128)(4,1)} %bitcast.6), calls=%async_computation.6 | async-start | bytes 8388608
  45.3 16.2 %collective-permute-start.4 = (bf16[40,5120]{1,0:T(8,128)(2,1)S(1)}, bf16[40,5120]{1,0:T(8,128)(2,1)S(1)}, u32[]{:S(2)}, u32[]{:S(2)}) collective-permute-start(bf16[40,5120]{1,0:T(8,128)(2,1)S(1)} %bitcast.10), channel_id=1, source_target_pairs={{0,96},{16,112},{32,0},{48,16},{64,32},{80,48},{96,64},{112,80},{1... | collective-permute-start | bytes 1228808 | tf_op jit(solution)/shard_map/ppermute | solution.py:494
  46.0 15.5 %collective-permute-start.3 = (bf16[40,5120]{1,0:T(8,128)(2,1)S(1)}, bf16[40,5120]{1,0:T(8,128)(2,1)S(1)}, u32[]{:S(2)}, u32[]{:S(2)}) collective-permute-start(bf16[40,5120]{1,0:T(8,128)(2,1)S(1)} %bitcast.11), channel_id=1, source_target_pairs={{0,32},{16,48},{32,64},{48,80},{64,96},{80,112},{96,0},{112,16},{1... | collective-permute-start | bytes 1228808 | tf_op jit(solution)/shard_map/ppermute | solution.py:493
  46.8 14.7 %collective-permute-start.2 = (bf16[40,5120]{1,0:T(8,128)(2,1)S(1)}, bf16[40,5120]{1,0:T(8,128)(2,1)S(1)}, u32[]{:S(2)}, u32[]{:S(2)}) collective-permute-start(bf16[40,5120]{1,0:T(8,128)(2,1)S(1)} %bitcast.12), channel_id=1, source_target_pairs={{0,16},{16,0},{32,48},{48,32},{64,80},{80,64},{96,112},{112,96},{1... | collective-permute-start | bytes 1228808 | tf_op jit(solution)/shard_map/ppermute | solution.py:492
  61.5 30.9 %copy-start.1 = (bf16[5120,320]{0,1:T(8,128)(2,1)S(1)}, bf16[5120,320]{0,1:T(8,128)(2,1)}, u32[]{:S(2)}) copy-start(bf16[5120,320]{0,1:T(8,128)(2,1)} %param.14) | copy-start | bytes 9830404
  61.5 17.9 %collective-permute-start.5 = (bf16[40,5120]{1,0:T(8,128)(2,1)S(1)}, bf16[40,5120]{1,0:T(8,128)(2,1)S(1)}, u32[]{:S(2)}, u32[]{:S(2)}) collective-permute-start(bf16[40,5120]{1,0:T(8,128)(2,1)S(1)} %collective-permute-done.2.refs_3_), channel_id=1, source_target_pairs={{0,96},{16,112},{32,0},{48,16},{64,32},{80,48},{96,64},{112,80},{1... | collective-permute-start | bytes 1228808 | tf_op jit(solution)/shard_map/ppermute | solution.py:500
  63.6 15.8 %collective-permute-start.6 = (bf16[40,5120]{1,0:T(8,128)(2,1)S(1)}, bf16[40,5120]{1,0:T(8,128)(2,1)S(1)}, u32[]{:S(2)}, u32[]{:S(2)}) collective-permute-start(bf16[40,5120]{1,0:T(8,128)(2,1)S(1)} %collective-permute-done.3.refs_8_), channel_id=1, source_target_pairs={{0,32},{16,48},{32,64},{48,80},{64,96},{80,112},{96,0},{112,16},{1... | collective-permute-start | bytes 1228808 | tf_op jit(solution)/shard_map/ppermute | solution.py:499
  79.4 13.0 %collective-permute-start.8 = (bf16[40,5120]{1,0:T(8,128)(2,1)S(1)}, bf16[40,5120]{1,0:T(8,128)(2,1)S(1)}, u32[]{:S(2)}, u32[]{:S(2)}) collective-permute-start(bf16[40,5120]{1,0:T(8,128)(2,1)S(1)} %collective-permute-done.2.refs_3_), channel_id=1, source_target_pairs={{0,32},{16,48},{32,64},{48,80},{64,96},{80,112},{96,0},{112,16},{1... | collective-permute-start | bytes 1228808 | tf_op jit(solution)/shard_map/ppermute | solution.py:506
  79.4 13.0 %collective-permute-start.7 = (bf16[40,5120]{1,0:T(8,128)(2,1)S(1)}, bf16[40,5120]{1,0:T(8,128)(2,1)S(1)}, u32[]{:S(2)}, u32[]{:S(2)}) collective-permute-start(bf16[40,5120]{1,0:T(8,128)(2,1)S(1)} %collective-permute-done.5.refs_5_), channel_id=1, source_target_pairs={{0,96},{16,112},{32,0},{48,16},{64,32},{80,48},{96,64},{112,80},{1... | collective-permute-start | bytes 1228808 | tf_op jit(solution)/shard_map/ppermute | solution.py:505
